TPU v7x, 256 devices: a whole 4x4x8 slice. The times are simulated.
256 devices in a mesh: blk: 64 (over y_lo, x, z), uly: 4 (over y_hi, core).
Axes of the slice: x: 4, y: 4 (y_hi: 2, y_lo: 2; y = y_hi * 2 + y_lo), z: 8, core: 2. Of those that a mesh axis runs over, the one named last changes fastest.
Arguments:
- queries: bfloat16 [32768, 3072], P(('blk', 'uly')), may hold values from -40 to 40
- keys: bfloat16 [32768, 3072], P(('blk', 'uly')), may hold values from -8 to 8
- values: bfloat16 [32768, 3072], P(('blk', 'uly')), may hold values from -6 to 6
- tile_order: int32 [256], replicated, may hold values from 0 to 255, as said below
- tile_mask: int32 [256, 20], replicated, may hold values from 0 to 1, as said below
Outputs:
- attended: bfloat16 [32768, 3072], P(('blk', 'uly'))
Inputs may be any that keep to these rules, and one draw needn't show every extreme that they name: `tile_order`: entries 4 * f to 4 * f + 3 are a permutation of the tile numbers 4 * f to 4 * f + 3: every slot holds a tile of its own frame. tile_mask[a, (e + 2) * 4 + b] is 1 where tile a may attend to tile 4 * (a // 4 + e) + b; it is 0 where a // 4 + e is not a frame; tile_mask[a, 8 + a % 4] is 1.
All inputs are finite; a program needn't handle non-finite values.
Results may differ from a plain program's by a relative error of at most 0.0055.
Values may be sent and summed in bfloat16 or wider, within the bound.
No kernel may reach another device: no remote copies, remote signals or barrier semaphores. Data moves between devices by JAX's collectives and lax.ppermute only.
A program may use at most 64 MiB of HBM per device.

v0:
```python
import math

import jax
import jax.numpy as jnp
from jax import lax
from jax.sharding import PartitionSpec as P

HEAD = 128
TPS = 4
REACH = 2


def passed_along(block, axis, distance):
    devices = range(lax.axis_size(axis))
    route = [((i - distance) % len(devices), i) for i in devices]
    return lax.ppermute(block, axis, route)


def select_matrix(indices, count):
    return (indices[:, None] == jnp.arange(count, dtype=jnp.int32)[None, :]).astype(jnp.float32)


def per_device(queries, keys, values, tile_order, tile_mask):
    head_queries, head_keys, head_values = (
        lax.all_to_all(queries, "uly", split_axis=1, concat_axis=0, tiled=True),
        lax.all_to_all(keys, "uly", split_axis=1, concat_axis=0, tiled=True),
        lax.all_to_all(values, "uly", split_axis=1, concat_axis=0, tiled=True),
    )
    block_rows = head_queries.shape[0]
    local_heads = head_queries.shape[1] // HEAD
    tile_rows = block_rows // TPS
    position = lax.axis_index("blk")
    frame_count = lax.axis_size("blk")
    scale = 1.0 / math.sqrt(HEAD)
    query_heads = head_queries.reshape(block_rows, local_heads, HEAD)
    own_order = lax.dynamic_slice_in_dim(tile_order, position * TPS, TPS) - position * TPS
    own_rows = lax.dynamic_slice_in_dim(tile_mask, position * TPS, TPS, 0).astype(jnp.float32)
    slot_rows = jnp.dot(
        select_matrix(own_order, TPS),
        own_rows,
        precision=lax.Precision.HIGHEST,
        preferred_element_type=jnp.float32,
    )

    def absorb(state, stacked, offset):
        other_frame = position + offset
        inside = ((other_frame >= 0) & (other_frame < frame_count)).astype(jnp.float32)
        clipped = jnp.clip(other_frame, 0, frame_count - 1)
        other_order = lax.dynamic_slice_in_dim(tile_order, clipped * TPS, TPS) - clipped * TPS
        columns = slot_rows[:, (offset + REACH) * TPS : (offset + REACH + 1) * TPS]
        tile_allowed = (
            jnp.dot(
                columns,
                select_matrix(other_order, TPS).T,
                precision=lax.Precision.HIGHEST,
                preferred_element_type=jnp.float32,
            )
            * inside
        )
        active = jnp.any(tile_allowed > 0.5)

        def update(carried):
            top_score, total, accum = carried
            allowed = jnp.repeat(
                jnp.repeat(tile_allowed > 0.5, tile_rows, axis=0), tile_rows, axis=1
            )
            key_heads = stacked[0].reshape(block_rows, local_heads, HEAD)
            value_heads = stacked[1].reshape(block_rows, local_heads, HEAD)
            scores = (
                jnp.einsum(
                    "qhd,khd->qhk", query_heads, key_heads, preferred_element_type=jnp.float32
                )
                * scale
            )
            masked = jnp.where(allowed[:, None, :], scores, -1e30)
            new_top = jnp.maximum(top_score, jnp.max(masked, axis=2))
            weights = jnp.where(allowed[:, None, :], jnp.exp(masked - new_top[:, :, None]), 0.0)
            factor = jnp.exp(top_score - new_top)
            new_total = total * factor + jnp.sum(weights, axis=2)
            new_accum = accum * factor[:, :, None] + jnp.einsum(
                "qhk,khd->qhd",
                weights.astype(jnp.bfloat16),
                value_heads,
                preferred_element_type=jnp.float32,
            )
            return (new_top, new_total, new_accum)

        def unchanged(carried):
            return carried

        return lax.cond(active, update, unchanged, state)

    state = (
        jnp.full((block_rows, local_heads), -1e30, jnp.float32),
        jnp.zeros((block_rows, local_heads), jnp.float32),
        jnp.zeros((block_rows, local_heads, HEAD), jnp.float32),
    )
    own_pair = jnp.stack([head_keys, head_values])
    arriving = passed_along(own_pair, "blk", -REACH)
    state = absorb(state, arriving, REACH)
    for step_index in range(2 * REACH):
        arriving = passed_along(arriving, "blk", 1)
        state = absorb(state, arriving, REACH - 1 - step_index)
    top_score, total, accum = state
    outputs = (
        (accum / total[:, :, None]).astype(jnp.bfloat16).reshape(block_rows, local_heads * HEAD)
    )
    return lax.all_to_all(outputs, "uly", split_axis=0, concat_axis=1, tiled=True)


def solution(mesh):
    return jax.shard_map(
        per_device,
        mesh=mesh,
        in_specs=(
            P(("blk", "uly"), None),
            P(("blk", "uly"), None),
            P(("blk", "uly"), None),
            P(),
            P(),
        ),
        out_specs=P(("blk", "uly"), None),
        check_vma=False,
    )
```

profile of v0, /device:TPU:8, one launch (start us, length us, event | category | flops | bytes accessed | tf_op | source)
XLA Modules:
  0.0 353.7 jit_solution(8033766370934859093)
XLA Ops:
  0.0 2.4 copy.125
  2.4 3.6 %all-to-all-start = ((bf16[128,4,768]{0,2,1:T(8,128)(2,1)}), bf16[128,4,768]{0,2,1:T(8,128)(2,1)S(1)}, u32[]{:S(2)}, u32[]{:S(2)}) async-start(bf16[128,4,768]{0,2,1:T(8,128)(2,1)} %bitcast.25), calls=%async_computation | async-start | bytes 1572864 | tf_op jit(solution)/shard_map/all_to_all | solution.py:26
  5.9 2.3 copy.127
  8.2 10.9 %all-to-all-done = bf16[128,4,768]{0,2,1:T(8,128)(2,1)S(1)} async-done(((bf16[128,4,768]{0,2,1:T(8,128)(2,1)}), bf16[128,4,768]{0,2,1:T(8,128)(2,1)S(1)}, u32[]{:S(2)}, u32[]{:S(2)}) %all-to-all-start) | async-done | bytes 786464 | tf_op jit(solution)/shard_map/all_to_all | solution.py:26
  19.1 3.5 all-to-all-start.1
  22.9 12.8 %all-to-all-done.1 = bf16[128,4,768]{0,2,1:T(8,128)(2,1)S(1)} async-done(((bf16[128,4,768]{0,2,1:T(8,128)(2,1)}), bf16[128,4,768]{0,2,1:T(8,128)(2,1)S(1)}, u32[]{:S(2)}, u32[]{:S(2)}) %all-to-all-start.1) | async-done | bytes 786464 | tf_op jit(solution)/shard_map/all_to_all | solution.py:27
  36.2 9.4 %collective-permute-start = (bf16[2,512,768]{2,1,0:T(8,128)(2,1)S(1)}, bf16[2,512,768]{2,1,0:T(8,128)(2,1)S(1)}, u32[]{:S(2)}, u32[]{:S(2)}) collective-permute-start(bf16[2,512,768]{2,1,0:T(8,128)(2,1)S(1)} %pad_maximum_fusion), channel_id=1, source_target_pairs={{8,0},{12,4},{16,8},{20,12},{24,16},{28,20},{32,24},{36,28},{40,32... | collective-permute-start | bytes 4718600 | tf_op jit(solution)/shard_map/ppermute | solution.py:16
  45.5 67.2 %collective-permute-done = bf16[2,512,768]{2,1,0:T(8,128)(2,1)S(1)} collective-permute-done((bf16[2,512,768]{2,1,0:T(8,128)(2,1)S(1)}, bf16[2,512,768]{2,1,0:T(8,128)(2,1)S(1)}, u32[]{:S(2)}, u32[]{:S(2)}) %collective-permute-start) | collective-permute-done | bytes 1572896 | tf_op jit(solution)/shard_map/ppermute | solution.py:16
  113.8 38.9 %collective-permute-done.1 = bf16[2,512,768]{2,1,0:T(8,128)(2,1)S(1)} collective-permute-done((bf16[2,512,768]{2,1,0:T(8,128)(2,1)S(1)}, bf16[2,512,768]{2,1,0:T(8,128)(2,1)S(1)}, u32[]{:S(2)}, u32[]{:S(2)}) %collective-permute-start.1) | collective-permute-done | bytes 1572896 | tf_op jit(solution)/shard_map/ppermute | solution.py:16
  152.7 39.1 %collective-permute-done.2 = bf16[2,512,768]{2,1,0:T(8,128)(2,1)S(1)} collective-permute-done((bf16[2,512,768]{2,1,0:T(8,128)(2,1)S(1)}, bf16[2,512,768]{2,1,0:T(8,128)(2,1)S(1)}, u32[]{:S(2)}, u32[]{:S(2)}) %collective-permute-start.2) | collective-permute-done | bytes 1572896 | tf_op jit(solution)/shard_map/ppermute | solution.py:16
  193.0 38.3 %collective-permute-done.3 = bf16[2,512,768]{2,1,0:T(8,128)(2,1)} collective-permute-done((bf16[2,512,768]{2,1,0:T(8,128)(2,1)S(1)}, bf16[2,512,768]{2,1,0:T(8,128)(2,1)}, u32[]{:S(2)}, u32[]{:S(2)}) %collective-permute-start.3) | collective-permute-done | bytes 1572896 | tf_op jit(solution)/shard_map/ppermute | solution.py:16
  232.4 3.5 all-to-all-start.2
  243.7 32.0 %all-to-all-done.2 = bf16[128,4,768]{0,2,1:T(8,128)(2,1)S(1)} async-done(((bf16[128,4,768]{0,2,1:T(8,128)(2,1)}), bf16[128,4,768]{0,2,1:T(8,128)(2,1)S(1)}, u32[]{:S(2)}, u32[]{:S(2)}) %all-to-all-start.2) | async-done | bytes 786464 | tf_op jit(solution)/shard_map/all_to_all | solution.py:25
  276.6 10.7 %conditional.5 = (f32[512,6]{0,1:T(8,128)}, f32[512,6]{0,1:T(8,128)S(1)}, f32[512,6,128]{2,0,1:T(8,128)S(1)}) conditional(s32[]{:T(128)} %convert_element_type.67, () %tuple.38, (f32[4,4]{1,0:T(4,128)S(1)}, bf16[2,512,768]{2,1,0:T(8,128)(2,1)}, bf16[512,6,128]{0,2,1:T(8,128)(2,1)S(1)}) %tuple.115), branch_computations={%region_5.6_spmd, %region_6.0_spmd} | conditional | flops 826159104 | bytes 30290168 | solution.py:91
  277.4 1.7 copy.132
  281.2 2.2 fusion.2
  284.2 3.2 bitcast_add_fusion
  287.4 12.0 %conditional.6 = ((f32[512,6]{0,1:T(8,128)}, f32[512,6]{0,1:T(8,128)S(1)}, f32[512,6,128]{2,0,1:T(8,128)S(1)})) conditional(s32[]{:T(128)} %convert_element_type.65, (f32[512,6]{0,1:T(8,128)}, f32[512,6]{0,1:T(8,128)S(1)}, f32[512,6,128]{2,0,1:T(8,128)S(1)}) %conditional.5, (f32[4,4]{1,0:T(4,128)S(1)}, bf16[2,512,768]{2,1,0:T(8,128)(2,1)}, ...), branch_computations={%region_9.10_spmd, %region_10.0_spmd} | conditional | flops 826546176 | bytes 31924480 | solution.py:91
  287.7 2.6 copy.135
  296.1 2.8 bitcast_add_fusion.1
  299.4 12.2 %conditional.7 = ((f32[512,6]{0,1:T(8,128)}, f32[512,6]{0,1:T(8,128)S(1)}, f32[512,6,128]{2,0,1:T(8,128)S(1)})) conditional(s32[]{:T(128)} %convert_element_type.63, (f32[512,6]{0,1:T(8,128)}, f32[512,6]{0,1:T(8,128)S(1)}, f32[512,6,128]{2,0,1:T(8,128)S(1)}) %get-tuple-element.345, (f32[4,4]{1,0:T(4,128)S(1)}, bf16[2,512,768]{2,1,0:T(8,128)(2,1)}, ...), branch_computations={%region_13.14_spmd, %region_14.17_spmd} | conditional | flops 826546176 | bytes 31924480 | solution.py:91
  299.9 2.6 copy.138
  306.0 1.5 fusion.25
  308.3 2.8 bitcast_add_fusion.2
  311.7 12.1 %conditional.8 = ((f32[512,6]{0,1:T(8,128)}, f32[512,6]{0,1:T(8,128)S(1)}, f32[512,6,128]{2,0,1:T(8,128)S(1)})) conditional(s32[]{:T(128)} %convert_element_type.61, (f32[512,6]{0,1:T(8,128)}, f32[512,6]{0,1:T(8,128)S(1)}, f32[512,6,128]{2,0,1:T(8,128)S(1)}) %get-tuple-element.346, (f32[4,4]{1,0:T(4,128)S(1)}, bf16[2,512,768]{2,1,0:T(8,128)(2,1)}, ...), branch_computations={%region_17.18_spmd, %region_18.21_spmd} | conditional | flops 826546176 | bytes 31924480 | solution.py:91
  311.9 2.6 copy.141
  320.3 2.8 bitcast_add_fusion.3
  323.7 11.6 %conditional.9 = ((f32[512,6]{0,1:T(8,128)S(1)}, f32[512,6,128]{2,0,1:T(8,128)S(1)})) conditional(s32[]{:T(128)} %convert_element_type.59, (f32[512,6]{0,1:T(8,128)S(1)}, f32[512,6,128]{2,0,1:T(8,128)S(1)}) %tuple.43, (f32[4,4]{1,0:T(4,128)S(1)}, bf16[2,512,768]{2,1,0:T(8,128)(2,1)}, bf16[512,6,128]{0,2,1:T(8,128)(2,1)S(1)}, f32[512,6]{0,1:T(8,128)}, ...), branch_computations={%region_21.22_spmd, %region_22.25_spmd} | conditional | flops 826546176 | bytes 31899896 | solution.py:91
  324.2 2.6 copy.144
  330.3 1.5 fusion.47
  332.6 2.8 bitcast_add_fusion.4
  336.4 15.9 %all_to_all.67 = bf16[4,128,768]{1,2,0:T(8,128)(2,1)S(1)} all-to-all(bf16[4,128,768]{1,2,0:T(8,128)(2,1)S(1)} %copy.147), channel_id=1, replica_groups=mesh['blk'=64,'uly'=4] {'uly'}, dimensions={0} | all-to-all | bytes 1572864 | tf_op jit(solution)/shard_map/all_to_all | solution.py:108
  (85 shorter events, 37.8 us)
Async XLA Ops:
  0.0 231.3 %copy-start.3 = (bf16[128,3072]{1,0:T(8,128)(2,1)S(1)}, bf16[128,3072]{1,0:T(8,128)(2,1)}, u32[]{:S(2)}) copy-start(bf16[128,3072]{1,0:T(8,128)(2,1)} %param.15) | copy-start | bytes 2359300
  2.4 16.7 %all-to-all-start = ((bf16[128,4,768]{0,2,1:T(8,128)(2,1)}), bf16[128,4,768]{0,2,1:T(8,128)(2,1)S(1)}, u32[]{:S(2)}, u32[]{:S(2)}) async-start(bf16[128,4,768]{0,2,1:T(8,128)(2,1)} %bitcast.25), calls=%async_computation | async-start | bytes 1572864 | tf_op jit(solution)/shard_map/all_to_all | solution.py:26
  5.9 230.0 %copy-start.4 = (s32[256]{0:T(256)S(1)}, s32[256]{0:T(256)}, u32[]{:S(2)}) copy-start(s32[256]{0:T(256)} %param.18) | copy-start | bytes 3076
  5.9 230.1 %copy-start.5 = (s32[256,20]{0,1:T(8,128)S(1)}, s32[256,20]{0,1:T(8,128)}, u32[]{:S(2)}) copy-start(s32[256,20]{0,1:T(8,128)} %param.19) | copy-start | bytes 61444
  19.1 16.6 %all-to-all-start.1 = ((bf16[128,4,768]{0,2,1:T(8,128)(2,1)}), bf16[128,4,768]{0,2,1:T(8,128)(2,1)S(1)}, u32[]{:S(2)}, u32[]{:S(2)}) async-start(bf16[128,4,768]{0,2,1:T(8,128)(2,1)} %bitcast.28), calls=%async_computation.1 | async-start | bytes 1572864 | tf_op jit(solution)/shard_map/all_to_all | solution.py:27
  36.2 76.5 %collective-permute-start = (bf16[2,512,768]{2,1,0:T(8,128)(2,1)S(1)}, bf16[2,512,768]{2,1,0:T(8,128)(2,1)S(1)}, u32[]{:S(2)}, u32[]{:S(2)}) collective-permute-start(bf16[2,512,768]{2,1,0:T(8,128)(2,1)S(1)} %pad_maximum_fusion), channel_id=1, source_target_pairs={{8,0},{12,4},{16,8},{20,12},{24,16},{28,20},{32,24},{36,28},{40,32... | collective-permute-start | bytes 4718600 | tf_op jit(solution)/shard_map/ppermute | solution.py:16
  112.7 1.1 copy-start.2
  112.7 40.0 %collective-permute-start.1 = (bf16[2,512,768]{2,1,0:T(8,128)(2,1)S(1)}, bf16[2,512,768]{2,1,0:T(8,128)(2,1)S(1)}, u32[]{:S(2)}, u32[]{:S(2)}) collective-permute-start(bf16[2,512,768]{2,1,0:T(8,128)(2,1)S(1)} %collective-permute-done), channel_id=1, source_target_pairs={{252,0},{0,4},{4,8},{8,12},{12,16},{16,20},{20,24},{24,28},{28,32}... | collective-permute-start | bytes 4718600 | tf_op jit(solution)/shard_map/ppermute | solution.py:16
  152.7 78.6 %copy-start.1 = (bf16[2,512,768]{2,1,0:T(8,128)(2,1)}, bf16[2,512,768]{2,1,0:T(8,128)(2,1)S(1)}, u32[]{:S(2)}) copy-start(bf16[2,512,768]{2,1,0:T(8,128)(2,1)S(1)} %collective-permute-done.1) | copy-start | bytes 4718596
  152.7 39.1 %collective-permute-start.2 = (bf16[2,512,768]{2,1,0:T(8,128)(2,1)S(1)}, bf16[2,512,768]{2,1,0:T(8,128)(2,1)S(1)}, u32[]{:S(2)}, u32[]{:S(2)}) collective-permute-start(bf16[2,512,768]{2,1,0:T(8,128)(2,1)S(1)} %collective-permute-done.1), channel_id=1, source_target_pairs={{252,0},{0,4},{4,8},{8,12},{12,16},{16,20},{20,24},{24,28},{28,32}... | collective-permute-start | bytes 4718600 | tf_op jit(solution)/shard_map/ppermute | solution.py:16
  191.8 1.1 copy-start
  193.0 38.3 %collective-permute-start.3 = (bf16[2,512,768]{2,1,0:T(8,128)(2,1)S(1)}, bf16[2,512,768]{2,1,0:T(8,128)(2,1)}, u32[]{:S(2)}, u32[]{:S(2)}) collective-permute-start(bf16[2,512,768]{2,1,0:T(8,128)(2,1)S(1)} %collective-permute-done.2), channel_id=1, source_target_pairs={{252,0},{0,4},{4,8},{8,12},{12,16},{16,20},{20,24},{24,28},{28,32}... | collective-permute-start | bytes 4718600 | tf_op jit(solution)/shard_map/ppermute | solution.py:16
  231.3 92.4 %collective-permute-start.4 = (bf16[2,512,768]{2,1,0:T(8,128)(2,1)}, bf16[2,512,768]{2,1,0:T(8,128)(2,1)}, u32[]{:S(2)}, u32[]{:S(2)}) collective-permute-start(bf16[2,512,768]{2,1,0:T(8,128)(2,1)} %collective-permute-done.3), channel_id=1, source_target_pairs={{252,0},{0,4},{4,8},{8,12},{12,16},{16,20},{20,24},{24,28},{28,32}... | collective-permute-start | bytes 4718600 | tf_op jit(solution)/shard_map/ppermute | solution.py:16
  232.4 43.3 %all-to-all-start.2 = ((bf16[128,4,768]{0,2,1:T(8,128)(2,1)}), bf16[128,4,768]{0,2,1:T(8,128)(2,1)S(1)}, u32[]{:S(2)}, u32[]{:S(2)}) async-start(bf16[128,4,768]{0,2,1:T(8,128)(2,1)} %bitcast.31), calls=%async_computation.2 | async-start | bytes 1572864 | tf_op jit(solution)/shard_map/all_to_all | solution.py:25
where the time goes:
time: 360 us; the launch traced here: 354 us
  waiting for transfers between devices  239 us (66%)
  local copies, waits for them, and re-layouts  32.5 us (9%)
  matrix products  25.4 us (7%)
  starting transfers between devices  19.9 us (6%)
  other arithmetic  16.3 us (5%)
  blocking collectives  15.9 us (4%)
    ppermute x5, waiting for transfers between devices, passed_along(): return lax.ppermute(block, axis, route)  183 us
    all_to_all x1, waiting for transfers between devices, per_device(): lax.all_to_all(queries, 'uly', split_axis=1, concat_axis=0, tiled=True)  32 us
    all_to_all x1, blocking collectives, per_device(): lax.all_to_all(outputs, 'uly', split_axis=0, concat_axis=1, tiled=True)  15.9 us
    dot_general x5, matrix products, update(): jnp.einsum('qhk,khd->qhd', weights.astype(jnp.bfloat16), value_heads, pre...  14.3 us
    all_to_all x1, waiting for transfers between devices, per_device(): lax.all_to_all(values, 'uly', split_axis=1, concat_axis=0, tiled=True)  12.8 us
    another operation x10, local copies, waits for them, and re-layouts  12.6 us
    all_to_all x1, waiting for transfers between devices, per_device(): lax.all_to_all(keys, 'uly', split_axis=1, concat_axis=0, tiled=True)  10.9 us
    ppermute x5, starting transfers between devices, passed_along(): return lax.ppermute(block, axis, route)  9.37 us
  transfers between devices with their start and end apart: 8, of which 7 were waited for; matrix products, arithmetic and copies ran while one was open for 16% of the time, Pallas kernels for 0%

commit v1 on v0

v1 whole, which is shorter than its diff:
```python
import functools
import math

import jax
import jax.numpy as jnp
from jax import lax
from jax.experimental import pallas as pl
from jax.experimental.pallas import tpu as pltpu
from jax.sharding import PartitionSpec as P

HEAD = 128
TPS = 4
REACH = 2
SPAN = 2 * REACH + 1
CHUNKS = (2, 2, 2)
NEG = -1e30


def pack_kernel(groups, q_ref, k_ref, v_ref, *out_refs):
    width = q_ref.shape[1] // groups
    count = len(out_refs) // 2
    for u in range(groups):
        first = 0
        for c in range(count):
            kv_ref, qc_ref = out_refs[c], out_refs[count + c]
            cols = kv_ref.shape[-1]
            at = slice(u * width + first, u * width + first + cols)
            kv_ref[u, 0] = k_ref[:, at]
            kv_ref[u, 1] = v_ref[:, at]
            qc_ref[u] = q_ref[:, at]
            first += cols


def pack(queries, keys, values, groups, chunks):
    rows = queries.shape[0]
    kv = [jax.ShapeDtypeStruct((groups, 2, rows, n * HEAD), jnp.bfloat16) for n in chunks]
    q = [jax.ShapeDtypeStruct((groups, rows, n * HEAD), jnp.bfloat16) for n in chunks]
    outs = pl.pallas_call(
        functools.partial(pack_kernel, groups),
        out_shape=kv + q,
        name="pack",
    )(queries, keys, values)
    return outs[: len(chunks)], outs[len(chunks) :]


def unpack_kernel(groups, *refs):
    out_ref = refs[-1]
    width = out_ref.shape[1] // groups
    for u in range(groups):
        first = 0
        for ref in refs[:-1]:
            cols = ref.shape[-1]
            out_ref[:, u * width + first : u * width + first + cols] = ref[u]
            first += cols


def unpack(parts):
    groups, rows = parts[0].shape[:2]
    width = groups * sum(p.shape[-1] for p in parts)
    return pl.pallas_call(
        functools.partial(unpack_kernel, groups),
        out_shape=jax.ShapeDtypeStruct((rows, width), jnp.bfloat16),
        name="unpack",
    )(*parts)


def attend_kernel(scale, bias_ref, q_ref, *refs):
    kv_refs, out_ref, s_ref = refs[:SPAN], refs[SPAN], refs[SPAN + 1]
    rows = q_ref.shape[1]
    frame_rows = TPS * rows
    q = q_ref[...].reshape(frame_rows, HEAD)
    tops = [None] * TPS
    for e in range(SPAN):
        k = kv_refs[e][:, 0].reshape(frame_rows, HEAD)
        s = lax.dot_general(q, k, (((1,), (1,)), ((), ())), preferred_element_type=jnp.float32)
        for a in range(TPS):
            for b in range(TPS):
                block = s[a * rows : (a + 1) * rows, b * rows : (b + 1) * rows]
                block = block * scale + bias_ref[a * SPAN * TPS + e * TPS + b]
                s_ref[a, e * TPS + b] = block
                tops[a] = block if tops[a] is None else jnp.maximum(tops[a], block)
    tops = [jnp.max(top, axis=1, keepdims=True) for top in tops]
    sums = [None] * TPS
    accum = None
    for e in range(SPAN):
        weights = []
        for a in range(TPS):
            row = []
            for b in range(TPS):
                w = jnp.exp2(s_ref[a, e * TPS + b] - tops[a])
                sums[a] = w if sums[a] is None else sums[a] + w
                row.append(w.astype(jnp.bfloat16))
            weights.append(jnp.concatenate(row, axis=1))
        v = kv_refs[e][:, 1].reshape(frame_rows, HEAD)
        part = jnp.dot(
            jnp.concatenate(weights, axis=0), v, preferred_element_type=jnp.float32
        )
        accum = part if accum is None else accum + part
    for a in range(TPS):
        total = jnp.sum(sums[a], axis=1, keepdims=True)
        out_ref[a] = (accum[a * rows : (a + 1) * rows] / total).astype(out_ref.dtype)


def attend(bias, q, kvs):
    groups, rows, cols = q.shape
    heads = cols // HEAD
    keys = SPAN * groups * rows
    q_spec = pl.BlockSpec((groups, rows, HEAD), lambda h: (0, 0, h))
    kv_spec = pl.BlockSpec((groups, 2, rows, HEAD), lambda h: (0, 0, 0, h))
    return pl.pallas_call(
        functools.partial(attend_kernel, math.log2(math.e) / math.sqrt(HEAD)),
        grid=(heads,),
        in_specs=[pl.BlockSpec(memory_space=pltpu.SMEM), q_spec] + [kv_spec] * SPAN,
        out_specs=q_spec,
        out_shape=jax.ShapeDtypeStruct((groups, rows, cols), jnp.bfloat16),
        scratch_shapes=[pltpu.VMEM((TPS, SPAN * TPS, rows, rows), jnp.float32)],
        compiler_params=pltpu.CompilerParams(vmem_limit_bytes=32 * 1024 * 1024),
        cost_estimate=pl.CostEstimate(
            flops=4 * heads * groups * rows * keys * HEAD,
            bytes_accessed=2 * cols * (2 * groups * rows + 2 * keys),
            transcendentals=heads * groups * rows * keys,
        ),
        name="attend",
    )(bias, q, *kvs)


def tile_bias(tile_order, tile_mask, position, frames):
    pad = REACH * TPS
    padded = jnp.pad(tile_order, (pad, pad))
    near = lax.dynamic_slice_in_dim(padded, position * TPS, SPAN * TPS).reshape(SPAN, TPS)
    near_frames = position + jnp.arange(-REACH, REACH + 1, dtype=jnp.int32)[:, None]
    inside = (near_frames >= 0) & (near_frames < frames)
    spatial = near - near_frames * TPS
    own = lax.dynamic_slice_in_dim(tile_order, position * TPS, TPS) - position * TPS
    rows = lax.dynamic_slice_in_dim(tile_mask, position * TPS, TPS, 0).reshape(TPS, SPAN, TPS)
    ids = jnp.arange(TPS, dtype=jnp.int32)
    pick_q = own[:, None] == ids
    pick_k = (spatial[:, :, None] == ids) & inside[:, :, None]
    hit = (
        pick_q[:, None, None, :, None]
        & pick_k[None, :, :, None, :]
        & (rows != 0).transpose(1, 0, 2)[None, :, None, :, :]
    )
    allowed = jnp.any(hit, axis=(3, 4))
    return jnp.where(allowed, 0.0, NEG).astype(jnp.float32).reshape(-1)


def shifted(block, distance, frames):
    route = [(i, i + distance) for i in range(frames) if 0 <= i + distance < frames]
    return lax.ppermute(block, "blk", route)


def per_device(queries, keys, values, tile_order, tile_mask):
    groups = lax.axis_size("uly")
    frames = lax.axis_size("blk")
    position = lax.axis_index("blk")
    kv_parts, q_parts = pack(queries, keys, values, groups, CHUNKS)
    bias = tile_bias(tile_order, tile_mask, position, frames)
    outs = []
    for kv, q in zip(kv_parts, q_parts):
        own = lax.all_to_all(kv, "uly", split_axis=0, concat_axis=0, tiled=True)
        own_q = lax.all_to_all(q, "uly", split_axis=0, concat_axis=0, tiled=True)
        below = shifted(own, 1, frames)
        above = shifted(own, -1, frames)
        below2 = shifted(below, 1, frames)
        above2 = shifted(above, -1, frames)
        out = attend(bias, own_q, [below2, below, own, above, above2])
        outs.append(lax.all_to_all(out, "uly", split_axis=0, concat_axis=0, tiled=True))
    return unpack(outs)


def solution(mesh):
    return jax.shard_map(
        per_device,
        mesh=mesh,
        in_specs=(
            P(("blk", "uly"), None),
            P(("blk", "uly"), None),
            P(("blk", "uly"), None),
            P(),
            P(),
        ),
        out_specs=P(("blk", "uly"), None),
        check_vma=False,
    )
```

time: 360 us -> 185 us (0.51)
  the two profiles are of different devices: /device:TPU:8 before, /device:TPU:1 now
where the time goes in v1:
time: 185 us; the launch traced here: 184 us
  starting transfers between devices  90.8 us (49%)
  Pallas kernels  31.7 us (17%)
  waiting for transfers between devices  31.2 us (17%)
  blocking collectives  27.2 us (15%)
  local copies, waits for them, and re-layouts  2.18 us (1%)
    all_to_all x3, starting transfers between devices, per_device(): own_q = lax.all_to_all(q, 'uly', split_axis=0, concat_axis=0, tiled=True)  36.1 us
    ppermute x12, starting transfers between devices, shifted(): return lax.ppermute(block, 'blk', route)  35.7 us
    pallas_call x3, Pallas kernels, attend(): pl.pallas_call(functools.partial(attend_kernel, math.log2(math.e) / math....  26.6 us
    all_to_all x3, waiting for transfers between devices, per_device(): own_q = lax.all_to_all(q, 'uly', split_axis=0, concat_axis=0, tiled=True)  21.6 us
    all_to_all x1, blocking collectives, per_device(): own = lax.all_to_all(kv, 'uly', split_axis=0, concat_axis=0, tiled=True)  16 us
    all_to_all x1, blocking collectives, per_device(): lax.all_to_all(out, 'uly', split_axis=0, concat_axis=0, tiled=True)  11.2 us
    all_to_all x2, starting transfers between devices, per_device(): lax.all_to_all(out, 'uly', split_axis=0, concat_axis=0, tiled=True)  10.2 us
    all_to_all x2, starting transfers between devices, per_device(): own = lax.all_to_all(kv, 'uly', split_axis=0, concat_axis=0, tiled=True)  8.79 us
  transfers between devices with their start and end apart: 19, of which 4 were waited for; matrix products, arithmetic and copies ran while one was open for 1% of the time, Pallas kernels for 14%

profile of v1, /device:TPU:1, one launch (start us, length us, event | category | flops | bytes accessed | tf_op | source)
XLA Modules:
  0.0 183.6 jit_solution(7907950879547523943)
XLA Ops:
  0.0 3.0 %pack.1 = (bf16[4,2,128,256]{3,2,1,0:T(8,128)(2,1)}, bf16[4,2,128,256]{3,2,1,0:T(8,128)(2,1)}, bf16[4,2,128,256]{3,2,1,0:T(8,128)(2,1)}, bf16[4,128,256]{2,1,0:T...) custom-call(bf16[128,3072]{1,0:T(8,128)(2,1)} %q_ref.1, bf16[128,3072]{1,0:T(8,128)(2,1)} %k_ref.1, ...), custom_call_target="tpu_custom_call" | custom-call | tf_op jit(solution)/shard_map/pack/pallas_call | solution.py:38
  3.0 16.0 %all_to_all.45.refs_2_ = bf16[4,2,128,256]{3,2,1,0:T(8,128)(2,1)S(1)} all-to-all(bf16[4,2,128,256]{3,2,1,0:T(8,128)(2,1)} %get-tuple-element.14), channel_id=1, replica_groups=mesh['blk'=64,'uly'=4] {'uly'}, dimensions={0} | all-to-all | bytes 1048576 | tf_op jit(solution)/shard_map/all_to_all | solution.py:161
  19.0 4.5 %all-to-all-start.7 = ((bf16[4,2,128,256]{3,2,1,0:T(8,128)(2,1)}), bf16[4,2,128,256]{3,2,1,0:T(8,128)(2,1)S(1)}, u32[]{:S(2)}, u32[]{:S(2)}) async-start(bf16[4,2,128,256]{3,2,1,0:T(8,128)(2,1)} %get-tuple-element.16), calls=%async_computation.7 | async-start | bytes 1048576 | tf_op jit(solution)/shard_map/all_to_all | solution.py:161
  23.5 0.7 copy-done.3
  24.3 8.6 %all-to-all-done.7.refs_2_ = bf16[4,2,128,256]{3,2,1,0:T(8,128)(2,1)S(1)} async-done(((bf16[4,2,128,256]{3,2,1,0:T(8,128)(2,1)}), bf16[4,2,128,256]{3,2,1,0:T(8,128)(2,1)S(1)}, u32[]{:S(2)}, u32[]{:S(2)}) %all-to-all-start.7) | async-done | bytes 524320 | tf_op jit(solution)/shard_map/all_to_all | solution.py:161
  33.0 4.3 %all-to-all-start.1 = ((bf16[4,2,128,256]{3,2,1,0:T(8,128)(2,1)}), bf16[4,2,128,256]{3,2,1,0:T(8,128)(2,1)S(1)}, u32[]{:S(2)}, u32[]{:S(2)}) async-start(bf16[4,2,128,256]{3,2,1,0:T(8,128)(2,1)} %get-tuple-element.12), calls=%async_computation.1 | async-start | bytes 1048576 | tf_op jit(solution)/shard_map/all_to_all | solution.py:161
  37.3 1.3 collective-permute-start.10
  38.6 4.8 %collective-permute-start.8 = (bf16[4,2,128,256]{3,2,1,0:T(8,128)(2,1)S(1)}, bf16[4,2,128,256]{3,2,1,0:T(8,128)(2,1)}, u32[]{:S(2)}, u32[]{:S(2)}) collective-permute-start(bf16[4,2,128,256]{3,2,1,0:T(8,128)(2,1)S(1)} %all-to-all-done.7.refs_2_), channel_id=1, source_target_pairs={{0,4},{4,8},{8,12},{12,16},{16,20},{20,24},{24,28},{28,32},{32,36}... | collective-permute-start | bytes 1572872 | tf_op jit(solution)/shard_map/ppermute | solution.py:150
  43.4 1.3 collective-permute-start.6
  44.9 4.8 %collective-permute-start.4 = (bf16[4,2,128,256]{3,2,1,0:T(8,128)(2,1)S(1)}, bf16[4,2,128,256]{3,2,1,0:T(8,128)(2,1)}, u32[]{:S(2)}, u32[]{:S(2)}) collective-permute-start(bf16[4,2,128,256]{3,2,1,0:T(8,128)(2,1)S(1)} %all_to_all.45.refs_2_), channel_id=1, source_target_pairs={{0,4},{4,8},{8,12},{12,16},{16,20},{20,24},{24,28},{28,32},{32,36}... | collective-permute-start | bytes 1572872 | tf_op jit(solution)/shard_map/ppermute | solution.py:150
  49.7 5.9 %all-to-all-start = ((bf16[4,128,256]{2,1,0:T(8,128)(2,1)}), bf16[4,128,256]{2,1,0:T(8,128)(2,1)S(1)}, u32[]{:S(2)}, u32[]{:S(2)}) async-start(bf16[4,128,256]{2,1,0:T(8,128)(2,1)} %get-tuple-element.11), calls=%async_computation | async-start | bytes 524288 | tf_op jit(solution)/shard_map/all_to_all | solution.py:162
  55.6 1.3 collective-permute-start.2
  56.9 4.8 %collective-permute-start = (bf16[4,2,128,256]{3,2,1,0:T(8,128)(2,1)S(1)}, bf16[4,2,128,256]{3,2,1,0:T(8,128)(2,1)}, u32[]{:S(2)}, u32[]{:S(2)}) collective-permute-start(bf16[4,2,128,256]{3,2,1,0:T(8,128)(2,1)S(1)} %all-to-all-done.1.refs_2_), channel_id=1, source_target_pairs={{0,4},{4,8},{8,12},{12,16},{16,20},{20,24},{24,28},{28,32},{32,36}... | collective-permute-start | bytes 1572872 | tf_op jit(solution)/shard_map/ppermute | solution.py:150
  61.7 1.3 collective-permute-start.11
  63.1 0.8 collective-permute-done.6.refs_3_
  63.9 4.0 %collective-permute-start.9 = (bf16[4,2,128,256]{3,2,1,0:T(8,128)(2,1)}, bf16[4,2,128,256]{3,2,1,0:T(8,128)(2,1)}, u32[]{:S(2)}, u32[]{:S(2)}) collective-permute-start(bf16[4,2,128,256]{3,2,1,0:T(8,128)(2,1)} %collective-permute-done.8.refs_1_), channel_id=1, source_target_pairs={{0,4},{4,8},{8,12},{12,16},{16,20},{20,24},{24,28},{28,32},{32,36}... | collective-permute-start | bytes 1572872 | tf_op jit(solution)/shard_map/ppermute | solution.py:150
  68.0 14.9 %all-to-all-done.q_ref = bf16[4,128,256]{2,1,0:T(8,128)(2,1)S(1)} async-done(((bf16[4,128,256]{2,1,0:T(8,128)(2,1)}), bf16[4,128,256]{2,1,0:T(8,128)(2,1)S(1)}, u32[]{:S(2)}, u32[]{:S(2)}) %all-to-all-start) | async-done | bytes 262176 | tf_op jit(solution)/shard_map/all_to_all | solution.py:162
  83.0 26.4 %all-to-all-start.6 = ((bf16[4,128,256]{2,1,0:T(8,128)(2,1)}), bf16[4,128,256]{2,1,0:T(8,128)(2,1)S(1)}, u32[]{:S(2)}, u32[]{:S(2)}) async-start(bf16[4,128,256]{2,1,0:T(8,128)(2,1)} %get-tuple-element.15), calls=%async_computation.6 | async-start | bytes 524288 | tf_op jit(solution)/shard_map/all_to_all | solution.py:162
  109.8 1.3 collective-permute-start.7
  111.1 4.8 %collective-permute-start.5 = (bf16[4,2,128,256]{3,2,1,0:T(8,128)(2,1)}, bf16[4,2,128,256]{3,2,1,0:T(8,128)(2,1)}, u32[]{:S(2)}, u32[]{:S(2)}) collective-permute-start(bf16[4,2,128,256]{3,2,1,0:T(8,128)(2,1)} %collective-permute-done.4.refs_1_), channel_id=1, source_target_pairs={{0,4},{4,8},{8,12},{12,16},{16,20},{20,24},{24,28},{28,32},{32,36}... | collective-permute-start | bytes 1572872 | tf_op jit(solution)/shard_map/ppermute | solution.py:150
  116.0 6.7 %all-to-all-done.6.q_ref = bf16[4,128,256]{2,1,0:T(8,128)(2,1)S(1)} async-done(((bf16[4,128,256]{2,1,0:T(8,128)(2,1)}), bf16[4,128,256]{2,1,0:T(8,128)(2,1)S(1)}, u32[]{:S(2)}, u32[]{:S(2)}) %all-to-all-start.6) | async-done | bytes 262176 | tf_op jit(solution)/shard_map/all_to_all | solution.py:162
  122.7 3.8 %all-to-all-start.3 = ((bf16[4,128,256]{2,1,0:T(8,128)(2,1)}), bf16[4,128,256]{2,1,0:T(8,128)(2,1)S(1)}, u32[]{:S(2)}, u32[]{:S(2)}) async-start(bf16[4,128,256]{2,1,0:T(8,128)(2,1)} %get-tuple-element.13), calls=%async_computation.3 | async-start | bytes 524288 | tf_op jit(solution)/shard_map/all_to_all | solution.py:162
  126.6 1.3 collective-permute-start.3
  127.9 4.8 %collective-permute-start.1 = (bf16[4,2,128,256]{3,2,1,0:T(8,128)(2,1)}, bf16[4,2,128,256]{3,2,1,0:T(8,128)(2,1)}, u32[]{:S(2)}, u32[]{:S(2)}) collective-permute-start(bf16[4,2,128,256]{3,2,1,0:T(8,128)(2,1)} %collective-permute-done.refs_1_), channel_id=1, source_target_pairs={{0,4},{4,8},{8,12},{12,16},{16,20},{20,24},{24,28},{28,32},{32,36}... | collective-permute-start | bytes 1572872 | tf_op jit(solution)/shard_map/ppermute | solution.py:150
  132.9 9.1 %attend.5 = bf16[4,128,256]{2,1,0:T(8,128)(2,1)} custom-call(f32[80]{0:T(128)S(1)} %select_n.18.bias_ref, bf16[4,128,256]{2,1,0:T(8,128)(2,1)S(1)} %all-to-all-done.6.q_ref, bf16[4,2,128,256]{3,2,1,0:T(8,128)(2,1)} %collective-permute-done.9.refs_0_, bf16[4,2,128,256]{3,2,1,0:T(8,128)(2,1)} %collective-permute-done.8.refs_1_, ...), custom_call_target="tpu_custom_call" | custom-call | flops 1342177280 | bytes 3145728 | tf_op jit(solution)/shard_map/attend/pallas_call | solution.py:110
  142.0 5.4 %all-to-all-start.8 = ((bf16[4,128,256]{2,1,0:T(8,128)(2,1)}), bf16[4,128,256]{2,1,0:T(8,128)(2,1)S(1)}, u32[]{:S(2)}, u32[]{:S(2)}) async-start(bf16[4,128,256]{2,1,0:T(8,128)(2,1)} %attend.5), calls=%async_computation.8 | async-start | bytes 524288 | tf_op jit(solution)/shard_map/all_to_all | solution.py:168
  147.4 9.0 %attend.4 = bf16[4,128,256]{2,1,0:T(8,128)(2,1)} custom-call(f32[80]{0:T(128)S(1)} %select_n.18.bias_ref, bf16[4,128,256]{2,1,0:T(8,128)(2,1)S(1)} %all-to-all-done.3.q_ref, bf16[4,2,128,256]{3,2,1,0:T(8,128)(2,1)} %collective-permute-done.5.refs_0_, bf16[4,2,128,256]{3,2,1,0:T(8,128)(2,1)} %collective-permute-done.4.refs_1_, ...), custom_call_target="tpu_custom_call" | custom-call | flops 1342177280 | bytes 3145728 | tf_op jit(solution)/shard_map/attend/pallas_call | solution.py:110
  156.4 0.7 copy-done
  157.1 4.8 %all-to-all-start.5 = ((bf16[4,128,256]{2,1,0:T(8,128)(2,1)}), bf16[4,128,256]{2,1,0:T(8,128)(2,1)S(1)}, u32[]{:S(2)}, u32[]{:S(2)}) async-start(bf16[4,128,256]{2,1,0:T(8,128)(2,1)} %attend.4), calls=%async_computation.5 | async-start | bytes 524288 | tf_op jit(solution)/shard_map/all_to_all | solution.py:168
  161.9 8.4 %attend.3 = bf16[4,128,256]{2,1,0:T(8,128)(2,1)S(1)} custom-call(f32[80]{0:T(128)S(1)} %select_n.18.bias_ref, bf16[4,128,256]{2,1,0:T(8,128)(2,1)S(1)} %all-to-all-done.q_ref, bf16[4,2,128,256]{3,2,1,0:T(8,128)(2,1)} %collective-permute-done.1.refs_0_, bf16[4,2,128,256]{3,2,1,0:T(8,128)(2,1)} %collective-permute-done.refs_1_, ...), custom_call_target="tpu_custom_call" | custom-call | flops 1342177280 | bytes 3145728 | tf_op jit(solution)/shard_map/attend/pallas_call | solution.py:110
  170.4 11.2 %all_to_all.46.refs_0_ = bf16[4,128,256]{2,1,0:T(8,128)(2,1)} all-to-all(bf16[4,128,256]{2,1,0:T(8,128)(2,1)S(1)} %attend.3), channel_id=1, replica_groups=mesh['blk'=64,'uly'=4] {'uly'}, dimensions={0} | all-to-all | bytes 524288 | tf_op jit(solution)/shard_map/all_to_all | solution.py:168
  181.6 2.1 %unpack.1 = bf16[128,3072]{1,0:T(8,128)(2,1)} custom-call(bf16[4,128,256]{2,1,0:T(8,128)(2,1)} %all_to_all.46.refs_0_, bf16[4,128,256]{2,1,0:T(8,128)(2,1)} %copy-done.1, bf16[4,128,256]{2,1,0:T(8,128)(2,1)} %copy-done), custom_call_target="tpu_custom_call" | custom-call | tf_op jit(solution)/shard_map/unpack/pallas_call | solution.py:60
  (38 shorter events, 1.3 us)
Async XLA Ops:
  19.0 14.0 %all-to-all-start.7 = ((bf16[4,2,128,256]{3,2,1,0:T(8,128)(2,1)}), bf16[4,2,128,256]{3,2,1,0:T(8,128)(2,1)S(1)}, u32[]{:S(2)}, u32[]{:S(2)}) async-start(bf16[4,2,128,256]{3,2,1,0:T(8,128)(2,1)} %get-tuple-element.16), calls=%async_computation.7 | async-start | bytes 1048576 | tf_op jit(solution)/shard_map/all_to_all | solution.py:161
  23.5 0.7 copy-start.3
  33.0 16.7 %all-to-all-start.1 = ((bf16[4,2,128,256]{3,2,1,0:T(8,128)(2,1)}), bf16[4,2,128,256]{3,2,1,0:T(8,128)(2,1)S(1)}, u32[]{:S(2)}, u32[]{:S(2)}) async-start(bf16[4,2,128,256]{3,2,1,0:T(8,128)(2,1)} %get-tuple-element.12), calls=%async_computation.1 | async-start | bytes 1048576 | tf_op jit(solution)/shard_map/all_to_all | solution.py:161
  37.3 19.6 %collective-permute-start.10 = (bf16[4,2,128,256]{3,2,1,0:T(8,128)(2,1)S(1)}, bf16[4,2,128,256]{3,2,1,0:T(8,128)(2,1)}, u32[]{:S(2)}, u32[]{:S(2)}) collective-permute-start(bf16[4,2,128,256]{3,2,1,0:T(8,128)(2,1)S(1)} %all-to-all-done.7.refs_2_), channel_id=1, source_target_pairs={{4,0},{8,4},{12,8},{16,12},{20,16},{24,20},{28,24},{32,28},{36,32}... | collective-permute-start | bytes 1572872 | tf_op jit(solution)/shard_map/ppermute | solution.py:150
  38.6 23.1 %collective-permute-start.8 = (bf16[4,2,128,256]{3,2,1,0:T(8,128)(2,1)S(1)}, bf16[4,2,128,256]{3,2,1,0:T(8,128)(2,1)}, u32[]{:S(2)}, u32[]{:S(2)}) collective-permute-start(bf16[4,2,128,256]{3,2,1,0:T(8,128)(2,1)S(1)} %all-to-all-done.7.refs_2_), channel_id=1, source_target_pairs={{0,4},{4,8},{8,12},{12,16},{16,20},{20,24},{24,28},{28,32},{32,36}... | collective-permute-start | bytes 1572872 | tf_op jit(solution)/shard_map/ppermute | solution.py:150
  43.4 20.5 %collective-permute-start.6 = (bf16[4,2,128,256]{3,2,1,0:T(8,128)(2,1)S(1)}, bf16[4,2,128,256]{3,2,1,0:T(8,128)(2,1)S(1)}, u32[]{:S(2)}, u32[]{:S(2)}) collective-permute-start(bf16[4,2,128,256]{3,2,1,0:T(8,128)(2,1)S(1)} %all_to_all.45.refs_2_), channel_id=1, source_target_pairs={{4,0},{8,4},{12,8},{16,12},{20,16},{24,20},{28,24},{32,28},{36,32}... | collective-permute-start | bytes 1572872 | tf_op jit(solution)/shard_map/ppermute | solution.py:150
  44.9 64.9 %collective-permute-start.4 = (bf16[4,2,128,256]{3,2,1,0:T(8,128)(2,1)S(1)}, bf16[4,2,128,256]{3,2,1,0:T(8,128)(2,1)}, u32[]{:S(2)}, u32[]{:S(2)}) collective-permute-start(bf16[4,2,128,256]{3,2,1,0:T(8,128)(2,1)S(1)} %all_to_all.45.refs_2_), channel_id=1, source_target_pairs={{0,4},{4,8},{8,12},{12,16},{16,20},{20,24},{24,28},{28,32},{32,36}... | collective-permute-start | bytes 1572872 | tf_op jit(solution)/shard_map/ppermute | solution.py:150
  49.7 33.3 %all-to-all-start = ((bf16[4,128,256]{2,1,0:T(8,128)(2,1)}), bf16[4,128,256]{2,1,0:T(8,128)(2,1)S(1)}, u32[]{:S(2)}, u32[]{:S(2)}) async-start(bf16[4,128,256]{2,1,0:T(8,128)(2,1)} %get-tuple-element.11), calls=%async_computation | async-start | bytes 524288 | tf_op jit(solution)/shard_map/all_to_all | solution.py:162
  55.6 55.5 %collective-permute-start.2 = (bf16[4,2,128,256]{3,2,1,0:T(8,128)(2,1)S(1)}, bf16[4,2,128,256]{3,2,1,0:T(8,128)(2,1)S(1)}, u32[]{:S(2)}, u32[]{:S(2)}) collective-permute-start(bf16[4,2,128,256]{3,2,1,0:T(8,128)(2,1)S(1)} %all-to-all-done.1.refs_2_), channel_id=1, source_target_pairs={{4,0},{8,4},{12,8},{16,12},{20,16},{24,20},{28,24},{32,28},{36,32}... | collective-permute-start | bytes 1572872 | tf_op jit(solution)/shard_map/ppermute | solution.py:150
  56.9 69.6 %collective-permute-start = (bf16[4,2,128,256]{3,2,1,0:T(8,128)(2,1)S(1)}, bf16[4,2,128,256]{3,2,1,0:T(8,128)(2,1)}, u32[]{:S(2)}, u32[]{:S(2)}) collective-permute-start(bf16[4,2,128,256]{3,2,1,0:T(8,128)(2,1)S(1)} %all-to-all-done.1.refs_2_), channel_id=1, source_target_pairs={{0,4},{4,8},{8,12},{12,16},{16,20},{20,24},{24,28},{28,32},{32,36}... | collective-permute-start | bytes 1572872 | tf_op jit(solution)/shard_map/ppermute | solution.py:150
  61.7 66.1 %collective-permute-start.11 = (bf16[4,2,128,256]{3,2,1,0:T(8,128)(2,1)}, bf16[4,2,128,256]{3,2,1,0:T(8,128)(2,1)}, u32[]{:S(2)}, u32[]{:S(2)}) collective-permute-start(bf16[4,2,128,256]{3,2,1,0:T(8,128)(2,1)} %collective-permute-done.10.refs_3_), channel_id=1, source_target_pairs={{4,0},{8,4},{12,8},{16,12},{20,16},{24,20},{28,24},{32,28},{36,32}... | collective-permute-start | bytes 1572872 | tf_op jit(solution)/shard_map/ppermute | solution.py:150
  63.9 68.9 %collective-permute-start.9 = (bf16[4,2,128,256]{3,2,1,0:T(8,128)(2,1)}, bf16[4,2,128,256]{3,2,1,0:T(8,128)(2,1)}, u32[]{:S(2)}, u32[]{:S(2)}) collective-permute-start(bf16[4,2,128,256]{3,2,1,0:T(8,128)(2,1)} %collective-permute-done.8.refs_1_), channel_id=1, source_target_pairs={{0,4},{4,8},{8,12},{12,16},{16,20},{20,24},{24,28},{28,32},{32,36}... | collective-permute-start | bytes 1572872 | tf_op jit(solution)/shard_map/ppermute | solution.py:150
  82.9 26.4 %copy-start.2 = (s32[256,20]{0,1:T(8,128)S(1)}, s32[256,20]{0,1:T(8,128)}, u32[]{:S(2)}) copy-start(s32[256,20]{0,1:T(8,128)} %param.9) | copy-start | bytes 61444
  83.0 39.8 %all-to-all-start.6 = ((bf16[4,128,256]{2,1,0:T(8,128)(2,1)}), bf16[4,128,256]{2,1,0:T(8,128)(2,1)S(1)}, u32[]{:S(2)}, u32[]{:S(2)}) async-start(bf16[4,128,256]{2,1,0:T(8,128)(2,1)} %get-tuple-element.15), calls=%async_computation.6 | async-start | bytes 524288 | tf_op jit(solution)/shard_map/all_to_all | solution.py:162
  109.8 37.6 %collective-permute-start.7 = (bf16[4,2,128,256]{3,2,1,0:T(8,128)(2,1)S(1)}, bf16[4,2,128,256]{3,2,1,0:T(8,128)(2,1)}, u32[]{:S(2)}, u32[]{:S(2)}) collective-permute-start(bf16[4,2,128,256]{3,2,1,0:T(8,128)(2,1)S(1)} %collective-permute-done.6.refs_3_), channel_id=1, source_target_pairs={{4,0},{8,4},{12,8},{16,12},{20,16},{24,20},{28,24},{32,28},{36,32}... | collective-permute-start | bytes 1572872 | tf_op jit(solution)/shard_map/ppermute | solution.py:150
  111.1 36.3 %collective-permute-start.5 = (bf16[4,2,128,256]{3,2,1,0:T(8,128)(2,1)}, bf16[4,2,128,256]{3,2,1,0:T(8,128)(2,1)}, u32[]{:S(2)}, u32[]{:S(2)}) collective-permute-start(bf16[4,2,128,256]{3,2,1,0:T(8,128)(2,1)} %collective-permute-done.4.refs_1_), channel_id=1, source_target_pairs={{0,4},{4,8},{8,12},{12,16},{16,20},{20,24},{24,28},{28,32},{32,36}... | collective-permute-start | bytes 1572872 | tf_op jit(solution)/shard_map/ppermute | solution.py:150
  122.7 19.3 %all-to-all-start.3 = ((bf16[4,128,256]{2,1,0:T(8,128)(2,1)}), bf16[4,128,256]{2,1,0:T(8,128)(2,1)S(1)}, u32[]{:S(2)}, u32[]{:S(2)}) async-start(bf16[4,128,256]{2,1,0:T(8,128)(2,1)} %get-tuple-element.13), calls=%async_computation.3 | async-start | bytes 524288 | tf_op jit(solution)/shard_map/all_to_all | solution.py:162
  126.6 35.4 %collective-permute-start.3 = (bf16[4,2,128,256]{3,2,1,0:T(8,128)(2,1)S(1)}, bf16[4,2,128,256]{3,2,1,0:T(8,128)(2,1)}, u32[]{:S(2)}, u32[]{:S(2)}) collective-permute-start(bf16[4,2,128,256]{3,2,1,0:T(8,128)(2,1)S(1)} %collective-permute-done.2.refs_3_), channel_id=1, source_target_pairs={{4,0},{8,4},{12,8},{16,12},{20,16},{24,20},{28,24},{32,28},{36,32}... | collective-permute-start | bytes 1572872 | tf_op jit(solution)/shard_map/ppermute | solution.py:150
  127.9 34.1 %collective-permute-start.1 = (bf16[4,2,128,256]{3,2,1,0:T(8,128)(2,1)}, bf16[4,2,128,256]{3,2,1,0:T(8,128)(2,1)}, u32[]{:S(2)}, u32[]{:S(2)}) collective-permute-start(bf16[4,2,128,256]{3,2,1,0:T(8,128)(2,1)} %collective-permute-done.refs_1_), channel_id=1, source_target_pairs={{0,4},{4,8},{8,12},{12,16},{16,20},{20,24},{24,28},{28,32},{32,36}... | collective-permute-start | bytes 1572872 | tf_op jit(solution)/shard_map/ppermute | solution.py:150
  142.0 14.4 %all-to-all-start.8 = ((bf16[4,128,256]{2,1,0:T(8,128)(2,1)}), bf16[4,128,256]{2,1,0:T(8,128)(2,1)S(1)}, u32[]{:S(2)}, u32[]{:S(2)}) async-start(bf16[4,128,256]{2,1,0:T(8,128)(2,1)} %attend.5), calls=%async_computation.8 | async-start | bytes 524288 | tf_op jit(solution)/shard_map/all_to_all | solution.py:168
  156.4 0.7 copy-start
  157.1 13.2 %all-to-all-start.5 = ((bf16[4,128,256]{2,1,0:T(8,128)(2,1)}), bf16[4,128,256]{2,1,0:T(8,128)(2,1)S(1)}, u32[]{:S(2)}, u32[]{:S(2)}) async-start(bf16[4,128,256]{2,1,0:T(8,128)(2,1)} %attend.4), calls=%async_computation.5 | async-start | bytes 524288 | tf_op jit(solution)/shard_map/all_to_all | solution.py:168
  170.4 11.2 %copy-start.1 = (bf16[4,128,256]{2,1,0:T(8,128)(2,1)}, bf16[4,128,256]{2,1,0:T(8,128)(2,1)S(1)}, u32[]{:S(2)}) copy-start(bf16[4,128,256]{2,1,0:T(8,128)(2,1)S(1)} %all-to-all-done.5.refs_1_) | copy-start | bytes 786436

commit v2 on v1

v2 whole, which is shorter than its diff:
```python
import functools
import math

import jax
import jax.numpy as jnp
from jax import lax
from jax.experimental import pallas as pl
from jax.experimental.pallas import tpu as pltpu
from jax.sharding import PartitionSpec as P

HEAD = 128
TPS = 4
REACH = 2
SPAN = 2 * REACH + 1
CHUNKS = (3, 3)
NEG = -1e30
AXES = ("blk", "uly")


def member(u, far):
    return u if u % 2 == 0 else jnp.where(far, u ^ 2, u)


def copy_kernel(plan, groups, far_ref, *refs):
    far = far_ref[0] != 0
    for source, target, slot, first in plan:
        src, dst = refs[source], refs[target]
        width = src.shape[1] // groups
        cols = dst.shape[-1]
        for u in range(groups):
            start = pl.multiple_of(member(u, far) * width + first, HEAD)
            block = src[:, pl.ds(start, cols)]
            if slot is None:
                dst[u] = block
            else:
                dst[u, slot] = block


def pack_kv(keys, values, far, groups, chunks, skip):
    rows = keys.shape[0]
    plan, first = [], skip
    for c, n in enumerate(chunks):
        plan += [(0, 2 + c, 0, first * HEAD), (1, 2 + c, 1, first * HEAD)]
        first += n
    return pl.pallas_call(
        functools.partial(copy_kernel, plan, groups),
        in_specs=[pl.BlockSpec(memory_space=pltpu.SMEM)] + [pl.BlockSpec()] * 2,
        out_shape=[
            jax.ShapeDtypeStruct((groups, 2, rows, n * HEAD), jnp.bfloat16) for n in chunks
        ],
        name="pack_kv",
    )(far, keys, values)


def pack_q(queries, far, groups, chunks):
    rows = queries.shape[0]
    plan, first = [], 0
    for c, n in enumerate(chunks):
        plan.append((0, 1 + c, None, first * HEAD))
        first += n
    return pl.pallas_call(
        functools.partial(copy_kernel, plan, groups),
        in_specs=[pl.BlockSpec(memory_space=pltpu.SMEM), pl.BlockSpec()],
        out_shape=[jax.ShapeDtypeStruct((groups, rows, n * HEAD), jnp.bfloat16) for n in chunks],
        name="pack_q",
    )(far, queries)


def unpack_kernel(groups, far_ref, *refs):
    far = far_ref[0] != 0
    out_ref = refs[-1]
    width = out_ref.shape[1] // groups
    for u in range(groups):
        first = 0
        for ref in refs[:-1]:
            cols = ref.shape[-1]
            start = pl.multiple_of(member(u, far) * width + first, HEAD)
            out_ref[:, pl.ds(start, cols)] = ref[u]
            first += cols


def unpack(parts, far):
    groups, rows = parts[0].shape[:2]
    width = groups * sum(p.shape[-1] for p in parts)
    return pl.pallas_call(
        functools.partial(unpack_kernel, groups),
        in_specs=[pl.BlockSpec(memory_space=pltpu.SMEM)] + [pl.BlockSpec()] * len(parts),
        out_shape=jax.ShapeDtypeStruct((rows, width), jnp.bfloat16),
        name="unpack",
    )(far, *parts)


def attend_kernel(scale, bias_ref, q_ref, *refs):
    kv_refs, out_ref, s_ref = refs[:SPAN], refs[SPAN], refs[SPAN + 1]
    rows = q_ref.shape[1]
    frame_rows = TPS * rows
    q = q_ref[...].reshape(frame_rows, HEAD)
    tops = [None] * TPS
    for e in range(SPAN):
        k = kv_refs[e][:, 0].reshape(frame_rows, HEAD)
        s = lax.dot_general(k, q, (((1,), (1,)), ((), ())), preferred_element_type=jnp.float32)
        for b in range(TPS):
            for a in range(TPS):
                block = s[b * rows : (b + 1) * rows, a * rows : (a + 1) * rows]
                block = block + bias_ref[a * SPAN * TPS + e * TPS + b]
                s_ref[e * TPS + b, :, a * rows : (a + 1) * rows] = block
                top = jnp.max(block, axis=0, keepdims=True)
                tops[a] = top if tops[a] is None else jnp.maximum(tops[a], top)
    top = jnp.concatenate(tops, axis=1) * scale
    total = jnp.zeros((1, frame_rows), jnp.float32)
    accum = None
    for e in range(SPAN):
        s = s_ref[e * TPS : (e + 1) * TPS].reshape(frame_rows, frame_rows)
        w = jnp.exp2(s * scale - top)
        total = total + jnp.sum(w, axis=0, keepdims=True)
        v = kv_refs[e][:, 1].reshape(frame_rows, HEAD)
        part = lax.dot_general(
            v, w.astype(jnp.bfloat16), (((0,), (0,)), ((), ())), preferred_element_type=jnp.float32
        )
        accum = part if accum is None else accum + part
    out = (accum / total).T
    out_ref[...] = out.reshape(TPS, rows, HEAD).astype(out_ref.dtype)


def attend(bias, q, kvs, first):
    groups, rows, cols = kvs[0].shape[0], kvs[0].shape[2], kvs[0].shape[3]
    heads = cols // HEAD
    keys = SPAN * groups * rows
    kv_spec = pl.BlockSpec((groups, 2, rows, HEAD), lambda h: (0, 0, 0, h))
    return pl.pallas_call(
        functools.partial(attend_kernel, math.log2(math.e) / math.sqrt(HEAD)),
        grid=(heads,),
        in_specs=[
            pl.BlockSpec(memory_space=pltpu.SMEM),
            pl.BlockSpec((groups, rows, HEAD), lambda h: (0, 0, h + first)),
        ]
        + [kv_spec] * SPAN,
        out_specs=pl.BlockSpec((groups, rows, HEAD), lambda h: (0, 0, h)),
        out_shape=jax.ShapeDtypeStruct((groups, rows, cols), jnp.bfloat16),
        scratch_shapes=[pltpu.VMEM((SPAN * TPS, rows, TPS * rows), jnp.float32)],
        compiler_params=pltpu.CompilerParams(vmem_limit_bytes=32 * 1024 * 1024),
        cost_estimate=pl.CostEstimate(
            flops=4 * heads * groups * rows * keys * HEAD,
            bytes_accessed=2 * cols * (2 * groups * rows + 2 * keys),
            transcendentals=heads * groups * rows * keys,
        ),
        name="attend",
    )(bias, q, *kvs)


def tile_bias(tile_order, tile_mask, position, frames):
    pad = REACH * TPS
    padded = jnp.pad(tile_order, (pad, pad))
    near = lax.dynamic_slice_in_dim(padded, position * TPS, SPAN * TPS).reshape(SPAN, TPS)
    near_frames = position + jnp.arange(-REACH, REACH + 1, dtype=jnp.int32)[:, None]
    inside = (near_frames >= 0) & (near_frames < frames)
    spatial = near - near_frames * TPS
    own = lax.dynamic_slice_in_dim(tile_order, position * TPS, TPS) - position * TPS
    rows = lax.dynamic_slice_in_dim(tile_mask, position * TPS, TPS, 0).reshape(TPS, SPAN, TPS)
    ids = jnp.arange(TPS, dtype=jnp.int32)
    pick_q = own[:, None] == ids
    pick_k = (spatial[:, :, None] == ids) & inside[:, :, None]
    hit = (
        pick_q[:, None, None, :, None]
        & pick_k[None, :, :, None, :]
        & (rows != 0).transpose(1, 0, 2)[None, :, None, :, :]
    )
    allowed = jnp.any(hit, axis=(3, 4))
    return jnp.where(allowed, 0.0, NEG).astype(jnp.float32).reshape(-1)


def shifted(block, distance, frames, groups):
    route = []
    for i in range(frames):
        j = i + distance
        if 0 <= j < frames:
            trade = (i < frames // 2) != (j < frames // 2)
            for u in range(groups):
                to = u ^ 2 if trade and u % 2 else u
                route.append((i * groups + u, j * groups + to))
    return lax.ppermute(block, AXES, route)


def after(x, *others):
    return lax.optimization_barrier((x, *others))[0]


def exchanged(x):
    return lax.all_to_all(x, "uly", split_axis=0, concat_axis=0, tiled=True)


def per_device(queries, keys, values, tile_order, tile_mask):
    groups = lax.axis_size("uly")
    frames = lax.axis_size("blk")
    position = lax.axis_index("blk")
    far = (position >= frames // 2).astype(jnp.int32).reshape(1)
    (kv0,) = pack_kv(keys, values, far, groups, CHUNKS[:1], 0)
    (kv1,) = pack_kv(keys, values, far, groups, CHUNKS[1:], CHUNKS[0])
    (q,) = pack_q(queries, far, groups, (sum(CHUNKS),))
    bias = tile_bias(tile_order, tile_mask, position, frames)
    move = functools.partial(shifted, frames=frames, groups=groups)

    own0 = exchanged(kv0)
    up0, down0 = move(own0, 1), move(own0, -1)
    own1 = exchanged(after(kv1, own0))
    own_q = exchanged(after(q, up0))
    up1, down1 = move(own1, 1), move(own1, -1)
    up0b, down0b = move(up0, 1), move(down0, -1)
    up1b, down1b = move(up1, 1), move(down1, -1)
    out0 = attend(bias, own_q, [up0b, up0, own0, down0, down0b], 0)
    res0 = exchanged(out0)
    out1 = attend(bias, own_q, [up1b, up1, own1, down1, down1b], CHUNKS[0])
    res1 = exchanged(out1)
    return unpack([res0, res1], far)


def solution(mesh):
    return jax.shard_map(
        per_device,
        mesh=mesh,
        in_specs=(
            P(AXES, None),
            P(AXES, None),
            P(AXES, None),
            P(),
            P(),
        ),
        out_specs=P(AXES, None),
        check_vma=False,
    )
```

time: 185 us -> 126 us (0.68)
  the two profiles are of different devices: /device:TPU:1 before, /device:TPU:8 now
where the time goes in v2:
time: 126 us; the launch traced here: 125 us
  starting transfers between devices  62 us (49%)
  waiting for transfers between devices  25.1 us (20%)
  Pallas kernels  24.3 us (19%)
  blocking collectives  12.2 us (10%)
    ppermute x8, starting transfers between devices, shifted(): return lax.ppermute(block, AXES, route)  46.2 us
    all_to_all x4, waiting for transfers between devices, exchanged(): return lax.all_to_all(x, 'uly', split_axis=0, concat_axis=0, tiled=True)  18.8 us
    all_to_all x4, starting transfers between devices, exchanged(): return lax.all_to_all(x, 'uly', split_axis=0, concat_axis=0, tiled=True)  15.7 us
    pallas_call x2, Pallas kernels, attend(): pl.pallas_call(functools.partial(attend_kernel, math.log2(math.e) / math....  15.5 us
    all_to_all x1, blocking collectives, exchanged(): return lax.all_to_all(x, 'uly', split_axis=0, concat_axis=0, tiled=True)  12.2 us
    ppermute x8, waiting for transfers between devices, shifted(): return lax.ppermute(block, AXES, route)  6.32 us
    pallas_call x2, Pallas kernels, pack_kv(): pl.pallas_call(functools.partial(copy_kernel, plan, groups), in_specs=[pl...  4.66 us
  transfers between devices with their start and end apart: 12, of which 7 were waited for; matrix products, arithmetic and copies ran while one was open for 1% of the time, Pallas kernels for 16%

profile of v2, /device:TPU:8, one launch (start us, length us, event | category | flops | bytes accessed | tf_op | source)
XLA Modules:
  0.0 125.0 jit_solution(17327138248284460529)
XLA Ops:
  0.0 2.3 %pack_kv.2 = bf16[4,2,128,384]{3,2,1,0:T(8,128)(2,1)} custom-call(s32[1]{0:T(128)} %bitcast.far_ref, bf16[128,3072]{1,0:T(8,128)(2,1)} %refs_0_.5, bf16[128,3072]{1,0:T(8,128)(2,1)} %refs_1_.3), custom_call_target="tpu_custom_call" | custom-call | tf_op jit(solution)/shard_map/pack_kv/pallas_call | solution.py:45
  2.3 3.6 %all-to-all-start = ((bf16[4,2,128,384]{3,2,1,0:T(8,128)(2,1)}), bf16[4,2,128,384]{3,2,1,0:T(8,128)(2,1)S(1)}, u32[]{:S(2)}, u32[]{:S(2)}) async-start(bf16[4,2,128,384]{3,2,1,0:T(8,128)(2,1)} %pack_kv.2), calls=%async_computation | async-start | bytes 1572864 | tf_op jit(solution)/shard_map/all_to_all | solution.py:189
  5.9 2.3 %pack_kv.3 = bf16[4,2,128,384]{3,2,1,0:T(8,128)(2,1)} custom-call(s32[1]{0:T(128)} %bitcast.far_ref, bf16[128,3072]{1,0:T(8,128)(2,1)} %refs_0_.5, bf16[128,3072]{1,0:T(8,128)(2,1)} %refs_1_.3), custom_call_target="tpu_custom_call" | custom-call | tf_op jit(solution)/shard_map/pack_kv/pallas_call | solution.py:45
  8.2 10.8 %all-to-all-done.refs_2_ = bf16[4,2,128,384]{3,2,1,0:T(8,128)(2,1)S(1)} async-done(((bf16[4,2,128,384]{3,2,1,0:T(8,128)(2,1)}), bf16[4,2,128,384]{3,2,1,0:T(8,128)(2,1)S(1)}, u32[]{:S(2)}, u32[]{:S(2)}) %all-to-all-start) | async-done | bytes 786464 | tf_op jit(solution)/shard_map/all_to_all | solution.py:189
  19.0 3.5 %all-to-all-start.3 = ((bf16[4,2,128,384]{3,2,1,0:T(8,128)(2,1)}), bf16[4,2,128,384]{3,2,1,0:T(8,128)(2,1)S(1)}, u32[]{:S(2)}, u32[]{:S(2)}) async-start(bf16[4,2,128,384]{3,2,1,0:T(8,128)(2,1)} %pack_kv.3), calls=%async_computation.3 | async-start | bytes 1572864 | tf_op jit(solution)/shard_map/all_to_all | solution.py:189
  22.5 3.8 %collective-permute-start = (bf16[4,2,128,384]{3,2,1,0:T(8,128)(2,1)S(1)}, bf16[4,2,128,384]{3,2,1,0:T(8,128)(2,1)S(1)}, u32[]{:S(2)}, u32[]{:S(2)}) collective-permute-start(bf16[4,2,128,384]{3,2,1,0:T(8,128)(2,1)S(1)} %all-to-all-done.refs_2_), channel_id=1, source_target_pairs={{0,4},{1,5},{2,6},{3,7},{4,8},{5,9},{6,10},{7,11},{8,12},{9,13},{1... | collective-permute-start | bytes 2359304 | tf_op jit(solution)/shard_map/ppermute | solution.py:181
  26.4 8.8 %collective-permute-start.2 = (bf16[4,2,128,384]{3,2,1,0:T(8,128)(2,1)S(1)}, bf16[4,2,128,384]{3,2,1,0:T(8,128)(2,1)}, u32[]{:S(2)}, u32[]{:S(2)}) collective-permute-start(bf16[4,2,128,384]{3,2,1,0:T(8,128)(2,1)S(1)} %all-to-all-done.refs_2_), channel_id=1, source_target_pairs={{4,0},{5,1},{6,2},{7,3},{8,4},{9,5},{10,6},{11,7},{12,8},{13,9},{1... | collective-permute-start | bytes 2359304 | tf_op jit(solution)/shard_map/ppermute | solution.py:181
  35.3 0.4 all-to-all-done.3.refs_2_
  35.7 3.8 %collective-permute-start.4 = (bf16[4,2,128,384]{3,2,1,0:T(8,128)(2,1)S(1)}, bf16[4,2,128,384]{3,2,1,0:T(8,128)(2,1)}, u32[]{:S(2)}, u32[]{:S(2)}) collective-permute-start(bf16[4,2,128,384]{3,2,1,0:T(8,128)(2,1)S(1)} %all-to-all-done.3.refs_2_), channel_id=1, source_target_pairs={{0,4},{1,5},{2,6},{3,7},{4,8},{5,9},{6,10},{7,11},{8,12},{9,13},{1... | collective-permute-start | bytes 2359304 | tf_op jit(solution)/shard_map/ppermute | solution.py:181
  39.5 9.7 %collective-permute-start.6 = (bf16[4,2,128,384]{3,2,1,0:T(8,128)(2,1)S(1)}, bf16[4,2,128,384]{3,2,1,0:T(8,128)(2,1)}, u32[]{:S(2)}, u32[]{:S(2)}) collective-permute-start(bf16[4,2,128,384]{3,2,1,0:T(8,128)(2,1)S(1)} %all-to-all-done.3.refs_2_), channel_id=1, source_target_pairs={{4,0},{5,1},{6,2},{7,3},{8,4},{9,5},{10,6},{11,7},{12,8},{13,9},{1... | collective-permute-start | bytes 2359304 | tf_op jit(solution)/shard_map/ppermute | solution.py:181
  49.4 0.1 copy.14
  49.5 2.1 %pack_q.1 = bf16[4,128,768]{2,1,0:T(8,128)(2,1)} custom-call(s32[1]{0:T(128)} %bitcast.far_ref, bf16[128,3072]{1,0:T(8,128)(2,1)} %refs_0_.3), custom_call_target="tpu_custom_call" | custom-call | tf_op jit(solution)/shard_map/pack_q/pallas_call | solution.py:61
  51.7 1.9 %collective-permute-start.1 = (bf16[4,2,128,384]{3,2,1,0:T(8,128)(2,1)S(1)}, bf16[4,2,128,384]{3,2,1,0:T(8,128)(2,1)}, u32[]{:S(2)}, u32[]{:S(2)}) collective-permute-start(bf16[4,2,128,384]{3,2,1,0:T(8,128)(2,1)S(1)} %collective-permute-done.refs_1_), channel_id=1, source_target_pairs={{0,4},{1,5},{2,6},{3,7},{4,8},{5,9},{6,10},{7,11},{8,12},{9,13},{1... | collective-permute-start | bytes 2359304 | tf_op jit(solution)/shard_map/ppermute | solution.py:181
  53.6 8.1 %collective-permute-start.3 = (bf16[4,2,128,384]{3,2,1,0:T(8,128)(2,1)}, bf16[4,2,128,384]{3,2,1,0:T(8,128)(2,1)}, u32[]{:S(2)}, u32[]{:S(2)}) collective-permute-start(bf16[4,2,128,384]{3,2,1,0:T(8,128)(2,1)} %collective-permute-done.2.refs_3_), channel_id=1, source_target_pairs={{4,0},{5,1},{6,2},{7,3},{8,4},{9,5},{10,6},{11,7},{12,8},{13,9},{1... | collective-permute-start | bytes 2359304 | tf_op jit(solution)/shard_map/ppermute | solution.py:181
  61.8 4.3 %all-to-all-start.1 = ((bf16[4,128,768]{2,1,0:T(8,128)(2,1)}), bf16[4,128,768]{2,1,0:T(8,128)(2,1)S(1)}, u32[]{:S(2)}, u32[]{:S(2)}) async-start(bf16[4,128,768]{2,1,0:T(8,128)(2,1)} %pack_q.1), calls=%async_computation.1 | async-start | bytes 1572864 | tf_op jit(solution)/shard_map/all_to_all | solution.py:189
  66.2 0.1 copy.19
  66.3 0.1 ne.11
  66.4 0.1 copy.16
  66.5 2.1 %collective-permute-done.4.refs_1_ = bf16[4,2,128,384]{3,2,1,0:T(8,128)(2,1)} collective-permute-done((bf16[4,2,128,384]{3,2,1,0:T(8,128)(2,1)S(1)}, bf16[4,2,128,384]{3,2,1,0:T(8,128)(2,1)}, u32[]{:S(2)}, u32[]{:S(2)}) %collective-permute-start.4) | collective-permute-done | bytes 786464 | tf_op jit(solution)/shard_map/ppermute | solution.py:181
  68.6 1.9 %collective-permute-start.5 = (bf16[4,2,128,384]{3,2,1,0:T(8,128)(2,1)}, bf16[4,2,128,384]{3,2,1,0:T(8,128)(2,1)}, u32[]{:S(2)}, u32[]{:S(2)}) collective-permute-start(bf16[4,2,128,384]{3,2,1,0:T(8,128)(2,1)} %collective-permute-done.4.refs_1_), channel_id=1, source_target_pairs={{0,4},{1,5},{2,6},{3,7},{4,8},{5,9},{6,10},{7,11},{8,12},{9,13},{1... | collective-permute-start | bytes 2359304 | tf_op jit(solution)/shard_map/ppermute | solution.py:181
  70.6 8.1 %collective-permute-start.7 = (bf16[4,2,128,384]{3,2,1,0:T(8,128)(2,1)}, bf16[4,2,128,384]{3,2,1,0:T(8,128)(2,1)}, u32[]{:S(2)}, u32[]{:S(2)}) collective-permute-start(bf16[4,2,128,384]{3,2,1,0:T(8,128)(2,1)} %collective-permute-done.6.refs_3_), channel_id=1, source_target_pairs={{4,0},{5,1},{6,2},{7,3},{8,4},{9,5},{10,6},{11,7},{12,8},{13,9},{1... | collective-permute-start | bytes 2359304 | tf_op jit(solution)/shard_map/ppermute | solution.py:181
  78.8 0.1 and_reduce_fusion
  78.9 0.1 copy.17
  79.1 0.1 select_n.18.bias_ref
  79.1 7.6 %all-to-all-done.1.q_ref = bf16[4,128,768]{2,1,0:T(8,128)(2,1)S(1)} async-done(((bf16[4,128,768]{2,1,0:T(8,128)(2,1)}), bf16[4,128,768]{2,1,0:T(8,128)(2,1)S(1)}, u32[]{:S(2)}, u32[]{:S(2)}) %all-to-all-start.1) | async-done | bytes 786464 | tf_op jit(solution)/shard_map/all_to_all | solution.py:189
  86.7 8.0 %attend.2 = bf16[4,128,384]{2,1,0:T(8,128)(2,1)} custom-call(f32[80]{0:T(128)S(1)} %select_n.18.bias_ref, bf16[4,128,768]{2,1,0:T(8,128)(2,1)S(1)} %all-to-all-done.1.q_ref, bf16[4,2,128,384]{3,2,1,0:T(8,128)(2,1)} %collective-permute-done.1.refs_0_, bf16[4,2,128,384]{3,2,1,0:T(8,128)(2,1)S(1)} %collective-permute-done.refs_1_, ...), custom_call_target="tpu_custom_call" | custom-call | flops 2013265920 | bytes 4718592 | tf_op jit(solution)/shard_map/attend/pallas_call | solution.py:130
  94.7 4.4 %all-to-all-start.2 = ((bf16[4,128,384]{2,1,0:T(8,128)(2,1)}), bf16[4,128,384]{2,1,0:T(8,128)(2,1)S(1)}, u32[]{:S(2)}, u32[]{:S(2)}) async-start(bf16[4,128,384]{2,1,0:T(8,128)(2,1)} %attend.2), calls=%async_computation.2 | async-start | bytes 786432 | tf_op jit(solution)/shard_map/all_to_all | solution.py:189
  99.1 3.1 %collective-permute-done.5.refs_0_ = bf16[4,2,128,384]{3,2,1,0:T(8,128)(2,1)} collective-permute-done((bf16[4,2,128,384]{3,2,1,0:T(8,128)(2,1)}, bf16[4,2,128,384]{3,2,1,0:T(8,128)(2,1)}, u32[]{:S(2)}, u32[]{:S(2)}) %collective-permute-start.5) | collective-permute-done | bytes 786464 | tf_op jit(solution)/shard_map/ppermute | solution.py:181
  102.2 1.1 collective-permute-done.7.refs_4_
  103.3 7.4 %attend.3 = bf16[4,128,384]{2,1,0:T(8,128)(2,1)S(1)} custom-call(f32[80]{0:T(128)S(1)} %select_n.18.bias_ref, bf16[4,128,768]{2,1,0:T(8,128)(2,1)S(1)} %all-to-all-done.1.q_ref, bf16[4,2,128,384]{3,2,1,0:T(8,128)(2,1)} %collective-permute-done.5.refs_0_, bf16[4,2,128,384]{3,2,1,0:T(8,128)(2,1)} %collective-permute-done.4.refs_1_, ...), custom_call_target="tpu_custom_call" | custom-call | flops 2013265920 | bytes 4718592 | tf_op jit(solution)/shard_map/attend/pallas_call | solution.py:130
  110.7 12.2 %all_to_all.25.refs_1_ = bf16[4,128,384]{2,1,0:T(8,128)(2,1)} all-to-all(bf16[4,128,384]{2,1,0:T(8,128)(2,1)S(1)} %attend.3), channel_id=1, replica_groups=mesh['blk'=64,'uly'=4] {'uly'}, dimensions={0} | all-to-all | bytes 786432 | tf_op jit(solution)/shard_map/all_to_all | solution.py:189
  123.0 2.1 %unpack.1 = bf16[128,3072]{1,0:T(8,128)(2,1)} custom-call(s32[1]{0:T(128)} %bitcast.far_ref, bf16[4,128,384]{2,1,0:T(8,128)(2,1)} %copy-done, bf16[4,128,384]{2,1,0:T(8,128)(2,1)} %all_to_all.25.refs_1_), custom_call_target="tpu_custom_call" | custom-call | tf_op jit(solution)/shard_map/unpack/pallas_call | solution.py:85
  (22 shorter events, 0.6 us)
Async XLA Ops:
  2.3 16.7 %all-to-all-start = ((bf16[4,2,128,384]{3,2,1,0:T(8,128)(2,1)}), bf16[4,2,128,384]{3,2,1,0:T(8,128)(2,1)S(1)}, u32[]{:S(2)}, u32[]{:S(2)}) async-start(bf16[4,2,128,384]{3,2,1,0:T(8,128)(2,1)} %pack_kv.2), calls=%async_computation | async-start | bytes 1572864 | tf_op jit(solution)/shard_map/all_to_all | solution.py:189
  19.0 16.6 %all-to-all-start.3 = ((bf16[4,2,128,384]{3,2,1,0:T(8,128)(2,1)}), bf16[4,2,128,384]{3,2,1,0:T(8,128)(2,1)S(1)}, u32[]{:S(2)}, u32[]{:S(2)}) async-start(bf16[4,2,128,384]{3,2,1,0:T(8,128)(2,1)} %pack_kv.3), calls=%async_computation.3 | async-start | bytes 1572864 | tf_op jit(solution)/shard_map/all_to_all | solution.py:189
  22.5 29.1 %collective-permute-start = (bf16[4,2,128,384]{3,2,1,0:T(8,128)(2,1)S(1)}, bf16[4,2,128,384]{3,2,1,0:T(8,128)(2,1)S(1)}, u32[]{:S(2)}, u32[]{:S(2)}) collective-permute-start(bf16[4,2,128,384]{3,2,1,0:T(8,128)(2,1)S(1)} %all-to-all-done.refs_2_), channel_id=1, source_target_pairs={{0,4},{1,5},{2,6},{3,7},{4,8},{5,9},{6,10},{7,11},{8,12},{9,13},{1... | collective-permute-start | bytes 2359304 | tf_op jit(solution)/shard_map/ppermute | solution.py:181
  26.4 27.2 %collective-permute-start.2 = (bf16[4,2,128,384]{3,2,1,0:T(8,128)(2,1)S(1)}, bf16[4,2,128,384]{3,2,1,0:T(8,128)(2,1)}, u32[]{:S(2)}, u32[]{:S(2)}) collective-permute-start(bf16[4,2,128,384]{3,2,1,0:T(8,128)(2,1)S(1)} %all-to-all-done.refs_2_), channel_id=1, source_target_pairs={{4,0},{5,1},{6,2},{7,3},{8,4},{9,5},{10,6},{11,7},{12,8},{13,9},{1... | collective-permute-start | bytes 2359304 | tf_op jit(solution)/shard_map/ppermute | solution.py:181
  35.2 13.9 %copy-start.2 = (s32[256]{0:T(256)S(1)}, s32[256]{0:T(256)}, u32[]{:S(2)}) copy-start(s32[256]{0:T(256)} %param.8) | copy-start | bytes 3076
  35.7 33.0 %collective-permute-start.4 = (bf16[4,2,128,384]{3,2,1,0:T(8,128)(2,1)S(1)}, bf16[4,2,128,384]{3,2,1,0:T(8,128)(2,1)}, u32[]{:S(2)}, u32[]{:S(2)}) collective-permute-start(bf16[4,2,128,384]{3,2,1,0:T(8,128)(2,1)S(1)} %all-to-all-done.3.refs_2_), channel_id=1, source_target_pairs={{0,4},{1,5},{2,6},{3,7},{4,8},{5,9},{6,10},{7,11},{8,12},{9,13},{1... | collective-permute-start | bytes 2359304 | tf_op jit(solution)/shard_map/ppermute | solution.py:181
  39.5 31.1 %collective-permute-start.6 = (bf16[4,2,128,384]{3,2,1,0:T(8,128)(2,1)S(1)}, bf16[4,2,128,384]{3,2,1,0:T(8,128)(2,1)}, u32[]{:S(2)}, u32[]{:S(2)}) collective-permute-start(bf16[4,2,128,384]{3,2,1,0:T(8,128)(2,1)S(1)} %all-to-all-done.3.refs_2_), channel_id=1, source_target_pairs={{4,0},{5,1},{6,2},{7,3},{8,4},{9,5},{10,6},{11,7},{12,8},{13,9},{1... | collective-permute-start | bytes 2359304 | tf_op jit(solution)/shard_map/ppermute | solution.py:181
  49.5 12.3 %copy-start.1 = (s32[256,20]{0,1:T(8,128)S(1)}, s32[256,20]{0,1:T(8,128)}, u32[]{:S(2)}) copy-start(s32[256,20]{0,1:T(8,128)} %param.9) | copy-start | bytes 61444
  51.7 35.0 %collective-permute-start.1 = (bf16[4,2,128,384]{3,2,1,0:T(8,128)(2,1)S(1)}, bf16[4,2,128,384]{3,2,1,0:T(8,128)(2,1)}, u32[]{:S(2)}, u32[]{:S(2)}) collective-permute-start(bf16[4,2,128,384]{3,2,1,0:T(8,128)(2,1)S(1)} %collective-permute-done.refs_1_), channel_id=1, source_target_pairs={{0,4},{1,5},{2,6},{3,7},{4,8},{5,9},{6,10},{7,11},{8,12},{9,13},{1... | collective-permute-start | bytes 2359304 | tf_op jit(solution)/shard_map/ppermute | solution.py:181
  53.6 33.1 %collective-permute-start.3 = (bf16[4,2,128,384]{3,2,1,0:T(8,128)(2,1)}, bf16[4,2,128,384]{3,2,1,0:T(8,128)(2,1)}, u32[]{:S(2)}, u32[]{:S(2)}) collective-permute-start(bf16[4,2,128,384]{3,2,1,0:T(8,128)(2,1)} %collective-permute-done.2.refs_3_), channel_id=1, source_target_pairs={{4,0},{5,1},{6,2},{7,3},{8,4},{9,5},{10,6},{11,7},{12,8},{13,9},{1... | collective-permute-start | bytes 2359304 | tf_op jit(solution)/shard_map/ppermute | solution.py:181
  61.8 24.9 %all-to-all-start.1 = ((bf16[4,128,768]{2,1,0:T(8,128)(2,1)}), bf16[4,128,768]{2,1,0:T(8,128)(2,1)S(1)}, u32[]{:S(2)}, u32[]{:S(2)}) async-start(bf16[4,128,768]{2,1,0:T(8,128)(2,1)} %pack_q.1), calls=%async_computation.1 | async-start | bytes 1572864 | tf_op jit(solution)/shard_map/all_to_all | solution.py:189
  68.6 33.6 %collective-permute-start.5 = (bf16[4,2,128,384]{3,2,1,0:T(8,128)(2,1)}, bf16[4,2,128,384]{3,2,1,0:T(8,128)(2,1)}, u32[]{:S(2)}, u32[]{:S(2)}) collective-permute-start(bf16[4,2,128,384]{3,2,1,0:T(8,128)(2,1)} %collective-permute-done.4.refs_1_), channel_id=1, source_target_pairs={{0,4},{1,5},{2,6},{3,7},{4,8},{5,9},{6,10},{7,11},{8,12},{9,13},{1... | collective-permute-start | bytes 2359304 | tf_op jit(solution)/shard_map/ppermute | solution.py:181
  70.6 32.7 %collective-permute-start.7 = (bf16[4,2,128,384]{3,2,1,0:T(8,128)(2,1)}, bf16[4,2,128,384]{3,2,1,0:T(8,128)(2,1)}, u32[]{:S(2)}, u32[]{:S(2)}) collective-permute-start(bf16[4,2,128,384]{3,2,1,0:T(8,128)(2,1)} %collective-permute-done.6.refs_3_), channel_id=1, source_target_pairs={{4,0},{5,1},{6,2},{7,3},{8,4},{9,5},{10,6},{11,7},{12,8},{13,9},{1... | collective-permute-start | bytes 2359304 | tf_op jit(solution)/shard_map/ppermute | solution.py:181
  94.7 16.0 %all-to-all-start.2 = ((bf16[4,128,384]{2,1,0:T(8,128)(2,1)}), bf16[4,128,384]{2,1,0:T(8,128)(2,1)S(1)}, u32[]{:S(2)}, u32[]{:S(2)}) async-start(bf16[4,128,384]{2,1,0:T(8,128)(2,1)} %attend.2), calls=%async_computation.2 | async-start | bytes 786432 | tf_op jit(solution)/shard_map/all_to_all | solution.py:189
  110.7 12.2 %copy-start = (bf16[4,128,384]{2,1,0:T(8,128)(2,1)}, bf16[4,128,384]{2,1,0:T(8,128)(2,1)S(1)}, u32[]{:S(2)}) copy-start(bf16[4,128,384]{2,1,0:T(8,128)(2,1)S(1)} %all-to-all-done.2.refs_0_) | copy-start | bytes 1179652

commit v3 on v2

v3 whole, which is shorter than its diff:
```python
import functools
import math

import jax
import jax.numpy as jnp
from jax import lax
from jax.experimental import pallas as pl
from jax.experimental.pallas import tpu as pltpu
from jax.sharding import PartitionSpec as P

HEAD = 128
TPS = 4
REACH = 2
SPAN = 2 * REACH + 1
CHUNKS = (3, 3)
NEG = -1e30
AXES = ("blk", "uly")


def run_copies(pairs, sems):
    copies = [pltpu.make_async_copy(src, dst, sems.at[i]) for i, (src, dst) in enumerate(pairs)]
    for copy in copies:
        copy.start()
    for copy in copies:
        copy.wait()


def pack_kv_kernel(groups, skip, k_ref, v_ref, out_ref, sems):
    width, cols = k_ref.shape[1] // groups, out_ref.shape[-1]
    pairs = []
    for u in range(groups):
        at = pl.ds(u * width + skip * HEAD, cols)
        pairs += [(k_ref.at[:, at], out_ref.at[u, 0]), (v_ref.at[:, at], out_ref.at[u, 1])]
    run_copies(pairs, sems)


def pack_kv(keys, values, groups, heads, skip):
    rows = keys.shape[0]
    return pl.pallas_call(
        functools.partial(pack_kv_kernel, groups, skip),
        in_specs=[pl.BlockSpec(memory_space=pl.ANY)] * 2,
        out_shape=jax.ShapeDtypeStruct((groups, 2, rows, heads * HEAD), jnp.bfloat16),
        scratch_shapes=[pltpu.SemaphoreType.DMA((2 * groups,))],
        name="pack_kv",
    )(keys, values)


def pack_q_kernel(groups, q_ref, out_ref, sems):
    width = q_ref.shape[1] // groups
    run_copies(
        [(q_ref.at[:, pl.ds(u * width, width)], out_ref.at[u]) for u in range(groups)], sems
    )


def pack_q(queries, groups):
    rows, cols = queries.shape
    return pl.pallas_call(
        functools.partial(pack_q_kernel, groups),
        in_specs=[pl.BlockSpec(memory_space=pl.ANY)],
        out_shape=jax.ShapeDtypeStruct((groups, rows, cols // groups), jnp.bfloat16),
        scratch_shapes=[pltpu.SemaphoreType.DMA((groups,))],
        name="pack_q",
    )(queries)


def unpack_kernel(groups, place_ref, first_ref, *refs):
    rest, out_ref = refs[:groups], refs[groups]
    width, cols = out_ref.shape[1] // groups, first_ref.shape[-1]
    place = place_ref[0]
    for u in range(groups):
        out_ref[:, u * width : u * width + cols] = first_ref[u]
    for t in range(groups):
        start = pl.multiple_of((place ^ t) * width + cols, HEAD)
        out_ref[:, pl.ds(start, width - cols)] = rest[t][...]


def unpack(place, first, rest):
    groups, rows, cols = first.shape
    width = groups * (cols + rest[0].shape[-1])
    return pl.pallas_call(
        functools.partial(unpack_kernel, groups),
        in_specs=[pl.BlockSpec(memory_space=pltpu.SMEM)] + [pl.BlockSpec()] * (1 + groups),
        out_shape=jax.ShapeDtypeStruct((rows, width), jnp.bfloat16),
        name="unpack",
    )(place, first, *rest)


def attend_kernel(scale, offsets, carried, final, spread, bias_ref, place_ref, q_ref, *refs):
    count = len(offsets)
    kv_refs, refs = refs[:count], refs[count:]
    s_ref, o_ref, refs = refs[-2], refs[-1], refs[:-2]
    rows = q_ref.shape[1]
    frame_rows = TPS * rows
    q = q_ref[...].reshape(frame_rows, HEAD)
    tops = [None] * TPS
    for i, offset in enumerate(offsets):
        e = offset + REACH
        k = kv_refs[i][:, 0].reshape(frame_rows, HEAD)
        s = lax.dot_general(k, q, (((1,), (1,)), ((), ())), preferred_element_type=jnp.float32)
        for b in range(TPS):
            for a in range(TPS):
                block = s[b * rows : (b + 1) * rows, a * rows : (a + 1) * rows]
                block = block + bias_ref[a * SPAN * TPS + e * TPS + b]
                s_ref[i * TPS + b, :, a * rows : (a + 1) * rows] = block
                top = jnp.max(block, axis=0, keepdims=True)
                tops[a] = top if tops[a] is None else jnp.maximum(tops[a], top)
    top = jnp.concatenate(tops, axis=1) * scale
    if carried:
        accum_ref, stats_ref = refs[:2]
        refs = refs[2:]
        before = stats_ref[0, 0:1]
        top = jnp.maximum(top, before)
        factor = jnp.exp2(before - top)
        total = stats_ref[0, 1:2] * factor
        accum = accum_ref[0] * factor
    else:
        total = jnp.zeros((1, frame_rows), jnp.float32)
        accum = None
    for i in range(count):
        s = s_ref[i * TPS : (i + 1) * TPS].reshape(frame_rows, frame_rows)
        w = jnp.exp2(s * scale - top)
        total = total + jnp.sum(w, axis=0, keepdims=True)
        v = kv_refs[i][:, 1].reshape(frame_rows, HEAD)
        part = lax.dot_general(
            v, w.astype(jnp.bfloat16), (((0,), (0,)), ((), ())), preferred_element_type=jnp.float32
        )
        accum = part if accum is None else accum + part
    if final:
        out = (accum / total).T.reshape(TPS, rows, HEAD).astype(jnp.bfloat16)
        if spread:
            o_ref[...] = out
            for t in range(TPS):
                refs[t][...] = o_ref[place_ref[0] ^ t]
        else:
            refs[0][...] = out
    else:
        refs[0][0] = accum
        refs[1][0, 0:1] = top
        refs[1][0, 1:2] = total


def attend(bias, place, q, kvs, first, carry=None, final=True, spread=False):
    offsets = sorted(kvs)
    groups, _, rows, cols = kvs[offsets[0]].shape
    heads = cols // HEAD
    queries = groups * rows
    keys = len(offsets) * queries
    kv_spec = pl.BlockSpec((groups, 2, rows, HEAD), lambda h: (0, 0, 0, h))
    state_specs = [
        pl.BlockSpec((1, HEAD, queries), lambda h: (h, 0, 0)),
        pl.BlockSpec((1, 2, queries), lambda h: (h, 0, 0)),
    ]
    if spread:
        out_specs = [pl.BlockSpec((rows, HEAD), lambda h: (0, h))] * groups
        out_shape = [jax.ShapeDtypeStruct((rows, cols), jnp.bfloat16)] * groups
    elif final:
        out_specs = pl.BlockSpec((groups, rows, HEAD), lambda h: (0, 0, h))
        out_shape = jax.ShapeDtypeStruct((groups, rows, cols), jnp.bfloat16)
    else:
        out_specs = state_specs
        out_shape = [
            jax.ShapeDtypeStruct((heads, HEAD, queries), jnp.float32),
            jax.ShapeDtypeStruct((heads, 2, queries), jnp.float32),
        ]
    return pl.pallas_call(
        functools.partial(
            attend_kernel,
            math.log2(math.e) / math.sqrt(HEAD),
            offsets,
            carry is not None,
            final,
            spread,
        ),
        grid=(heads,),
        in_specs=[
            pl.BlockSpec(memory_space=pltpu.SMEM),
            pl.BlockSpec(memory_space=pltpu.SMEM),
            pl.BlockSpec((groups, rows, HEAD), lambda h: (0, 0, h + first)),
        ]
        + [kv_spec] * len(offsets)
        + (state_specs if carry is not None else []),
        out_specs=out_specs,
        out_shape=out_shape,
        scratch_shapes=[
            pltpu.VMEM((len(offsets) * TPS, rows, queries), jnp.float32),
            pltpu.VMEM((TPS, rows, HEAD), jnp.bfloat16),
        ],
        compiler_params=pltpu.CompilerParams(vmem_limit_bytes=32 * 1024 * 1024),
        cost_estimate=pl.CostEstimate(
            flops=4 * heads * queries * keys * HEAD,
            bytes_accessed=2 * cols * (2 * queries + 2 * keys),
            transcendentals=heads * queries * keys,
        ),
        name="attend",
    )(bias, place, q, *[kvs[o] for o in offsets], *(carry or ()))


def tile_bias(tile_order, tile_mask, position, frames):
    pad = REACH * TPS
    padded = jnp.pad(tile_order, (pad, pad))
    near = lax.dynamic_slice_in_dim(padded, position * TPS, SPAN * TPS).reshape(SPAN, TPS)
    near_frames = position + jnp.arange(-REACH, REACH + 1, dtype=jnp.int32)[:, None]
    inside = (near_frames >= 0) & (near_frames < frames)
    spatial = near - near_frames * TPS
    spatial = jnp.where(near_frames >= frames // 2, traded(spatial), spatial)
    own = lax.dynamic_slice_in_dim(tile_order, position * TPS, TPS) - position * TPS
    own = jnp.where(position >= frames // 2, traded(own), own)
    rows = lax.dynamic_slice_in_dim(tile_mask, position * TPS, TPS, 0).reshape(TPS, SPAN, TPS)
    ids = jnp.arange(TPS, dtype=jnp.int32)
    pick_q = own[:, None] == ids
    pick_k = (spatial[:, :, None] == ids) & inside[:, :, None]
    hit = (
        pick_q[:, None, None, :, None]
        & pick_k[None, :, :, None, :]
        & (rows != 0).transpose(1, 0, 2)[None, :, None, :, :]
    )
    allowed = jnp.any(hit, axis=(3, 4))
    return jnp.where(allowed, 0.0, NEG).astype(jnp.float32).reshape(-1)


def partner(u, frame, frames):
    return u ^ 2 if frame >= frames // 2 and u % 2 else u


def traded(slots):
    return jnp.stack([slots[..., i ^ 2 if i % 2 else i] for i in range(TPS)], axis=-1)


def shifted(block, distance, frames, groups):
    route = []
    for i in range(frames):
        j = i + distance
        if 0 <= j < frames:
            for u in range(groups):
                to = partner(partner(u, i, frames), j, frames)
                route.append((i * groups + u, j * groups + to))
    return lax.ppermute(block, AXES, route)


def exchanged(x, frames, groups):
    places = [
        [f * groups + partner(p, f, frames) for p in range(groups)] for f in range(frames)
    ]
    return lax.all_to_all(
        x, AXES, split_axis=0, concat_axis=0, axis_index_groups=places, tiled=True
    )


def swapped(x, step, frames, groups):
    route = []
    for f in range(frames):
        for u in range(groups):
            to = partner(partner(u, f, frames) ^ step, f, frames)
            route.append((f * groups + u, f * groups + to))
    return lax.ppermute(x, AXES, route)


def after(x, *others):
    return lax.optimization_barrier((x, *others))[0]


def per_device(queries, keys, values, tile_order, tile_mask):
    groups = lax.axis_size("uly")
    frames = lax.axis_size("blk")
    position = lax.axis_index("blk")
    move = functools.partial(shifted, frames=frames, groups=groups)
    swap = functools.partial(exchanged, frames=frames, groups=groups)
    u = lax.axis_index("uly")
    place = jnp.where((position >= frames // 2) & (u % 2 == 1), u ^ 2, u).astype(jnp.int32).reshape(1)
    kv0 = pack_kv(keys, values, groups, CHUNKS[0], 0)
    kv1 = pack_kv(keys, values, groups, CHUNKS[1], CHUNKS[0])
    q = pack_q(queries, groups)
    bias = tile_bias(tile_order, tile_mask, position, frames)

    own0 = swap(kv0)
    up0, down0 = move(own0, 1), move(own0, -1)
    own1 = swap(after(kv1, own0))
    own_q = swap(after(q, own1))
    up1, down1 = move(own1, 1), move(own1, -1)
    up0b, down0b = move(up0, 1), move(down0, -1)
    up1b, down1b = move(up1, 1), move(down1, -1)
    part1 = attend(bias, place, own_q, {-1: up1, 0: own1, 1: down1}, CHUNKS[0], None, False)
    kvs0 = {-2: up0b, -1: up0, 0: own0, 1: down0, 2: down0b}
    out0 = attend(after(bias, part1[0]), place, own_q, kvs0, 0)
    res0 = swap(out0)
    out1 = attend(
        bias, place, own_q, {-2: up1b, 2: down1b}, CHUNKS[0], part1, spread=True
    )
    res1 = [out1[0]] + [
        swapped(out1[t], t, frames, groups) for t in (2, 3, 1)
    ]
    return unpack(place, res0, [res1[0], res1[3], res1[1], res1[2]])


def solution(mesh):
    return jax.shard_map(
        per_device,
        mesh=mesh,
        in_specs=(
            P(AXES, None),
            P(AXES, None),
            P(AXES, None),
            P(),
            P(),
        ),
        out_specs=P(AXES, None),
        check_vma=False,
    )
```

time: 126 us -> 122 us (0.968)
  blocking collectives: 12.2 us -> 0 us
  starting transfers between devices: 62 us -> 65.2 us
  waiting for transfers between devices: 25.1 us -> 22 us
  local copies, waits for them, and re-layouts: 0.8 us -> 3.69 us
  other arithmetic: 0.47 us -> 3.2 us
  Pallas kernels: 24.3 us -> 26.8 us
    all_to_all x1 -> x0, blocking collectives: 12.2 us -> none  [exchanged(): return lax.all_to_all(x, 'uly', split_axis=0, concat_axis=0, tiled=True)]
    all_to_all x4, waiting for transfers between devices: 18.8 us -> 10.9 us  [exchanged(): lax.all_to_all(x, AXES, split_axis=0, concat_axis=0, axis_index_groups=pl...]
    ppermute x0 -> x3, waiting for transfers between devices: none -> 5.86 us  [swapped(): return lax.ppermute(x, AXES, route)]
    ppermute x0 -> x3, starting transfers between devices: none -> 3.79 us  [swapped(): return lax.ppermute(x, AXES, route)]
    pallas_call x2 -> x3, Pallas kernels: 15.5 us -> 18.2 us  [attend(): pl.pallas_call(functools.partial(attend_kernel, math.log2(math.e) / math....]
    select_n x0 -> x2, other arithmetic: none -> 2.72 us  [the longest x1 2.64 us: tile_bias(): own = jnp.where(position >= frames // 2, traded(own), own)]
    unnamed x7 -> x19, local copies, waits for them, and re-layouts: 0.12 us -> 2.26 us
  transfers between devices with their start and end apart: 12 -> 15, of which waited for: 7 -> 7; matrix products, arithmetic and copies ran while one was open for 1% -> 4% of each run, Pallas kernels for 16% -> 19%
where the time goes in v3:
time: 122 us; the launch traced here: 121 us
  starting transfers between devices  65.2 us (53%)
  Pallas kernels  26.8 us (22%)
  waiting for transfers between devices  22 us (18%)
  local copies, waits for them, and re-layouts  3.69 us (3%)
  other arithmetic  3.2 us (3%)
    ppermute x8, starting transfers between devices, shifted(): return lax.ppermute(block, AXES, route)  46 us
    pallas_call x3, Pallas kernels, attend(): pl.pallas_call(functools.partial(attend_kernel, math.log2(math.e) / math....  18.2 us
    all_to_all x4, starting transfers between devices, exchanged(): lax.all_to_all(x, AXES, split_axis=0, concat_axis=0, axis_index_groups=pl...  15.3 us
    all_to_all x4, waiting for transfers between devices, exchanged(): lax.all_to_all(x, AXES, split_axis=0, concat_axis=0, axis_index_groups=pl...  10.9 us
    ppermute x3, waiting for transfers between devices, swapped(): return lax.ppermute(x, AXES, route)  5.86 us
    ppermute x8, waiting for transfers between devices, shifted(): return lax.ppermute(block, AXES, route)  5.22 us
    pallas_call x2, Pallas kernels, pack_kv(): pl.pallas_call(functools.partial(pack_kv_kernel, groups, skip), in_specs=...  4.35 us
    ppermute x3, starting transfers between devices, swapped(): return lax.ppermute(x, AXES, route)  3.79 us
  transfers between devices with their start and end apart: 15, of which 7 were waited for; matrix products, arithmetic and copies ran while one was open for 4% of the time, Pallas kernels for 19%

profile of v3, /device:TPU:8, one launch (start us, length us, event | category | flops | bytes accessed | tf_op | source)
XLA Modules:
  0.0 121.2 jit_solution(4206222457754969028)
XLA Ops:
  0.0 2.2 %pack_kv.3 = bf16[4,2,128,384]{3,2,1,0:T(8,128)(2,1)} custom-call(bf16[128,3072]{1,0:T(8,128)(2,1)} %k_ref.3, bf16[128,3072]{1,0:T(8,128)(2,1)} %v_ref.3), custom_call_target="tpu_custom_call" | custom-call | tf_op jit(solution)/shard_map/pack_kv/pallas_call | solution.py:39
  2.2 3.6 %all-to-all-start = ((bf16[4,2,128,384]{3,2,1,0:T(8,128)(2,1)}), bf16[4,2,128,384]{3,2,1,0:T(8,128)(2,1)S(1)}, u32[]{:S(2)}, u32[]{:S(2)}) async-start(bf16[4,2,128,384]{3,2,1,0:T(8,128)(2,1)} %pack_kv.3), calls=%async_computation | async-start | bytes 1572864 | tf_op jit(solution)/shard_map/all_to_all | solution.py:244
  5.7 2.2 %pack_kv.2 = bf16[4,2,128,384]{3,2,1,0:T(8,128)(2,1)} custom-call(bf16[128,3072]{1,0:T(8,128)(2,1)} %k_ref.3, bf16[128,3072]{1,0:T(8,128)(2,1)} %v_ref.3), custom_call_target="tpu_custom_call" | custom-call | tf_op jit(solution)/shard_map/pack_kv/pallas_call | solution.py:39
  8.0 10.9 %all-to-all-done.refs_2_ = bf16[4,2,128,384]{3,2,1,0:T(8,128)(2,1)S(1)} async-done(((bf16[4,2,128,384]{3,2,1,0:T(8,128)(2,1)}), bf16[4,2,128,384]{3,2,1,0:T(8,128)(2,1)S(1)}, u32[]{:S(2)}, u32[]{:S(2)}) %all-to-all-start) | async-done | bytes 786464 | tf_op jit(solution)/shard_map/all_to_all | solution.py:244
  18.9 3.5 %all-to-all-start.1 = ((bf16[4,2,128,384]{3,2,1,0:T(8,128)(2,1)}), bf16[4,2,128,384]{3,2,1,0:T(8,128)(2,1)S(1)}, u32[]{:S(2)}, u32[]{:S(2)}) async-start(bf16[4,2,128,384]{3,2,1,0:T(8,128)(2,1)} %pack_kv.2), calls=%async_computation.1 | async-start | bytes 1572864 | tf_op jit(solution)/shard_map/all_to_all | solution.py:244
  22.7 3.8 %collective-permute-start.2 = (bf16[4,2,128,384]{3,2,1,0:T(8,128)(2,1)S(1)}, bf16[4,2,128,384]{3,2,1,0:T(8,128)(2,1)}, u32[]{:S(2)}, u32[]{:S(2)}) collective-permute-start(bf16[4,2,128,384]{3,2,1,0:T(8,128)(2,1)S(1)} %all-to-all-done.refs_2_), channel_id=1, source_target_pairs={{0,4},{1,5},{2,6},{3,7},{4,8},{5,9},{6,10},{7,11},{8,12},{9,13},{1... | collective-permute-start | bytes 2359304 | tf_op jit(solution)/shard_map/ppermute | solution.py:237
  26.5 8.9 %collective-permute-start.4 = (bf16[4,2,128,384]{3,2,1,0:T(8,128)(2,1)S(1)}, bf16[4,2,128,384]{3,2,1,0:T(8,128)(2,1)}, u32[]{:S(2)}, u32[]{:S(2)}) collective-permute-start(bf16[4,2,128,384]{3,2,1,0:T(8,128)(2,1)S(1)} %all-to-all-done.refs_2_), channel_id=1, source_target_pairs={{4,0},{5,1},{6,2},{7,3},{8,4},{9,5},{10,6},{11,7},{12,8},{13,9},{1... | collective-permute-start | bytes 2359304 | tf_op jit(solution)/shard_map/ppermute | solution.py:237
  35.5 3.8 %collective-permute-start = (bf16[4,2,128,384]{3,2,1,0:T(8,128)(2,1)S(1)}, bf16[4,2,128,384]{3,2,1,0:T(8,128)(2,1)}, u32[]{:S(2)}, u32[]{:S(2)}) collective-permute-start(bf16[4,2,128,384]{3,2,1,0:T(8,128)(2,1)S(1)} %all-to-all-done.1.refs_1_), channel_id=1, source_target_pairs={{0,4},{1,5},{2,6},{3,7},{4,8},{5,9},{6,10},{7,11},{8,12},{9,13},{1... | collective-permute-start | bytes 2359304 | tf_op jit(solution)/shard_map/ppermute | solution.py:237
  39.3 9.4 %collective-permute-start.1 = (bf16[4,2,128,384]{3,2,1,0:T(8,128)(2,1)S(1)}, bf16[4,2,128,384]{3,2,1,0:T(8,128)(2,1)}, u32[]{:S(2)}, u32[]{:S(2)}) collective-permute-start(bf16[4,2,128,384]{3,2,1,0:T(8,128)(2,1)S(1)} %all-to-all-done.1.refs_1_), channel_id=1, source_target_pairs={{4,0},{5,1},{6,2},{7,3},{8,4},{9,5},{10,6},{11,7},{12,8},{13,9},{1... | collective-permute-start | bytes 2359304 | tf_op jit(solution)/shard_map/ppermute | solution.py:237
  48.9 2.1 %pack_q.1 = bf16[4,128,768]{2,1,0:T(8,128)(2,1)} custom-call(bf16[128,3072]{1,0:T(8,128)(2,1)} %q_ref.1), custom_call_target="tpu_custom_call" | custom-call | tf_op jit(solution)/shard_map/pack_q/pallas_call | solution.py:57
  51.1 0.7 fusion.2
  51.8 2.6 %broadcast_select_fusion.1 = s32[4]{0:T(128)S(1)} fusion(pred[]{:T(512)S(6)} %ge.21, s32[1]{0:T(128)} %get-tuple-element.28, s32[1]{0:T(128)} %get-tuple-element.29, s32[1]{0:T(128)} %get-tuple-element.30, s32[1]{0:T(128)} %get-tuple-element.27, s32[]{:T(128)S(6)} %mul.14, s32[256]{0:T(256)S(1)} %copy-done.8, s32[]{:T(128)S(6)} %select_n.44), kind=kLoop, calls=%fused_computation.10 | loop fusion | flops 20 | bytes 57 | tf_op jit(solution)/shard_map/jit(_where)/select_n | solution.py:207
  54.5 3.5 %all-to-all-start.2 = ((bf16[4,128,768]{2,1,0:T(8,128)(2,1)}), bf16[4,128,768]{2,1,0:T(8,128)(2,1)S(1)}, u32[]{:S(2)}, u32[]{:S(2)}) async-start(bf16[4,128,768]{2,1,0:T(8,128)(2,1)} %pack_q.1), calls=%async_computation.2 | async-start | bytes 1572864 | tf_op jit(solution)/shard_map/all_to_all | solution.py:244
  58.0 1.9 %collective-permute-start.3 = (bf16[4,2,128,384]{3,2,1,0:T(8,128)(2,1)}, bf16[4,2,128,384]{3,2,1,0:T(8,128)(2,1)}, u32[]{:S(2)}, u32[]{:S(2)}) collective-permute-start(bf16[4,2,128,384]{3,2,1,0:T(8,128)(2,1)} %collective-permute-done.2.refs_1_), channel_id=1, source_target_pairs={{0,4},{1,5},{2,6},{3,7},{4,8},{5,9},{6,10},{7,11},{8,12},{9,13},{1... | collective-permute-start | bytes 2359304 | tf_op jit(solution)/shard_map/ppermute | solution.py:237
  59.9 8.1 %collective-permute-start.5 = (bf16[4,2,128,384]{3,2,1,0:T(8,128)(2,1)}, bf16[4,2,128,384]{3,2,1,0:T(8,128)(2,1)}, u32[]{:S(2)}, u32[]{:S(2)}) collective-permute-start(bf16[4,2,128,384]{3,2,1,0:T(8,128)(2,1)} %collective-permute-done.4.refs_3_), channel_id=1, source_target_pairs={{4,0},{5,1},{6,2},{7,3},{8,4},{9,5},{10,6},{11,7},{12,8},{13,9},{1... | collective-permute-start | bytes 2359304 | tf_op jit(solution)/shard_map/ppermute | solution.py:237
  68.7 1.9 %collective-permute-start.6 = (bf16[4,2,128,384]{3,2,1,0:T(8,128)(2,1)}, bf16[4,2,128,384]{3,2,1,0:T(8,128)(2,1)S(1)}, u32[]{:S(2)}, u32[]{:S(2)}) collective-permute-start(bf16[4,2,128,384]{3,2,1,0:T(8,128)(2,1)} %collective-permute-done.refs_0_), channel_id=1, source_target_pairs={{0,4},{1,5},{2,6},{3,7},{4,8},{5,9},{6,10},{7,11},{8,12},{9,13},{1... | collective-permute-start | bytes 2359304 | tf_op jit(solution)/shard_map/ppermute | solution.py:237
  70.6 8.1 %collective-permute-start.7 = (bf16[4,2,128,384]{3,2,1,0:T(8,128)(2,1)}, bf16[4,2,128,384]{3,2,1,0:T(8,128)(2,1)}, u32[]{:S(2)}, u32[]{:S(2)}) collective-permute-start(bf16[4,2,128,384]{3,2,1,0:T(8,128)(2,1)} %collective-permute-done.1.refs_2_), channel_id=1, source_target_pairs={{4,0},{5,1},{6,2},{7,3},{8,4},{9,5},{10,6},{11,7},{12,8},{13,9},{1... | collective-permute-start | bytes 2359304 | tf_op jit(solution)/shard_map/ppermute | solution.py:237
  79.6 5.5 %attend.3 = (f32[3,128,512]{2,1,0:T(8,128)S(1)}, f32[3,2,512]{2,1,0:T(2,128)S(1)}) custom-call(f32[80]{0:T(128)S(1)} %select_n.49.bias_ref, s32[1]{0:T(128)} %bitcast.place_ref, bf16[4,128,768]{2,1,0:T(8,128)(2,1)S(1)} %all-to-all-done.2.q_ref, bf16[4,2,128,384]{3,2,1,0:T(8,128)(2,1)} %collective-permute-done.refs_0_, ...), custom_call_target="tpu_custom_call" | custom-call | flops 1207959552 | bytes 3145728 | tf_op jit(solution)/shard_map/attend/pallas_call | solution.py:165
  85.1 0.9 copy-done
  86.0 0.6 collective-permute-done.5.refs_4_
  86.6 8.1 %attend.4 = bf16[4,128,384]{2,1,0:T(8,128)(2,1)} custom-call(f32[80]{0:T(128)S(1)} %select_n.49.bias_ref, s32[1]{0:T(128)} %bitcast.place_ref, bf16[4,128,768]{2,1,0:T(8,128)(2,1)S(1)} %all-to-all-done.2.q_ref, bf16[4,2,128,384]{3,2,1,0:T(8,128)(2,1)} %collective-permute-done.3.refs_0_, bf16[4,2,128,384]{3,2,1,0:T(8,128)(2,1)} %collective-permute-done.2.refs_1_, ...), custom_call_target="tpu_custom_call" | custom-call | flops 2013265920 | bytes 4718592 | tf_op jit(solution)/shard_map/attend/pallas_call | solution.py:165
  94.7 4.7 %all-to-all-start.3 = ((bf16[4,128,384]{2,1,0:T(8,128)(2,1)}), bf16[4,128,384]{2,1,0:T(8,128)(2,1)S(1)}, u32[]{:S(2)}, u32[]{:S(2)}) async-start(bf16[4,128,384]{2,1,0:T(8,128)(2,1)} %attend.4), calls=%async_computation.3 | async-start | bytes 786432 | tf_op jit(solution)/shard_map/all_to_all | solution.py:244
  99.4 1.6 %collective-permute-done.6.refs_0_ = bf16[4,2,128,384]{3,2,1,0:T(8,128)(2,1)S(1)} collective-permute-done((bf16[4,2,128,384]{3,2,1,0:T(8,128)(2,1)}, bf16[4,2,128,384]{3,2,1,0:T(8,128)(2,1)S(1)}, u32[]{:S(2)}, u32[]{:S(2)}) %collective-permute-start.6) | collective-permute-done | bytes 786464 | tf_op jit(solution)/shard_map/ppermute | solution.py:237
  101.0 2.5 %collective-permute-done.7.refs_1_ = bf16[4,2,128,384]{3,2,1,0:T(8,128)(2,1)} collective-permute-done((bf16[4,2,128,384]{3,2,1,0:T(8,128)(2,1)}, bf16[4,2,128,384]{3,2,1,0:T(8,128)(2,1)}, u32[]{:S(2)}, u32[]{:S(2)}) %collective-permute-start.7) | collective-permute-done | bytes 786464 | tf_op jit(solution)/shard_map/ppermute | solution.py:237
  103.5 4.7 %attend.5 = (bf16[128,384]{1,0:T(8,128)(2,1)S(1)}, bf16[128,384]{1,0:T(8,128)(2,1)S(1)}, bf16[128,384]{1,0:T(8,128)(2,1)S(1)}, bf16[128,384]{1,0:T(8,128)(2,1)S(1)}) custom-call(f32[80]{0:T(128)S(1)} %select_n.49.bias_ref, s32[1]{0:T(128)} %bitcast.place_ref, bf16[4,128,768]{2,1,0:T(8,128)(2,1)S(1)} %all-to-all-done.2.q_ref, ...), custom_call_target="tpu_custom_call" | custom-call | flops 805306368 | bytes 2359296 | tf_op jit(solution)/shard_map/attend/pallas_call | solution.py:165
  108.1 0.6 copy-done.2
  108.8 0.7 collective-permute-start.10
  109.4 2.6 %collective-permute-start.8 = (bf16[128,384]{1,0:T(8,128)(2,1)S(1)}, bf16[128,384]{1,0:T(8,128)(2,1)S(1)}, u32[]{:S(2)}, u32[]{:S(2)}) collective-permute-start(bf16[128,384]{1,0:T(8,128)(2,1)S(1)} %get-tuple-element.20), channel_id=1, source_target_pairs={{0,1},{1,0},{2,3},{3,2},{4,5},{5,4},{6,7},{7,6},{8,9},{9,8},{10,11... | collective-permute-start | bytes 294920 | tf_op jit(solution)/shard_map/ppermute | solution.py:255
  112.6 3.3 %collective-permute-done.8.refs_1_ = bf16[128,384]{1,0:T(8,128)(2,1)S(1)} collective-permute-done((bf16[128,384]{1,0:T(8,128)(2,1)S(1)}, bf16[128,384]{1,0:T(8,128)(2,1)S(1)}, u32[]{:S(2)}, u32[]{:S(2)}) %collective-permute-start.8) | collective-permute-done | bytes 98336 | tf_op jit(solution)/shard_map/ppermute | solution.py:255
  115.8 2.6 %collective-permute-done.9.refs_2_ = bf16[128,384]{1,0:T(8,128)(2,1)S(1)} collective-permute-done((bf16[128,384]{1,0:T(8,128)(2,1)S(1)}, bf16[128,384]{1,0:T(8,128)(2,1)S(1)}, u32[]{:S(2)}, u32[]{:S(2)}) %collective-permute-start.9) | collective-permute-done | bytes 98336 | tf_op jit(solution)/shard_map/ppermute | solution.py:255
  118.5 0.6 copy-done.6
  119.1 2.1 %unpack.1 = bf16[128,3072]{1,0:T(8,128)(2,1)} custom-call(s32[1]{0:T(128)} %bitcast.place_ref, bf16[4,128,384]{2,1,0:T(8,128)(2,1)} %copy-done.3, bf16[128,384]{1,0:T(8,128)(2,1)} %copy-done.2, bf16[128,384]{1,0:T(8,128)(2,1)} %copy-done.5, bf16[128,384]{1,0:T(8,128)(2,1)} %copy-done.6, bf16[128,384]{1,0:T(8,128)(2,1)} %copy-done.4), custom_call_target="tpu_custom_call" | custom-call | tf_op jit(solution)/shard_map/unpack/pallas_call | solution.py:80
  (44 shorter events, 2.6 us)
Async XLA Ops:
  2.2 16.7 %all-to-all-start = ((bf16[4,2,128,384]{3,2,1,0:T(8,128)(2,1)}), bf16[4,2,128,384]{3,2,1,0:T(8,128)(2,1)S(1)}, u32[]{:S(2)}, u32[]{:S(2)}) async-start(bf16[4,2,128,384]{3,2,1,0:T(8,128)(2,1)} %pack_kv.3), calls=%async_computation | async-start | bytes 1572864 | tf_op jit(solution)/shard_map/all_to_all | solution.py:244
  8.0 14.4 %copy-start.8 = (s32[256]{0:T(256)S(1)}, s32[256]{0:T(256)}, u32[]{:S(2)}) copy-start(s32[256]{0:T(256)} %param.8) | copy-start | bytes 3076
  18.9 16.6 %all-to-all-start.1 = ((bf16[4,2,128,384]{3,2,1,0:T(8,128)(2,1)}), bf16[4,2,128,384]{3,2,1,0:T(8,128)(2,1)S(1)}, u32[]{:S(2)}, u32[]{:S(2)}) async-start(bf16[4,2,128,384]{3,2,1,0:T(8,128)(2,1)} %pack_kv.2), calls=%async_computation.1 | async-start | bytes 1572864 | tf_op jit(solution)/shard_map/all_to_all | solution.py:244
  22.7 35.3 %collective-permute-start.2 = (bf16[4,2,128,384]{3,2,1,0:T(8,128)(2,1)S(1)}, bf16[4,2,128,384]{3,2,1,0:T(8,128)(2,1)}, u32[]{:S(2)}, u32[]{:S(2)}) collective-permute-start(bf16[4,2,128,384]{3,2,1,0:T(8,128)(2,1)S(1)} %all-to-all-done.refs_2_), channel_id=1, source_target_pairs={{0,4},{1,5},{2,6},{3,7},{4,8},{5,9},{6,10},{7,11},{8,12},{9,13},{1... | collective-permute-start | bytes 2359304 | tf_op jit(solution)/shard_map/ppermute | solution.py:237
  26.5 33.4 %collective-permute-start.4 = (bf16[4,2,128,384]{3,2,1,0:T(8,128)(2,1)S(1)}, bf16[4,2,128,384]{3,2,1,0:T(8,128)(2,1)}, u32[]{:S(2)}, u32[]{:S(2)}) collective-permute-start(bf16[4,2,128,384]{3,2,1,0:T(8,128)(2,1)S(1)} %all-to-all-done.refs_2_), channel_id=1, source_target_pairs={{4,0},{5,1},{6,2},{7,3},{8,4},{9,5},{10,6},{11,7},{12,8},{13,9},{1... | collective-permute-start | bytes 2359304 | tf_op jit(solution)/shard_map/ppermute | solution.py:237
  35.5 33.2 %collective-permute-start = (bf16[4,2,128,384]{3,2,1,0:T(8,128)(2,1)S(1)}, bf16[4,2,128,384]{3,2,1,0:T(8,128)(2,1)}, u32[]{:S(2)}, u32[]{:S(2)}) collective-permute-start(bf16[4,2,128,384]{3,2,1,0:T(8,128)(2,1)S(1)} %all-to-all-done.1.refs_1_), channel_id=1, source_target_pairs={{0,4},{1,5},{2,6},{3,7},{4,8},{5,9},{6,10},{7,11},{8,12},{9,13},{1... | collective-permute-start | bytes 2359304 | tf_op jit(solution)/shard_map/ppermute | solution.py:237
  39.3 31.3 %collective-permute-start.1 = (bf16[4,2,128,384]{3,2,1,0:T(8,128)(2,1)S(1)}, bf16[4,2,128,384]{3,2,1,0:T(8,128)(2,1)}, u32[]{:S(2)}, u32[]{:S(2)}) collective-permute-start(bf16[4,2,128,384]{3,2,1,0:T(8,128)(2,1)S(1)} %all-to-all-done.1.refs_1_), channel_id=1, source_target_pairs={{4,0},{5,1},{6,2},{7,3},{8,4},{9,5},{10,6},{11,7},{12,8},{13,9},{1... | collective-permute-start | bytes 2359304 | tf_op jit(solution)/shard_map/ppermute | solution.py:237
  54.4 24.3 %copy-start.7 = (s32[256,20]{0,1:T(8,128)S(1)}, s32[256,20]{0,1:T(8,128)}, u32[]{:S(2)}) copy-start(s32[256,20]{0,1:T(8,128)} %param.9) | copy-start | bytes 61444
  54.5 25.1 %all-to-all-start.2 = ((bf16[4,128,768]{2,1,0:T(8,128)(2,1)}), bf16[4,128,768]{2,1,0:T(8,128)(2,1)S(1)}, u32[]{:S(2)}, u32[]{:S(2)}) async-start(bf16[4,128,768]{2,1,0:T(8,128)(2,1)} %pack_q.1), calls=%async_computation.2 | async-start | bytes 1572864 | tf_op jit(solution)/shard_map/all_to_all | solution.py:244
  58.0 28.0 %collective-permute-start.3 = (bf16[4,2,128,384]{3,2,1,0:T(8,128)(2,1)}, bf16[4,2,128,384]{3,2,1,0:T(8,128)(2,1)}, u32[]{:S(2)}, u32[]{:S(2)}) collective-permute-start(bf16[4,2,128,384]{3,2,1,0:T(8,128)(2,1)} %collective-permute-done.2.refs_1_), channel_id=1, source_target_pairs={{0,4},{1,5},{2,6},{3,7},{4,8},{5,9},{6,10},{7,11},{8,12},{9,13},{1... | collective-permute-start | bytes 2359304 | tf_op jit(solution)/shard_map/ppermute | solution.py:237
  59.9 26.7 %collective-permute-start.5 = (bf16[4,2,128,384]{3,2,1,0:T(8,128)(2,1)}, bf16[4,2,128,384]{3,2,1,0:T(8,128)(2,1)}, u32[]{:S(2)}, u32[]{:S(2)}) collective-permute-start(bf16[4,2,128,384]{3,2,1,0:T(8,128)(2,1)} %collective-permute-done.4.refs_3_), channel_id=1, source_target_pairs={{4,0},{5,1},{6,2},{7,3},{8,4},{9,5},{10,6},{11,7},{12,8},{13,9},{1... | collective-permute-start | bytes 2359304 | tf_op jit(solution)/shard_map/ppermute | solution.py:237
  68.7 32.3 %collective-permute-start.6 = (bf16[4,2,128,384]{3,2,1,0:T(8,128)(2,1)}, bf16[4,2,128,384]{3,2,1,0:T(8,128)(2,1)S(1)}, u32[]{:S(2)}, u32[]{:S(2)}) collective-permute-start(bf16[4,2,128,384]{3,2,1,0:T(8,128)(2,1)} %collective-permute-done.refs_0_), channel_id=1, source_target_pairs={{0,4},{1,5},{2,6},{3,7},{4,8},{5,9},{6,10},{7,11},{8,12},{9,13},{1... | collective-permute-start | bytes 2359304 | tf_op jit(solution)/shard_map/ppermute | solution.py:237
  70.6 32.8 %collective-permute-start.7 = (bf16[4,2,128,384]{3,2,1,0:T(8,128)(2,1)}, bf16[4,2,128,384]{3,2,1,0:T(8,128)(2,1)}, u32[]{:S(2)}, u32[]{:S(2)}) collective-permute-start(bf16[4,2,128,384]{3,2,1,0:T(8,128)(2,1)} %collective-permute-done.1.refs_2_), channel_id=1, source_target_pairs={{4,0},{5,1},{6,2},{7,3},{8,4},{9,5},{10,6},{11,7},{12,8},{13,9},{1... | collective-permute-start | bytes 2359304 | tf_op jit(solution)/shard_map/ppermute | solution.py:237
  85.1 0.9 copy-start
  94.7 8.8 %copy-start.1 = (f32[3,128,512]{2,1,0:T(8,128)S(1)}, f32[3,128,512]{2,1,0:T(8,128)}, u32[]{:S(2)}) copy-start(f32[3,128,512]{2,1,0:T(8,128)} %copy-done) | copy-start | bytes 2359300
  94.7 17.9 %all-to-all-start.3 = ((bf16[4,128,384]{2,1,0:T(8,128)(2,1)}), bf16[4,128,384]{2,1,0:T(8,128)(2,1)S(1)}, u32[]{:S(2)}, u32[]{:S(2)}) async-start(bf16[4,128,384]{2,1,0:T(8,128)(2,1)} %attend.4), calls=%async_computation.3 | async-start | bytes 786432 | tf_op jit(solution)/shard_map/all_to_all | solution.py:244
  108.1 0.6 copy-start.2
  108.8 3.8 %collective-permute-start.10 = (bf16[128,384]{1,0:T(8,128)(2,1)S(1)}, bf16[128,384]{1,0:T(8,128)(2,1)S(1)}, u32[]{:S(2)}, u32[]{:S(2)}) collective-permute-start(bf16[128,384]{1,0:T(8,128)(2,1)S(1)} %get-tuple-element.22), channel_id=1, source_target_pairs={{0,3},{1,2},{2,1},{3,0},{4,7},{5,6},{6,5},{7,4},{8,11},{9,10},{10,... | collective-permute-start | bytes 294920 | tf_op jit(solution)/shard_map/ppermute | solution.py:255
  109.4 6.4 %collective-permute-start.8 = (bf16[128,384]{1,0:T(8,128)(2,1)S(1)}, bf16[128,384]{1,0:T(8,128)(2,1)S(1)}, u32[]{:S(2)}, u32[]{:S(2)}) collective-permute-start(bf16[128,384]{1,0:T(8,128)(2,1)S(1)} %get-tuple-element.20), channel_id=1, source_target_pairs={{0,1},{1,0},{2,3},{3,2},{4,5},{5,4},{6,7},{7,6},{8,9},{9,8},{10,11... | collective-permute-start | bytes 294920 | tf_op jit(solution)/shard_map/ppermute | solution.py:255
  112.0 6.4 %collective-permute-start.9 = (bf16[128,384]{1,0:T(8,128)(2,1)S(1)}, bf16[128,384]{1,0:T(8,128)(2,1)S(1)}, u32[]{:S(2)}, u32[]{:S(2)}) collective-permute-start(bf16[128,384]{1,0:T(8,128)(2,1)S(1)} %get-tuple-element.21), channel_id=1, source_target_pairs={{0,2},{1,3},{2,0},{3,1},{4,6},{5,7},{6,4},{7,5},{8,10},{9,11},{10,... | collective-permute-start | bytes 294920 | tf_op jit(solution)/shard_map/ppermute | solution.py:255
  112.6 5.9 %copy-start.3 = (bf16[4,128,384]{2,1,0:T(8,128)(2,1)}, bf16[4,128,384]{2,1,0:T(8,128)(2,1)S(1)}, u32[]{:S(2)}) copy-start(bf16[4,128,384]{2,1,0:T(8,128)(2,1)S(1)} %all-to-all-done.3.first_ref) | copy-start | bytes 1179652
  112.6 5.9 %copy-start.4 = (bf16[128,384]{1,0:T(8,128)(2,1)}, bf16[128,384]{1,0:T(8,128)(2,1)S(1)}, u32[]{:S(2)}) copy-start(bf16[128,384]{1,0:T(8,128)(2,1)S(1)} %collective-permute-done.10.refs_3_) | copy-start | bytes 294916
  115.8 2.6 %copy-start.5 = (bf16[128,384]{1,0:T(8,128)(2,1)}, bf16[128,384]{1,0:T(8,128)(2,1)S(1)}, u32[]{:S(2)}) copy-start(bf16[128,384]{1,0:T(8,128)(2,1)S(1)} %collective-permute-done.8.refs_1_) | copy-start | bytes 294916
  118.4 0.6 copy-start.6

commit v4 on v3

--- a/solution.py
+++ b/solution.py
@@ -14,6 +14,8 @@
 SPAN = 2 * REACH + 1
 CHUNKS = (3, 3)
 NEG = -1e30
+SMALL = 4 * 1024 * 1024
+LARGE = 60 * 1024 * 1024
 AXES = ("blk", "uly")
 
 
@@ -25,53 +27,82 @@
         copy.wait()
 
 
-def pack_kv_kernel(groups, skip, k_ref, v_ref, out_ref, sems):
+def relay(triples, sems):
+    ins = [pltpu.make_async_copy(src, via, sems.at[i, 0]) for i, (src, via, _) in enumerate(triples)]
+    outs = [pltpu.make_async_copy(via, dst, sems.at[i, 1]) for i, (_, via, dst) in enumerate(triples)]
+    for copy in ins:
+        copy.start()
+    for first, second in zip(ins, outs):
+        first.wait()
+        second.start()
+    for copy in outs:
+        copy.wait()
+
+
+def pack_kv_kernel(groups, skip, k_ref, v_ref, out_ref, via_ref, sems):
     width, cols = k_ref.shape[1] // groups, out_ref.shape[-1]
-    pairs = []
+    triples = []
     for u in range(groups):
         at = pl.ds(u * width + skip * HEAD, cols)
-        pairs += [(k_ref.at[:, at], out_ref.at[u, 0]), (v_ref.at[:, at], out_ref.at[u, 1])]
-    run_copies(pairs, sems)
+        triples += [
+            (ref.at[:, at], via_ref.at[u, i], out_ref.at[u, i])
+            for i, ref in enumerate((k_ref, v_ref))
+        ]
+    relay(triples, sems)
 
 
 def pack_kv(keys, values, groups, heads, skip):
-    rows = keys.shape[0]
+    shape = (groups, 2, keys.shape[0], heads * HEAD)
     return pl.pallas_call(
         functools.partial(pack_kv_kernel, groups, skip),
-        in_specs=[pl.BlockSpec(memory_space=pl.ANY)] * 2,
-        out_shape=jax.ShapeDtypeStruct((groups, 2, rows, heads * HEAD), jnp.bfloat16),
-        scratch_shapes=[pltpu.SemaphoreType.DMA((2 * groups,))],
+        in_specs=[pl.BlockSpec(memory_space=pltpu.HBM)] * 2,
+        out_specs=pl.BlockSpec(memory_space=pltpu.HBM),
+        out_shape=jax.ShapeDtypeStruct(shape, jnp.bfloat16),
+        scratch_shapes=[
+            pltpu.VMEM(shape, jnp.bfloat16),
+            pltpu.SemaphoreType.DMA((2 * groups, 2)),
+        ],
+        compiler_params=pltpu.CompilerParams(vmem_limit_bytes=LARGE),
         name="pack_kv",
     )(keys, values)
 
 
-def pack_q_kernel(groups, q_ref, out_ref, sems):
+def pack_q_kernel(groups, q_ref, out_ref, via_ref, sems):
     width = q_ref.shape[1] // groups
-    run_copies(
-        [(q_ref.at[:, pl.ds(u * width, width)], out_ref.at[u]) for u in range(groups)], sems
-    )
+    triples = [
+        (q_ref.at[:, pl.ds(u * width, width)], via_ref.at[u], out_ref.at[u])
+        for u in range(groups)
+    ]
+    relay(triples, sems)
 
 
 def pack_q(queries, groups):
-    rows, cols = queries.shape
+    shape = (groups, queries.shape[0], queries.shape[1] // groups)
     return pl.pallas_call(
         functools.partial(pack_q_kernel, groups),
-        in_specs=[pl.BlockSpec(memory_space=pl.ANY)],
-        out_shape=jax.ShapeDtypeStruct((groups, rows, cols // groups), jnp.bfloat16),
-        scratch_shapes=[pltpu.SemaphoreType.DMA((groups,))],
+        in_specs=[pl.BlockSpec(memory_space=pltpu.HBM)],
+        out_specs=pl.BlockSpec(memory_space=pltpu.HBM),
+        out_shape=jax.ShapeDtypeStruct(shape, jnp.bfloat16),
+        scratch_shapes=[
+            pltpu.VMEM(shape, jnp.bfloat16),
+            pltpu.SemaphoreType.DMA((groups, 2)),
+        ],
+        compiler_params=pltpu.CompilerParams(vmem_limit_bytes=LARGE),
         name="pack_q",
     )(queries)
 
 
 def unpack_kernel(groups, place_ref, first_ref, *refs):
-    rest, out_ref = refs[:groups], refs[groups]
+    rest, out_ref, sems = refs[:groups], refs[groups], refs[groups + 1]
     width, cols = out_ref.shape[1] // groups, first_ref.shape[-1]
     place = place_ref[0]
-    for u in range(groups):
-        out_ref[:, u * width : u * width + cols] = first_ref[u]
+    pairs = []
     for t in range(groups):
         start = pl.multiple_of((place ^ t) * width + cols, HEAD)
-        out_ref[:, pl.ds(start, width - cols)] = rest[t][...]
+        pairs.append((rest[t], out_ref.at[:, pl.ds(start, width - cols)]))
+    for u in range(groups):
+        pairs.append((first_ref.at[u], out_ref.at[:, pl.ds(u * width, cols)]))
+    run_copies(pairs, sems)
 
 
 def unpack(place, first, rest):
@@ -79,8 +110,11 @@
     width = groups * (cols + rest[0].shape[-1])
     return pl.pallas_call(
         functools.partial(unpack_kernel, groups),
-        in_specs=[pl.BlockSpec(memory_space=pltpu.SMEM)] + [pl.BlockSpec()] * (1 + groups),
+        in_specs=[pl.BlockSpec(memory_space=pltpu.SMEM)]
+        + [pl.BlockSpec(memory_space=pl.ANY)] * (1 + groups),
         out_shape=jax.ShapeDtypeStruct((rows, width), jnp.bfloat16),
+        scratch_shapes=[pltpu.SemaphoreType.DMA((2 * groups,))],
+        compiler_params=pltpu.CompilerParams(vmem_limit_bytes=SMALL),
         name="unpack",
     )(place, first, *rest)
 
@@ -280,12 +314,12 @@
     up0b, down0b = move(up0, 1), move(down0, -1)
     up1b, down1b = move(up1, 1), move(down1, -1)
     part1 = attend(bias, place, own_q, {-1: up1, 0: own1, 1: down1}, CHUNKS[0], None, False)
-    kvs0 = {-2: up0b, -1: up0, 0: own0, 1: down0, 2: down0b}
-    out0 = attend(after(bias, part1[0]), place, own_q, kvs0, 0)
+    bias0 = after(bias, part1[0])
+    part0 = attend(bias0, place, own_q, {-1: up0, 0: own0, 1: down0}, 0, None, False)
+    out0 = attend(after(bias0, part0[0]), place, own_q, {-2: up0b, 2: down0b}, 0, part0)
     res0 = swap(out0)
-    out1 = attend(
-        bias, place, own_q, {-2: up1b, 2: down1b}, CHUNKS[0], part1, spread=True
-    )
+    bias1 = after(bias, out0)
+    out1 = attend(bias1, place, own_q, {-2: up1b, 2: down1b}, CHUNKS[0], part1, spread=True)
     res1 = [out1[0]] + [
         swapped(out1[t], t, frames, groups) for t in (2, 3, 1)
     ]

time: 122 us -> 119 us (0.975)
  waiting for transfers between devices: 22 us -> 19.8 us
  local copies, waits for them, and re-layouts: 3.69 us -> 1.54 us
  Pallas kernels: 26.8 us -> 28.2 us
    pallas_call x3 -> x4, Pallas kernels: 18.2 us -> 21.1 us  [attend(): pl.pallas_call(functools.partial(attend_kernel, math.log2(math.e) / math....]
    unnamed x19 -> x9, local copies, waits for them, and re-layouts: 2.26 us -> 0.13 us
    ppermute x8, waiting for transfers between devices: 5.22 us -> 3.17 us  [shifted(): return lax.ppermute(block, AXES, route)]
  transfers between devices with their start and end apart: 15 -> 15, of which waited for: 7 -> 6; matrix products, arithmetic and copies ran while one was open for 4% -> 4% of each run, Pallas kernels for 19% -> 21%
where the time goes in v4:
time: 119 us; the launch traced here: 118 us
  starting transfers between devices  65.6 us (55%)
  Pallas kernels  28.2 us (24%)
  waiting for transfers between devices  19.8 us (17%)
  other arithmetic  3.07 us (3%)
  local copies, waits for them, and re-layouts  1.54 us (1%)
    ppermute x8, starting transfers between devices, shifted(): return lax.ppermute(block, AXES, route)  46 us
    pallas_call x4, Pallas kernels, attend(): pl.pallas_call(functools.partial(attend_kernel, math.log2(math.e) / math....  21.1 us
    all_to_all x4, starting transfers between devices, exchanged(): lax.all_to_all(x, AXES, split_axis=0, concat_axis=0, axis_index_groups=pl...  15.6 us
    all_to_all x4, waiting for transfers between devices, exchanged(): lax.all_to_all(x, AXES, split_axis=0, concat_axis=0, axis_index_groups=pl...  11.1 us
    ppermute x3, waiting for transfers between devices, swapped(): return lax.ppermute(x, AXES, route)  5.47 us
    pallas_call x2, Pallas kernels, pack_kv(): pl.pallas_call(functools.partial(pack_kv_kernel, groups, skip), in_specs=...  4 us
    ppermute x3, starting transfers between devices, swapped(): return lax.ppermute(x, AXES, route)  3.97 us
    ppermute x8, waiting for transfers between devices, shifted(): return lax.ppermute(block, AXES, route)  3.17 us
  transfers between devices with their start and end apart: 15, of which 6 were waited for; matrix products, arithmetic and copies ran while one was open for 4% of the time, Pallas kernels for 21%

profile of v4, /device:TPU:8, one launch (start us, length us, event | category | flops | bytes accessed | tf_op | source)
XLA Modules:
  0.0 118.5 jit_solution(15775306776901561704)
XLA Ops:
  0.0 2.0 %pack_kv.3 = bf16[4,2,128,384]{3,2,1,0:T(8,128)(2,1)} custom-call(bf16[128,3072]{1,0:T(8,128)(2,1)} %k_ref.3, bf16[128,3072]{1,0:T(8,128)(2,1)} %v_ref.3), custom_call_target="tpu_custom_call" | custom-call | tf_op jit(solution)/shard_map/pack_kv/pallas_call | solution.py:56
  2.0 3.6 %all-to-all-start = ((bf16[4,2,128,384]{3,2,1,0:T(8,128)(2,1)}), bf16[4,2,128,384]{3,2,1,0:T(8,128)(2,1)S(1)}, u32[]{:S(2)}, u32[]{:S(2)}) async-start(bf16[4,2,128,384]{3,2,1,0:T(8,128)(2,1)} %pack_kv.3), calls=%async_computation | async-start | bytes 1572864 | tf_op jit(solution)/shard_map/all_to_all | solution.py:278
  5.6 2.0 %pack_kv.2 = bf16[4,2,128,384]{3,2,1,0:T(8,128)(2,1)} custom-call(bf16[128,3072]{1,0:T(8,128)(2,1)} %k_ref.3, bf16[128,3072]{1,0:T(8,128)(2,1)} %v_ref.3), custom_call_target="tpu_custom_call" | custom-call | tf_op jit(solution)/shard_map/pack_kv/pallas_call | solution.py:56
  7.6 11.1 %all-to-all-done.refs_1_ = bf16[4,2,128,384]{3,2,1,0:T(8,128)(2,1)S(1)} async-done(((bf16[4,2,128,384]{3,2,1,0:T(8,128)(2,1)}), bf16[4,2,128,384]{3,2,1,0:T(8,128)(2,1)S(1)}, u32[]{:S(2)}, u32[]{:S(2)}) %all-to-all-start) | async-done | bytes 786464 | tf_op jit(solution)/shard_map/all_to_all | solution.py:278
  18.7 3.5 %all-to-all-start.1 = ((bf16[4,2,128,384]{3,2,1,0:T(8,128)(2,1)}), bf16[4,2,128,384]{3,2,1,0:T(8,128)(2,1)S(1)}, u32[]{:S(2)}, u32[]{:S(2)}) async-start(bf16[4,2,128,384]{3,2,1,0:T(8,128)(2,1)} %pack_kv.2), calls=%async_computation.1 | async-start | bytes 1572864 | tf_op jit(solution)/shard_map/all_to_all | solution.py:278
  22.5 3.8 %collective-permute-start.2 = (bf16[4,2,128,384]{3,2,1,0:T(8,128)(2,1)S(1)}, bf16[4,2,128,384]{3,2,1,0:T(8,128)(2,1)}, u32[]{:S(2)}, u32[]{:S(2)}) collective-permute-start(bf16[4,2,128,384]{3,2,1,0:T(8,128)(2,1)S(1)} %all-to-all-done.refs_1_), channel_id=1, source_target_pairs={{0,4},{1,5},{2,6},{3,7},{4,8},{5,9},{6,10},{7,11},{8,12},{9,13},{1... | collective-permute-start | bytes 2359304 | tf_op jit(solution)/shard_map/ppermute | solution.py:271
  26.4 8.9 %collective-permute-start.3 = (bf16[4,2,128,384]{3,2,1,0:T(8,128)(2,1)S(1)}, bf16[4,2,128,384]{3,2,1,0:T(8,128)(2,1)}, u32[]{:S(2)}, u32[]{:S(2)}) collective-permute-start(bf16[4,2,128,384]{3,2,1,0:T(8,128)(2,1)S(1)} %all-to-all-done.refs_1_), channel_id=1, source_target_pairs={{4,0},{5,1},{6,2},{7,3},{8,4},{9,5},{10,6},{11,7},{12,8},{13,9},{1... | collective-permute-start | bytes 2359304 | tf_op jit(solution)/shard_map/ppermute | solution.py:271
  35.3 3.8 %collective-permute-start = (bf16[4,2,128,384]{3,2,1,0:T(8,128)(2,1)S(1)}, bf16[4,2,128,384]{3,2,1,0:T(8,128)(2,1)}, u32[]{:S(2)}, u32[]{:S(2)}) collective-permute-start(bf16[4,2,128,384]{3,2,1,0:T(8,128)(2,1)S(1)} %all-to-all-done.1.refs_1_), channel_id=1, source_target_pairs={{0,4},{1,5},{2,6},{3,7},{4,8},{5,9},{6,10},{7,11},{8,12},{9,13},{1... | collective-permute-start | bytes 2359304 | tf_op jit(solution)/shard_map/ppermute | solution.py:271
  39.1 9.4 %collective-permute-start.1 = (bf16[4,2,128,384]{3,2,1,0:T(8,128)(2,1)S(1)}, bf16[4,2,128,384]{3,2,1,0:T(8,128)(2,1)}, u32[]{:S(2)}, u32[]{:S(2)}) collective-permute-start(bf16[4,2,128,384]{3,2,1,0:T(8,128)(2,1)S(1)} %all-to-all-done.1.refs_1_), channel_id=1, source_target_pairs={{4,0},{5,1},{6,2},{7,3},{8,4},{9,5},{10,6},{11,7},{12,8},{13,9},{1... | collective-permute-start | bytes 2359304 | tf_op jit(solution)/shard_map/ppermute | solution.py:271
  48.7 2.0 %pack_q.1 = bf16[4,128,768]{2,1,0:T(8,128)(2,1)} custom-call(bf16[128,3072]{1,0:T(8,128)(2,1)} %q_ref.1), custom_call_target="tpu_custom_call" | custom-call | tf_op jit(solution)/shard_map/pack_q/pallas_call | solution.py:81
  50.8 0.7 fusion.2
  51.4 2.5 %broadcast_select_fusion.1 = s32[4]{0:T(128)S(1)} fusion(pred[]{:T(512)S(6)} %ge.21, s32[1]{0:T(128)} %get-tuple-element.36, s32[1]{0:T(128)} %get-tuple-element.37, s32[1]{0:T(128)} %get-tuple-element.38, s32[1]{0:T(128)} %get-tuple-element.35, s32[]{:T(128)S(6)} %mul.14, s32[256]{0:T(256)S(1)} %copy-done.3, s32[]{:T(128)S(6)} %select_n.44), kind=kLoop, calls=%fused_computation.10 | loop fusion | flops 20 | bytes 57 | tf_op jit(solution)/shard_map/jit(_where)/select_n | solution.py:241
  54.0 3.5 %all-to-all-start.2 = ((bf16[4,128,768]{2,1,0:T(8,128)(2,1)}), bf16[4,128,768]{2,1,0:T(8,128)(2,1)S(1)}, u32[]{:S(2)}, u32[]{:S(2)}) async-start(bf16[4,128,768]{2,1,0:T(8,128)(2,1)} %pack_q.1), calls=%async_computation.2 | async-start | bytes 1572864 | tf_op jit(solution)/shard_map/all_to_all | solution.py:278
  57.5 1.9 %collective-permute-start.4 = (bf16[4,2,128,384]{3,2,1,0:T(8,128)(2,1)}, bf16[4,2,128,384]{3,2,1,0:T(8,128)(2,1)}, u32[]{:S(2)}, u32[]{:S(2)}) collective-permute-start(bf16[4,2,128,384]{3,2,1,0:T(8,128)(2,1)} %collective-permute-done.2.refs_0_), channel_id=1, source_target_pairs={{0,4},{1,5},{2,6},{3,7},{4,8},{5,9},{6,10},{7,11},{8,12},{9,13},{1... | collective-permute-start | bytes 2359304 | tf_op jit(solution)/shard_map/ppermute | solution.py:271
  59.4 8.1 %collective-permute-start.5 = (bf16[4,2,128,384]{3,2,1,0:T(8,128)(2,1)}, bf16[4,2,128,384]{3,2,1,0:T(8,128)(2,1)}, u32[]{:S(2)}, u32[]{:S(2)}) collective-permute-start(bf16[4,2,128,384]{3,2,1,0:T(8,128)(2,1)} %collective-permute-done.3.refs_2_), channel_id=1, source_target_pairs={{4,0},{5,1},{6,2},{7,3},{8,4},{9,5},{10,6},{11,7},{12,8},{13,9},{1... | collective-permute-start | bytes 2359304 | tf_op jit(solution)/shard_map/ppermute | solution.py:271
  67.7 0.9 collective-permute-done.refs_0_
  68.5 1.9 %collective-permute-start.6 = (bf16[4,2,128,384]{3,2,1,0:T(8,128)(2,1)}, bf16[4,2,128,384]{3,2,1,0:T(8,128)(2,1)S(1)}, u32[]{:S(2)}, u32[]{:S(2)}) collective-permute-start(bf16[4,2,128,384]{3,2,1,0:T(8,128)(2,1)} %collective-permute-done.refs_0_), channel_id=1, source_target_pairs={{0,4},{1,5},{2,6},{3,7},{4,8},{5,9},{6,10},{7,11},{8,12},{9,13},{1... | collective-permute-start | bytes 2359304 | tf_op jit(solution)/shard_map/ppermute | solution.py:271
  70.4 8.1 %collective-permute-start.7 = (bf16[4,2,128,384]{3,2,1,0:T(8,128)(2,1)}, bf16[4,2,128,384]{3,2,1,0:T(8,128)(2,1)}, u32[]{:S(2)}, u32[]{:S(2)}) collective-permute-start(bf16[4,2,128,384]{3,2,1,0:T(8,128)(2,1)} %collective-permute-done.1.refs_2_), channel_id=1, source_target_pairs={{4,0},{5,1},{6,2},{7,3},{8,4},{9,5},{10,6},{11,7},{12,8},{13,9},{1... | collective-permute-start | bytes 2359304 | tf_op jit(solution)/shard_map/ppermute | solution.py:271
  79.0 0.1 and_reduce_fusion
  79.4 5.5 %attend.4 = (f32[3,128,512]{2,1,0:T(8,128)S(1)}, f32[3,2,512]{2,1,0:T(2,128)S(1)}) custom-call(f32[80]{0:T(128)S(1)} %select_n.49.bias_ref, s32[1]{0:T(128)} %bitcast.place_ref, bf16[4,128,768]{2,1,0:T(8,128)(2,1)S(1)} %all-to-all-done.2.q_ref, bf16[4,2,128,384]{3,2,1,0:T(8,128)(2,1)} %collective-permute-done.refs_0_, ...), custom_call_target="tpu_custom_call" | custom-call | flops 1207959552 | bytes 3145728 | tf_op jit(solution)/shard_map/attend/pallas_call | solution.py:199
  84.9 5.7 %attend.5 = (f32[3,128,512]{2,1,0:T(8,128)S(1)}, f32[3,2,512]{2,1,0:T(2,128)S(1)}) custom-call(f32[80]{0:T(128)S(1)} %select_n.49.bias_ref, s32[1]{0:T(128)} %bitcast.place_ref, bf16[4,128,768]{2,1,0:T(8,128)(2,1)S(1)} %all-to-all-done.2.q_ref, bf16[4,2,128,384]{3,2,1,0:T(8,128)(2,1)} %collective-permute-done.2.refs_0_, ...), custom_call_target="tpu_custom_call" | custom-call | flops 1207959552 | bytes 3145728 | tf_op jit(solution)/shard_map/attend/pallas_call | solution.py:199
  90.7 5.2 %attend.6 = bf16[4,128,384]{2,1,0:T(8,128)(2,1)} custom-call(f32[80]{0:T(128)S(1)} %select_n.49.bias_ref, s32[1]{0:T(128)} %bitcast.place_ref, bf16[4,128,768]{2,1,0:T(8,128)(2,1)S(1)} %all-to-all-done.2.q_ref, bf16[4,2,128,384]{3,2,1,0:T(8,128)(2,1)} %collective-permute-done.4.refs_0_, bf16[4,2,128,384]{3,2,1,0:T(8,128)(2,1)} %collective-permute-done.5.refs_1_, ...), custom_call_target="tpu_custom_call" | custom-call | flops 805306368 | bytes 2359296 | tf_op jit(solution)/shard_map/attend/pallas_call | solution.py:199
  96.0 5.0 %all-to-all-start.3 = ((bf16[4,128,384]{2,1,0:T(8,128)(2,1)}), bf16[4,128,384]{2,1,0:T(8,128)(2,1)S(1)}, u32[]{:S(2)}, u32[]{:S(2)}) async-start(bf16[4,128,384]{2,1,0:T(8,128)(2,1)} %attend.6), calls=%async_computation.3 | async-start | bytes 786432 | tf_op jit(solution)/shard_map/all_to_all | solution.py:278
  101.0 0.1 collective-permute-done.6.refs_0_
  101.1 2.2 %collective-permute-done.7.refs_1_ = bf16[4,2,128,384]{3,2,1,0:T(8,128)(2,1)} collective-permute-done((bf16[4,2,128,384]{3,2,1,0:T(8,128)(2,1)}, bf16[4,2,128,384]{3,2,1,0:T(8,128)(2,1)}, u32[]{:S(2)}, u32[]{:S(2)}) %collective-permute-start.7) | collective-permute-done | bytes 786464 | tf_op jit(solution)/shard_map/ppermute | solution.py:271
  103.3 4.7 %attend.7 = (bf16[128,384]{1,0:T(8,128)(2,1)S(1)}, bf16[128,384]{1,0:T(8,128)(2,1)S(1)}, bf16[128,384]{1,0:T(8,128)(2,1)S(1)}, bf16[128,384]{1,0:T(8,128)(2,1)S(1)}) custom-call(f32[80]{0:T(128)S(1)} %select_n.49.bias_ref, s32[1]{0:T(128)} %bitcast.place_ref, bf16[4,128,768]{2,1,0:T(8,128)(2,1)S(1)} %all-to-all-done.2.q_ref, ...), custom_call_target="tpu_custom_call" | custom-call | flops 805306368 | bytes 2359296 | tf_op jit(solution)/shard_map/attend/pallas_call | solution.py:199
  108.0 0.7 collective-permute-start.10
  108.7 2.3 %collective-permute-start.8 = (bf16[128,384]{1,0:T(8,128)(2,1)S(1)}, bf16[128,384]{1,0:T(8,128)(2,1)S(1)}, u32[]{:S(2)}, u32[]{:S(2)}) collective-permute-start(bf16[128,384]{1,0:T(8,128)(2,1)S(1)} %get-tuple-element.28), channel_id=1, source_target_pairs={{0,1},{1,0},{2,3},{3,2},{4,5},{5,4},{6,7},{7,6},{8,9},{9,8},{10,11... | collective-permute-start | bytes 294920 | tf_op jit(solution)/shard_map/ppermute | solution.py:289
  111.0 0.9 collective-permute-start.9
  111.9 3.1 %collective-permute-done.8.refs_1_ = bf16[128,384]{1,0:T(8,128)(2,1)S(1)} collective-permute-done((bf16[128,384]{1,0:T(8,128)(2,1)S(1)}, bf16[128,384]{1,0:T(8,128)(2,1)S(1)}, u32[]{:S(2)}, u32[]{:S(2)}) %collective-permute-start.8) | collective-permute-done | bytes 98336 | tf_op jit(solution)/shard_map/ppermute | solution.py:289
  115.0 2.4 %collective-permute-done.9.refs_2_ = bf16[128,384]{1,0:T(8,128)(2,1)S(1)} collective-permute-done((bf16[128,384]{1,0:T(8,128)(2,1)S(1)}, bf16[128,384]{1,0:T(8,128)(2,1)S(1)}, u32[]{:S(2)}, u32[]{:S(2)}) %collective-permute-start.9) | collective-permute-done | bytes 98336 | tf_op jit(solution)/shard_map/ppermute | solution.py:289
  117.4 1.1 unpack.1
  (35 shorter events, 1.4 us)
Async XLA Ops:
  2.0 16.7 %all-to-all-start = ((bf16[4,2,128,384]{3,2,1,0:T(8,128)(2,1)}), bf16[4,2,128,384]{3,2,1,0:T(8,128)(2,1)S(1)}, u32[]{:S(2)}, u32[]{:S(2)}) async-start(bf16[4,2,128,384]{3,2,1,0:T(8,128)(2,1)} %pack_kv.3), calls=%async_computation | async-start | bytes 1572864 | tf_op jit(solution)/shard_map/all_to_all | solution.py:278
  7.6 14.6 %copy-start.3 = (s32[256]{0:T(256)S(1)}, s32[256]{0:T(256)}, u32[]{:S(2)}) copy-start(s32[256]{0:T(256)} %param.8) | copy-start | bytes 3076
  18.7 16.6 %all-to-all-start.1 = ((bf16[4,2,128,384]{3,2,1,0:T(8,128)(2,1)}), bf16[4,2,128,384]{3,2,1,0:T(8,128)(2,1)S(1)}, u32[]{:S(2)}, u32[]{:S(2)}) async-start(bf16[4,2,128,384]{3,2,1,0:T(8,128)(2,1)} %pack_kv.2), calls=%async_computation.1 | async-start | bytes 1572864 | tf_op jit(solution)/shard_map/all_to_all | solution.py:278
  22.5 35.0 %collective-permute-start.2 = (bf16[4,2,128,384]{3,2,1,0:T(8,128)(2,1)S(1)}, bf16[4,2,128,384]{3,2,1,0:T(8,128)(2,1)}, u32[]{:S(2)}, u32[]{:S(2)}) collective-permute-start(bf16[4,2,128,384]{3,2,1,0:T(8,128)(2,1)S(1)} %all-to-all-done.refs_1_), channel_id=1, source_target_pairs={{0,4},{1,5},{2,6},{3,7},{4,8},{5,9},{6,10},{7,11},{8,12},{9,13},{1... | collective-permute-start | bytes 2359304 | tf_op jit(solution)/shard_map/ppermute | solution.py:271
  26.4 33.1 %collective-permute-start.3 = (bf16[4,2,128,384]{3,2,1,0:T(8,128)(2,1)S(1)}, bf16[4,2,128,384]{3,2,1,0:T(8,128)(2,1)}, u32[]{:S(2)}, u32[]{:S(2)}) collective-permute-start(bf16[4,2,128,384]{3,2,1,0:T(8,128)(2,1)S(1)} %all-to-all-done.refs_1_), channel_id=1, source_target_pairs={{4,0},{5,1},{6,2},{7,3},{8,4},{9,5},{10,6},{11,7},{12,8},{13,9},{1... | collective-permute-start | bytes 2359304 | tf_op jit(solution)/shard_map/ppermute | solution.py:271
  35.3 33.2 %collective-permute-start = (bf16[4,2,128,384]{3,2,1,0:T(8,128)(2,1)S(1)}, bf16[4,2,128,384]{3,2,1,0:T(8,128)(2,1)}, u32[]{:S(2)}, u32[]{:S(2)}) collective-permute-start(bf16[4,2,128,384]{3,2,1,0:T(8,128)(2,1)S(1)} %all-to-all-done.1.refs_1_), channel_id=1, source_target_pairs={{0,4},{1,5},{2,6},{3,7},{4,8},{5,9},{6,10},{7,11},{8,12},{9,13},{1... | collective-permute-start | bytes 2359304 | tf_op jit(solution)/shard_map/ppermute | solution.py:271
  39.1 31.3 %collective-permute-start.1 = (bf16[4,2,128,384]{3,2,1,0:T(8,128)(2,1)S(1)}, bf16[4,2,128,384]{3,2,1,0:T(8,128)(2,1)}, u32[]{:S(2)}, u32[]{:S(2)}) collective-permute-start(bf16[4,2,128,384]{3,2,1,0:T(8,128)(2,1)S(1)} %all-to-all-done.1.refs_1_), channel_id=1, source_target_pairs={{4,0},{5,1},{6,2},{7,3},{8,4},{9,5},{10,6},{11,7},{12,8},{13,9},{1... | collective-permute-start | bytes 2359304 | tf_op jit(solution)/shard_map/ppermute | solution.py:271
  54.0 24.6 %copy-start.2 = (s32[256,20]{0,1:T(8,128)S(1)}, s32[256,20]{0,1:T(8,128)}, u32[]{:S(2)}) copy-start(s32[256,20]{0,1:T(8,128)} %param.9) | copy-start | bytes 61444
  54.0 25.4 %all-to-all-start.2 = ((bf16[4,128,768]{2,1,0:T(8,128)(2,1)}), bf16[4,128,768]{2,1,0:T(8,128)(2,1)S(1)}, u32[]{:S(2)}, u32[]{:S(2)}) async-start(bf16[4,128,768]{2,1,0:T(8,128)(2,1)} %pack_q.1), calls=%async_computation.2 | async-start | bytes 1572864 | tf_op jit(solution)/shard_map/all_to_all | solution.py:278
  57.5 33.2 %collective-permute-start.4 = (bf16[4,2,128,384]{3,2,1,0:T(8,128)(2,1)}, bf16[4,2,128,384]{3,2,1,0:T(8,128)(2,1)}, u32[]{:S(2)}, u32[]{:S(2)}) collective-permute-start(bf16[4,2,128,384]{3,2,1,0:T(8,128)(2,1)} %collective-permute-done.2.refs_0_), channel_id=1, source_target_pairs={{0,4},{1,5},{2,6},{3,7},{4,8},{5,9},{6,10},{7,11},{8,12},{9,13},{1... | collective-permute-start | bytes 2359304 | tf_op jit(solution)/shard_map/ppermute | solution.py:271
  59.4 31.3 %collective-permute-start.5 = (bf16[4,2,128,384]{3,2,1,0:T(8,128)(2,1)}, bf16[4,2,128,384]{3,2,1,0:T(8,128)(2,1)}, u32[]{:S(2)}, u32[]{:S(2)}) collective-permute-start(bf16[4,2,128,384]{3,2,1,0:T(8,128)(2,1)} %collective-permute-done.3.refs_2_), channel_id=1, source_target_pairs={{4,0},{5,1},{6,2},{7,3},{8,4},{9,5},{10,6},{11,7},{12,8},{13,9},{1... | collective-permute-start | bytes 2359304 | tf_op jit(solution)/shard_map/ppermute | solution.py:271
  68.5 32.6 %collective-permute-start.6 = (bf16[4,2,128,384]{3,2,1,0:T(8,128)(2,1)}, bf16[4,2,128,384]{3,2,1,0:T(8,128)(2,1)S(1)}, u32[]{:S(2)}, u32[]{:S(2)}) collective-permute-start(bf16[4,2,128,384]{3,2,1,0:T(8,128)(2,1)} %collective-permute-done.refs_0_), channel_id=1, source_target_pairs={{0,4},{1,5},{2,6},{3,7},{4,8},{5,9},{6,10},{7,11},{8,12},{9,13},{1... | collective-permute-start | bytes 2359304 | tf_op jit(solution)/shard_map/ppermute | solution.py:271
  70.4 32.8 %collective-permute-start.7 = (bf16[4,2,128,384]{3,2,1,0:T(8,128)(2,1)}, bf16[4,2,128,384]{3,2,1,0:T(8,128)(2,1)}, u32[]{:S(2)}, u32[]{:S(2)}) collective-permute-start(bf16[4,2,128,384]{3,2,1,0:T(8,128)(2,1)} %collective-permute-done.1.refs_2_), channel_id=1, source_target_pairs={{4,0},{5,1},{6,2},{7,3},{8,4},{9,5},{10,6},{11,7},{12,8},{13,9},{1... | collective-permute-start | bytes 2359304 | tf_op jit(solution)/shard_map/ppermute | solution.py:271
  84.9 5.8 %copy-start = (f32[3,128,512]{2,1,0:T(8,128)}, f32[3,128,512]{2,1,0:T(8,128)S(1)}, u32[]{:S(2)}) copy-start(f32[3,128,512]{2,1,0:T(8,128)S(1)} %get-tuple-element.20.refs_2_) | copy-start | bytes 2359300
  96.0 7.3 %copy-start.1 = (f32[3,128,512]{2,1,0:T(8,128)S(1)}, f32[3,128,512]{2,1,0:T(8,128)}, u32[]{:S(2)}) copy-start(f32[3,128,512]{2,1,0:T(8,128)} %copy-done) | copy-start | bytes 2359300
  96.0 16.0 %all-to-all-start.3 = ((bf16[4,128,384]{2,1,0:T(8,128)(2,1)}), bf16[4,128,384]{2,1,0:T(8,128)(2,1)S(1)}, u32[]{:S(2)}, u32[]{:S(2)}) async-start(bf16[4,128,384]{2,1,0:T(8,128)(2,1)} %attend.6), calls=%async_computation.3 | async-start | bytes 786432 | tf_op jit(solution)/shard_map/all_to_all | solution.py:278
  108.0 4.0 %collective-permute-start.10 = (bf16[128,384]{1,0:T(8,128)(2,1)S(1)}, bf16[128,384]{1,0:T(8,128)(2,1)S(1)}, u32[]{:S(2)}, u32[]{:S(2)}) collective-permute-start(bf16[128,384]{1,0:T(8,128)(2,1)S(1)} %get-tuple-element.30), channel_id=1, source_target_pairs={{0,3},{1,2},{2,1},{3,0},{4,7},{5,6},{6,5},{7,4},{8,11},{9,10},{10,... | collective-permute-start | bytes 294920 | tf_op jit(solution)/shard_map/ppermute | solution.py:289
  108.7 6.3 %collective-permute-start.8 = (bf16[128,384]{1,0:T(8,128)(2,1)S(1)}, bf16[128,384]{1,0:T(8,128)(2,1)S(1)}, u32[]{:S(2)}, u32[]{:S(2)}) collective-permute-start(bf16[128,384]{1,0:T(8,128)(2,1)S(1)} %get-tuple-element.28), channel_id=1, source_target_pairs={{0,1},{1,0},{2,3},{3,2},{4,5},{5,4},{6,7},{7,6},{8,9},{9,8},{10,11... | collective-permute-start | bytes 294920 | tf_op jit(solution)/shard_map/ppermute | solution.py:289
  111.0 6.4 %collective-permute-start.9 = (bf16[128,384]{1,0:T(8,128)(2,1)S(1)}, bf16[128,384]{1,0:T(8,128)(2,1)S(1)}, u32[]{:S(2)}, u32[]{:S(2)}) collective-permute-start(bf16[128,384]{1,0:T(8,128)(2,1)S(1)} %get-tuple-element.29), channel_id=1, source_target_pairs={{0,2},{1,3},{2,0},{3,1},{4,6},{5,7},{6,4},{7,5},{8,10},{9,11},{10,... | collective-permute-start | bytes 294920 | tf_op jit(solution)/shard_map/ppermute | solution.py:289

commit v5 on v4

--- a/solution.py
+++ b/solution.py
@@ -119,58 +119,67 @@
     )(place, first, *rest)
 
 
-def attend_kernel(scale, offsets, carried, final, spread, bias_ref, place_ref, q_ref, *refs):
+def attend_kernel(scale, offsets, carried, final, spread, first, bias_ref, place_ref, q_ref, *refs):
     count = len(offsets)
     kv_refs, refs = refs[:count], refs[count:]
     s_ref, o_ref, refs = refs[-2], refs[-1], refs[:-2]
     rows = q_ref.shape[1]
     frame_rows = TPS * rows
-    q = q_ref[...].reshape(frame_rows, HEAD)
-    tops = [None] * TPS
-    for i, offset in enumerate(offsets):
-        e = offset + REACH
-        k = kv_refs[i][:, 0].reshape(frame_rows, HEAD)
-        s = lax.dot_general(k, q, (((1,), (1,)), ((), ())), preferred_element_type=jnp.float32)
-        for b in range(TPS):
-            for a in range(TPS):
-                block = s[b * rows : (b + 1) * rows, a * rows : (a + 1) * rows]
-                block = block + bias_ref[a * SPAN * TPS + e * TPS + b]
-                s_ref[i * TPS + b, :, a * rows : (a + 1) * rows] = block
-                top = jnp.max(block, axis=0, keepdims=True)
-                tops[a] = top if tops[a] is None else jnp.maximum(tops[a], top)
-    top = jnp.concatenate(tops, axis=1) * scale
     if carried:
         accum_ref, stats_ref = refs[:2]
         refs = refs[2:]
-        before = stats_ref[0, 0:1]
-        top = jnp.maximum(top, before)
-        factor = jnp.exp2(before - top)
-        total = stats_ref[0, 1:2] * factor
-        accum = accum_ref[0] * factor
-    else:
-        total = jnp.zeros((1, frame_rows), jnp.float32)
-        accum = None
-    for i in range(count):
-        s = s_ref[i * TPS : (i + 1) * TPS].reshape(frame_rows, frame_rows)
-        w = jnp.exp2(s * scale - top)
-        total = total + jnp.sum(w, axis=0, keepdims=True)
-        v = kv_refs[i][:, 1].reshape(frame_rows, HEAD)
-        part = lax.dot_general(
-            v, w.astype(jnp.bfloat16), (((0,), (0,)), ((), ())), preferred_element_type=jnp.float32
-        )
-        accum = part if accum is None else accum + part
-    if final:
-        out = (accum / total).T.reshape(TPS, rows, HEAD).astype(jnp.bfloat16)
-        if spread:
-            o_ref[...] = out
-            for t in range(TPS):
-                refs[t][...] = o_ref[place_ref[0] ^ t]
+    for h in range(kv_refs[0].shape[-1] // HEAD):
+        at = slice(h * HEAD, (h + 1) * HEAD)
+        q_at = slice((first + h) * HEAD, (first + h + 1) * HEAD)
+        q = q_ref[:, :, q_at].reshape(frame_rows, HEAD)
+        tops = [None] * TPS
+        for i, offset in enumerate(offsets):
+            e = offset + REACH
+            k = kv_refs[i][:, 0, :, at].reshape(frame_rows, HEAD)
+            s = lax.dot_general(
+                k, q, (((1,), (1,)), ((), ())), preferred_element_type=jnp.float32
+            )
+            for b in range(TPS):
+                for a in range(TPS):
+                    block = s[b * rows : (b + 1) * rows, a * rows : (a + 1) * rows]
+                    block = block + bias_ref[a * SPAN * TPS + e * TPS + b]
+                    s_ref[0, i * TPS + b, :, a * rows : (a + 1) * rows] = block
+                    top = jnp.max(block, axis=0, keepdims=True)
+                    tops[a] = top if tops[a] is None else jnp.maximum(tops[a], top)
+        top = jnp.concatenate(tops, axis=1) * scale
+        if carried:
+            before = stats_ref[h, 0:1]
+            top = jnp.maximum(top, before)
+            factor = jnp.exp2(before - top)
+            total = stats_ref[h, 1:2] * factor
+            accum = accum_ref[h] * factor
         else:
-            refs[0][...] = out
-    else:
-        refs[0][0] = accum
-        refs[1][0, 0:1] = top
-        refs[1][0, 1:2] = total
+            total = jnp.zeros((1, frame_rows), jnp.float32)
+            accum = None
+        for i in range(count):
+            s = s_ref[0, i * TPS : (i + 1) * TPS].reshape(frame_rows, frame_rows)
+            w = jnp.exp2(s * scale - top)
+            total = total + jnp.sum(w, axis=0, keepdims=True)
+            v = kv_refs[i][:, 1, :, at].reshape(frame_rows, HEAD)
+            part = lax.dot_general(
+                v,
+                w.astype(jnp.bfloat16),
+                (((0,), (0,)), ((), ())),
+                preferred_element_type=jnp.float32,
+            )
+            accum = part if accum is None else accum + part
+        if final:
+            out = (accum / total).T.reshape(TPS, rows, HEAD).astype(jnp.bfloat16)
+            if spread:
+                o_ref[h % 2] = out
+                for t in range(TPS):
+                    refs[t][:, at] = o_ref[h % 2, place_ref[0] ^ t]
+            else:
+                refs[0][:, :, at] = out
+        else:
+            refs[0][h] = accum
+            refs[1][h, 0:1] = top
+            refs[1][h, 1:2] = total
 
 
 def attend(bias, place, q, kvs, first, carry=None, final=True, spread=False):
@@ -179,23 +188,17 @@
     heads = cols // HEAD
     queries = groups * rows
     keys = len(offsets) * queries
-    kv_spec = pl.BlockSpec((groups, 2, rows, HEAD), lambda h: (0, 0, 0, h))
-    state_specs = [
-        pl.BlockSpec((1, HEAD, queries), lambda h: (h, 0, 0)),
-        pl.BlockSpec((1, 2, queries), lambda h: (h, 0, 0)),
-    ]
     if spread:
-        out_specs = [pl.BlockSpec((rows, HEAD), lambda h: (0, h))] * groups
         out_shape = [jax.ShapeDtypeStruct((rows, cols), jnp.bfloat16)] * groups
     elif final:
-        out_specs = pl.BlockSpec((groups, rows, HEAD), lambda h: (0, 0, h))
         out_shape = jax.ShapeDtypeStruct((groups, rows, cols), jnp.bfloat16)
     else:
-        out_specs = state_specs
         out_shape = [
             jax.ShapeDtypeStruct((heads, HEAD, queries), jnp.float32),
             jax.ShapeDtypeStruct((heads, 2, queries), jnp.float32),
         ]
+    whole = pl.BlockSpec(memory_space=pltpu.VMEM)
+    arrays = [q] + [kvs[o] for o in offsets] + list(carry or ())
     return pl.pallas_call(
         functools.partial(
             attend_kernel,
@@ -204,29 +207,25 @@
             carry is not None,
             final,
             spread,
+            first,
         ),
-        grid=(heads,),
-        in_specs=[
-            pl.BlockSpec(memory_space=pltpu.SMEM),
-            pl.BlockSpec(memory_space=pltpu.SMEM),
-            pl.BlockSpec((groups, rows, HEAD), lambda h: (0, 0, h + first)),
-        ]
-        + [kv_spec] * len(offsets)
-        + (state_specs if carry is not None else []),
-        out_specs=out_specs,
+        in_specs=[pl.BlockSpec(memory_space=pltpu.SMEM)] * 2 + [whole] * len(arrays),
         out_shape=out_shape,
+        out_specs=jax.tree.map(lambda _: whole, out_shape),
         scratch_shapes=[
-            pltpu.VMEM((len(offsets) * TPS, rows, queries), jnp.float32),
-            pltpu.VMEM((TPS, rows, HEAD), jnp.bfloat16),
+            pltpu.VMEM((1, len(offsets) * TPS, rows, queries), jnp.float32),
+            pltpu.VMEM((2, TPS, rows, HEAD), jnp.bfloat16),
         ],
-        compiler_params=pltpu.CompilerParams(vmem_limit_bytes=32 * 1024 * 1024),
+        compiler_params=pltpu.CompilerParams(
+            vmem_limit_bytes=(6 + 2 * len(offsets)) * 1024 * 1024
+        ),
         cost_estimate=pl.CostEstimate(
             flops=4 * heads * queries * keys * HEAD,
             bytes_accessed=2 * cols * (2 * queries + 2 * keys),
             transcendentals=heads * queries * keys,
         ),
         name="attend",
-    )(bias, place, q, *[kvs[o] for o in offsets], *(carry or ()))
+    )(bias, place, *arrays)
 
 
 def tile_bias(tile_order, tile_mask, position, frames):
@@ -319,7 +318,9 @@
     out0 = attend(after(bias0, part0[0]), place, own_q, {-2: up0b, 2: down0b}, 0, part0)
     res0 = swap(out0)
     bias1 = after(bias, out0)
-    out1 = attend(bias1, place, own_q, {-2: up1b, 2: down1b}, CHUNKS[0], part1, spread=True)
+    part1 = attend(bias1, place, own_q, {-2: up1b}, CHUNKS[0], part1, False)
+    bias1 = after(bias1, part1[0])
+    out1 = attend(bias1, place, own_q, {2: down1b}, CHUNKS[0], part1, spread=True)
     res1 = [out1[0]] + [
         swapped(out1[t], t, frames, groups) for t in (2, 3, 1)
     ]

time: 119 us -> 119 us (level)
  waiting for transfers between devices: 19.8 us -> 18 us
    ppermute x8, waiting for transfers between devices: 3.17 us -> 1.43 us  [shifted(): return lax.ppermute(block, AXES, route)]
    pallas_call x4 -> x5, Pallas kernels: 21.1 us -> 21.2 us  [attend(): pl.pallas_call(functools.partial(attend_kernel, math.log2(math.e) / math....]
  transfers between devices with their start and end apart: 15 -> 15, of which waited for: 6 -> 5; matrix products, arithmetic and copies ran while one was open for 4% -> 4% of each run, Pallas kernels for 21% -> 21%
where the time goes in v5:
time: 119 us; the launch traced here: 118 us
  starting transfers between devices  66.4 us (56%)
  Pallas kernels  28.3 us (24%)
  waiting for transfers between devices  18 us (15%)
  other arithmetic  3.13 us (3%)
  local copies, waits for them, and re-layouts  1.55 us (1%)
    ppermute x8, starting transfers between devices, shifted(): return lax.ppermute(block, AXES, route)  46 us
    pallas_call x5, Pallas kernels, attend(): pl.pallas_call(functools.partial(attend_kernel, math.log2(math.e) / math....  21.2 us
    all_to_all x4, starting transfers between devices, exchanged(): lax.all_to_all(x, AXES, split_axis=0, concat_axis=0, axis_index_groups=pl...  15.7 us
    all_to_all x4, waiting for transfers between devices, exchanged(): lax.all_to_all(x, AXES, split_axis=0, concat_axis=0, axis_index_groups=pl...  11.1 us
    ppermute x3, waiting for transfers between devices, swapped(): return lax.ppermute(x, AXES, route)  5.47 us
    ppermute x3, starting transfers between devices, swapped(): return lax.ppermute(x, AXES, route)  4.73 us
    pallas_call x2, Pallas kernels, pack_kv(): pl.pallas_call(functools.partial(pack_kv_kernel, groups, skip), in_specs=...  4 us
    select_n x1, other arithmetic, tile_bias(): own = jnp.where(position >= frames // 2, traded(own), own)  2.58 us
  transfers between devices with their start and end apart: 15, of which 5 were waited for; matrix products, arithmetic and copies ran while one was open for 4% of the time, Pallas kernels for 21%

profile of v5, /device:TPU:8, one launch (start us, length us, event | category | flops | bytes accessed | tf_op | source)
XLA Modules:
  0.0 117.9 jit_solution(7598409514030196702)
XLA Ops:
  0.0 2.0 %pack_kv.3 = bf16[4,2,128,384]{3,2,1,0:T(8,128)(2,1)} custom-call(bf16[128,3072]{1,0:T(8,128)(2,1)} %k_ref.3, bf16[128,3072]{1,0:T(8,128)(2,1)} %v_ref.3), custom_call_target="tpu_custom_call" | custom-call | tf_op jit(solution)/shard_map/pack_kv/pallas_call | solution.py:56
  2.0 3.6 %all-to-all-start = ((bf16[4,2,128,384]{3,2,1,0:T(8,128)(2,1)}), bf16[4,2,128,384]{3,2,1,0:T(8,128)(2,1)S(1)}, u32[]{:S(2)}, u32[]{:S(2)}) async-start(bf16[4,2,128,384]{3,2,1,0:T(8,128)(2,1)} %pack_kv.3), calls=%async_computation | async-start | bytes 1572864 | tf_op jit(solution)/shard_map/all_to_all | solution.py:277
  5.6 2.0 %pack_kv.2 = bf16[4,2,128,384]{3,2,1,0:T(8,128)(2,1)} custom-call(bf16[128,3072]{1,0:T(8,128)(2,1)} %k_ref.3, bf16[128,3072]{1,0:T(8,128)(2,1)} %v_ref.3), custom_call_target="tpu_custom_call" | custom-call | tf_op jit(solution)/shard_map/pack_kv/pallas_call | solution.py:56
  7.6 11.1 %all-to-all-done.refs_1_ = bf16[4,2,128,384]{3,2,1,0:T(8,128)(2,1)S(1)} async-done(((bf16[4,2,128,384]{3,2,1,0:T(8,128)(2,1)}), bf16[4,2,128,384]{3,2,1,0:T(8,128)(2,1)S(1)}, u32[]{:S(2)}, u32[]{:S(2)}) %all-to-all-start) | async-done | bytes 786464 | tf_op jit(solution)/shard_map/all_to_all | solution.py:277
  18.7 3.5 %all-to-all-start.1 = ((bf16[4,2,128,384]{3,2,1,0:T(8,128)(2,1)}), bf16[4,2,128,384]{3,2,1,0:T(8,128)(2,1)S(1)}, u32[]{:S(2)}, u32[]{:S(2)}) async-start(bf16[4,2,128,384]{3,2,1,0:T(8,128)(2,1)} %pack_kv.2), calls=%async_computation.1 | async-start | bytes 1572864 | tf_op jit(solution)/shard_map/all_to_all | solution.py:277
  22.5 3.8 %collective-permute-start.2 = (bf16[4,2,128,384]{3,2,1,0:T(8,128)(2,1)S(1)}, bf16[4,2,128,384]{3,2,1,0:T(8,128)(2,1)}, u32[]{:S(2)}, u32[]{:S(2)}) collective-permute-start(bf16[4,2,128,384]{3,2,1,0:T(8,128)(2,1)S(1)} %all-to-all-done.refs_1_), channel_id=1, source_target_pairs={{0,4},{1,5},{2,6},{3,7},{4,8},{5,9},{6,10},{7,11},{8,12},{9,13},{1... | collective-permute-start | bytes 2359304 | tf_op jit(solution)/shard_map/ppermute | solution.py:270
  26.4 8.9 %collective-permute-start.3 = (bf16[4,2,128,384]{3,2,1,0:T(8,128)(2,1)S(1)}, bf16[4,2,128,384]{3,2,1,0:T(8,128)(2,1)}, u32[]{:S(2)}, u32[]{:S(2)}) collective-permute-start(bf16[4,2,128,384]{3,2,1,0:T(8,128)(2,1)S(1)} %all-to-all-done.refs_1_), channel_id=1, source_target_pairs={{4,0},{5,1},{6,2},{7,3},{8,4},{9,5},{10,6},{11,7},{12,8},{13,9},{1... | collective-permute-start | bytes 2359304 | tf_op jit(solution)/shard_map/ppermute | solution.py:270
  35.3 3.8 %collective-permute-start = (bf16[4,2,128,384]{3,2,1,0:T(8,128)(2,1)S(1)}, bf16[4,2,128,384]{3,2,1,0:T(8,128)(2,1)}, u32[]{:S(2)}, u32[]{:S(2)}) collective-permute-start(bf16[4,2,128,384]{3,2,1,0:T(8,128)(2,1)S(1)} %all-to-all-done.1.refs_1_), channel_id=1, source_target_pairs={{0,4},{1,5},{2,6},{3,7},{4,8},{5,9},{6,10},{7,11},{8,12},{9,13},{1... | collective-permute-start | bytes 2359304 | tf_op jit(solution)/shard_map/ppermute | solution.py:270
  39.4 9.4 %collective-permute-start.1 = (bf16[4,2,128,384]{3,2,1,0:T(8,128)(2,1)S(1)}, bf16[4,2,128,384]{3,2,1,0:T(8,128)(2,1)}, u32[]{:S(2)}, u32[]{:S(2)}) collective-permute-start(bf16[4,2,128,384]{3,2,1,0:T(8,128)(2,1)S(1)} %all-to-all-done.1.refs_1_), channel_id=1, source_target_pairs={{4,0},{5,1},{6,2},{7,3},{8,4},{9,5},{10,6},{11,7},{12,8},{13,9},{1... | collective-permute-start | bytes 2359304 | tf_op jit(solution)/shard_map/ppermute | solution.py:270
  48.8 2.0 %pack_q.1 = bf16[4,128,768]{2,1,0:T(8,128)(2,1)} custom-call(bf16[128,3072]{1,0:T(8,128)(2,1)} %q_ref.1), custom_call_target="tpu_custom_call" | custom-call | tf_op jit(solution)/shard_map/pack_q/pallas_call | solution.py:81
  50.8 0.7 fusion.2
  51.4 2.6 %broadcast_select_fusion.1 = s32[4]{0:T(128)S(1)} fusion(pred[]{:T(512)S(6)} %ge.21, s32[1]{0:T(128)} %get-tuple-element.42, s32[1]{0:T(128)} %get-tuple-element.43, s32[1]{0:T(128)} %get-tuple-element.44, s32[1]{0:T(128)} %get-tuple-element.41, s32[]{:T(128)S(6)} %mul.14, s32[256]{0:T(256)S(1)} %copy-done.3, s32[]{:T(128)S(6)} %select_n.44), kind=kLoop, calls=%fused_computation.10 | loop fusion | flops 20 | bytes 57 | tf_op jit(solution)/shard_map/jit(_where)/select_n | solution.py:240
  54.0 3.5 %all-to-all-start.2 = ((bf16[4,128,768]{2,1,0:T(8,128)(2,1)}), bf16[4,128,768]{2,1,0:T(8,128)(2,1)S(1)}, u32[]{:S(2)}, u32[]{:S(2)}) async-start(bf16[4,128,768]{2,1,0:T(8,128)(2,1)} %pack_q.1), calls=%async_computation.2 | async-start | bytes 1572864 | tf_op jit(solution)/shard_map/all_to_all | solution.py:277
  57.6 1.9 %collective-permute-start.4 = (bf16[4,2,128,384]{3,2,1,0:T(8,128)(2,1)}, bf16[4,2,128,384]{3,2,1,0:T(8,128)(2,1)}, u32[]{:S(2)}, u32[]{:S(2)}) collective-permute-start(bf16[4,2,128,384]{3,2,1,0:T(8,128)(2,1)} %collective-permute-done.2.refs_0_), channel_id=1, source_target_pairs={{0,4},{1,5},{2,6},{3,7},{4,8},{5,9},{6,10},{7,11},{8,12},{9,13},{1... | collective-permute-start | bytes 2359304 | tf_op jit(solution)/shard_map/ppermute | solution.py:270
  59.5 8.1 %collective-permute-start.5 = (bf16[4,2,128,384]{3,2,1,0:T(8,128)(2,1)}, bf16[4,2,128,384]{3,2,1,0:T(8,128)(2,1)}, u32[]{:S(2)}, u32[]{:S(2)}) collective-permute-start(bf16[4,2,128,384]{3,2,1,0:T(8,128)(2,1)} %collective-permute-done.3.refs_2_), channel_id=1, source_target_pairs={{4,0},{5,1},{6,2},{7,3},{8,4},{9,5},{10,6},{11,7},{12,8},{13,9},{1... | collective-permute-start | bytes 2359304 | tf_op jit(solution)/shard_map/ppermute | solution.py:270
  67.7 0.8 collective-permute-done.refs_0_
  68.5 1.9 %collective-permute-start.6 = (bf16[4,2,128,384]{3,2,1,0:T(8,128)(2,1)}, bf16[4,2,128,384]{3,2,1,0:T(8,128)(2,1)S(1)}, u32[]{:S(2)}, u32[]{:S(2)}) collective-permute-start(bf16[4,2,128,384]{3,2,1,0:T(8,128)(2,1)} %collective-permute-done.refs_0_), channel_id=1, source_target_pairs={{0,4},{1,5},{2,6},{3,7},{4,8},{5,9},{6,10},{7,11},{8,12},{9,13},{1... | collective-permute-start | bytes 2359304 | tf_op jit(solution)/shard_map/ppermute | solution.py:270
  70.9 8.1 %collective-permute-start.7 = (bf16[4,2,128,384]{3,2,1,0:T(8,128)(2,1)}, bf16[4,2,128,384]{3,2,1,0:T(8,128)(2,1)}, u32[]{:S(2)}, u32[]{:S(2)}) collective-permute-start(bf16[4,2,128,384]{3,2,1,0:T(8,128)(2,1)} %collective-permute-done.1.refs_2_), channel_id=1, source_target_pairs={{4,0},{5,1},{6,2},{7,3},{8,4},{9,5},{10,6},{11,7},{12,8},{13,9},{1... | collective-permute-start | bytes 2359304 | tf_op jit(solution)/shard_map/ppermute | solution.py:270
  79.0 0.1 and_reduce_fusion
  79.4 5.3 %attend.5 = (f32[3,128,512]{2,1,0:T(8,128)S(1)}, f32[3,2,512]{2,1,0:T(2,128)S(1)}) custom-call(f32[80]{0:T(128)S(1)} %select_n.49.bias_ref, s32[1]{0:T(128)} %bitcast.place_ref, bf16[4,128,768]{2,1,0:T(8,128)(2,1)S(1)} %all-to-all-done.2.q_ref, bf16[4,2,128,384]{3,2,1,0:T(8,128)(2,1)} %collective-permute-done.refs_0_, ...), custom_call_target="tpu_custom_call" | custom-call | flops 1207959552 | bytes 3145728 | tf_op jit(solution)/shard_map/attend/pallas_call | solution.py:202
  84.7 5.6 %attend.6 = (f32[3,128,512]{2,1,0:T(8,128)S(1)}, f32[3,2,512]{2,1,0:T(2,128)S(1)}) custom-call(f32[80]{0:T(128)S(1)} %select_n.49.bias_ref, s32[1]{0:T(128)} %bitcast.place_ref, bf16[4,128,768]{2,1,0:T(8,128)(2,1)S(1)} %all-to-all-done.2.q_ref, bf16[4,2,128,384]{3,2,1,0:T(8,128)(2,1)} %collective-permute-done.2.refs_0_, ...), custom_call_target="tpu_custom_call" | custom-call | flops 1207959552 | bytes 3145728 | tf_op jit(solution)/shard_map/attend/pallas_call | solution.py:202
  90.3 5.0 %attend.7 = bf16[4,128,384]{2,1,0:T(8,128)(2,1)} custom-call(f32[80]{0:T(128)S(1)} %select_n.49.bias_ref, s32[1]{0:T(128)} %bitcast.place_ref, bf16[4,128,768]{2,1,0:T(8,128)(2,1)S(1)} %all-to-all-done.2.q_ref, bf16[4,2,128,384]{3,2,1,0:T(8,128)(2,1)} %collective-permute-done.4.refs_0_, bf16[4,2,128,384]{3,2,1,0:T(8,128)(2,1)} %collective-permute-done.5.refs_1_, ...), custom_call_target="tpu_custom_call" | custom-call | flops 805306368 | bytes 2359296 | tf_op jit(solution)/shard_map/attend/pallas_call | solution.py:202
  95.3 5.1 %all-to-all-start.3 = ((bf16[4,128,384]{2,1,0:T(8,128)(2,1)}), bf16[4,128,384]{2,1,0:T(8,128)(2,1)S(1)}, u32[]{:S(2)}, u32[]{:S(2)}) async-start(bf16[4,128,384]{2,1,0:T(8,128)(2,1)} %attend.7), calls=%async_computation.3 | async-start | bytes 786432 | tf_op jit(solution)/shard_map/all_to_all | solution.py:277
  100.4 0.6 collective-permute-done.6.refs_0_
  101.1 2.3 %attend.8 = (f32[3,128,512]{2,1,0:T(8,128)S(1)}, f32[3,2,512]{2,1,0:T(2,128)S(1)}) custom-call(f32[80]{0:T(128)S(1)} %select_n.49.bias_ref, s32[1]{0:T(128)} %bitcast.place_ref, bf16[4,128,768]{2,1,0:T(8,128)(2,1)S(1)} %all-to-all-done.2.q_ref, bf16[4,2,128,384]{3,2,1,0:T(8,128)(2,1)S(1)} %collective-permute-done.6.refs_0_, f32[3,128,512]{2,1,0:T(8,128)S(1)} %copy-done.1, ...), custom_call_target="tpu_custom_call" | custom-call | flops 402653184 | bytes 1572864 | tf_op jit(solution)/shard_map/attend/pallas_call | solution.py:202
  103.4 3.0 %attend.9 = (bf16[128,384]{1,0:T(8,128)(2,1)S(1)}, bf16[128,384]{1,0:T(8,128)(2,1)S(1)}, bf16[128,384]{1,0:T(8,128)(2,1)S(1)}, bf16[128,384]{1,0:T(8,128)(2,1)S(1)}) custom-call(f32[80]{0:T(128)S(1)} %select_n.49.bias_ref, s32[1]{0:T(128)} %bitcast.place_ref, bf16[4,128,768]{2,1,0:T(8,128)(2,1)S(1)} %all-to-all-done.2.q_ref, ...), custom_call_target="tpu_custom_call" | custom-call | flops 402653184 | bytes 1572864 | tf_op jit(solution)/shard_map/attend/pallas_call | solution.py:202
  106.5 1.5 %collective-permute-start.10 = (bf16[128,384]{1,0:T(8,128)(2,1)S(1)}, bf16[128,384]{1,0:T(8,128)(2,1)S(1)}, u32[]{:S(2)}, u32[]{:S(2)}) collective-permute-start(bf16[128,384]{1,0:T(8,128)(2,1)S(1)} %get-tuple-element.36), channel_id=1, source_target_pairs={{0,3},{1,2},{2,1},{3,0},{4,7},{5,6},{6,5},{7,4},{8,11},{9,10},{10,... | collective-permute-start | bytes 294920 | tf_op jit(solution)/shard_map/ppermute | solution.py:288
  107.9 2.4 %collective-permute-start.8 = (bf16[128,384]{1,0:T(8,128)(2,1)S(1)}, bf16[128,384]{1,0:T(8,128)(2,1)S(1)}, u32[]{:S(2)}, u32[]{:S(2)}) collective-permute-start(bf16[128,384]{1,0:T(8,128)(2,1)S(1)} %get-tuple-element.34), channel_id=1, source_target_pairs={{0,1},{1,0},{2,3},{3,2},{4,5},{5,4},{6,7},{7,6},{8,9},{9,8},{10,11... | collective-permute-start | bytes 294920 | tf_op jit(solution)/shard_map/ppermute | solution.py:288
  110.3 0.9 collective-permute-start.9
  111.2 3.1 %collective-permute-done.8.refs_1_ = bf16[128,384]{1,0:T(8,128)(2,1)S(1)} collective-permute-done((bf16[128,384]{1,0:T(8,128)(2,1)S(1)}, bf16[128,384]{1,0:T(8,128)(2,1)S(1)}, u32[]{:S(2)}, u32[]{:S(2)}) %collective-permute-start.8) | collective-permute-done | bytes 98336 | tf_op jit(solution)/shard_map/ppermute | solution.py:288
  114.3 2.4 %collective-permute-done.9.refs_2_ = bf16[128,384]{1,0:T(8,128)(2,1)S(1)} collective-permute-done((bf16[128,384]{1,0:T(8,128)(2,1)S(1)}, bf16[128,384]{1,0:T(8,128)(2,1)S(1)}, u32[]{:S(2)}, u32[]{:S(2)}) %collective-permute-start.9) | collective-permute-done | bytes 98336 | tf_op jit(solution)/shard_map/ppermute | solution.py:288
  116.7 1.1 unpack.1
  (36 shorter events, 1.4 us)
Async XLA Ops:
  2.0 16.7 %all-to-all-start = ((bf16[4,2,128,384]{3,2,1,0:T(8,128)(2,1)}), bf16[4,2,128,384]{3,2,1,0:T(8,128)(2,1)S(1)}, u32[]{:S(2)}, u32[]{:S(2)}) async-start(bf16[4,2,128,384]{3,2,1,0:T(8,128)(2,1)} %pack_kv.3), calls=%async_computation | async-start | bytes 1572864 | tf_op jit(solution)/shard_map/all_to_all | solution.py:277
  7.6 14.6 %copy-start.3 = (s32[256]{0:T(256)S(1)}, s32[256]{0:T(256)}, u32[]{:S(2)}) copy-start(s32[256]{0:T(256)} %param.8) | copy-start | bytes 3076
  18.7 16.6 %all-to-all-start.1 = ((bf16[4,2,128,384]{3,2,1,0:T(8,128)(2,1)}), bf16[4,2,128,384]{3,2,1,0:T(8,128)(2,1)S(1)}, u32[]{:S(2)}, u32[]{:S(2)}) async-start(bf16[4,2,128,384]{3,2,1,0:T(8,128)(2,1)} %pack_kv.2), calls=%async_computation.1 | async-start | bytes 1572864 | tf_op jit(solution)/shard_map/all_to_all | solution.py:277
  22.5 35.0 %collective-permute-start.2 = (bf16[4,2,128,384]{3,2,1,0:T(8,128)(2,1)S(1)}, bf16[4,2,128,384]{3,2,1,0:T(8,128)(2,1)}, u32[]{:S(2)}, u32[]{:S(2)}) collective-permute-start(bf16[4,2,128,384]{3,2,1,0:T(8,128)(2,1)S(1)} %all-to-all-done.refs_1_), channel_id=1, source_target_pairs={{0,4},{1,5},{2,6},{3,7},{4,8},{5,9},{6,10},{7,11},{8,12},{9,13},{1... | collective-permute-start | bytes 2359304 | tf_op jit(solution)/shard_map/ppermute | solution.py:270
  26.4 33.1 %collective-permute-start.3 = (bf16[4,2,128,384]{3,2,1,0:T(8,128)(2,1)S(1)}, bf16[4,2,128,384]{3,2,1,0:T(8,128)(2,1)}, u32[]{:S(2)}, u32[]{:S(2)}) collective-permute-start(bf16[4,2,128,384]{3,2,1,0:T(8,128)(2,1)S(1)} %all-to-all-done.refs_1_), channel_id=1, source_target_pairs={{4,0},{5,1},{6,2},{7,3},{8,4},{9,5},{10,6},{11,7},{12,8},{13,9},{1... | collective-permute-start | bytes 2359304 | tf_op jit(solution)/shard_map/ppermute | solution.py:270
  35.3 33.2 %collective-permute-start = (bf16[4,2,128,384]{3,2,1,0:T(8,128)(2,1)S(1)}, bf16[4,2,128,384]{3,2,1,0:T(8,128)(2,1)}, u32[]{:S(2)}, u32[]{:S(2)}) collective-permute-start(bf16[4,2,128,384]{3,2,1,0:T(8,128)(2,1)S(1)} %all-to-all-done.1.refs_1_), channel_id=1, source_target_pairs={{0,4},{1,5},{2,6},{3,7},{4,8},{5,9},{6,10},{7,11},{8,12},{9,13},{1... | collective-permute-start | bytes 2359304 | tf_op jit(solution)/shard_map/ppermute | solution.py:270
  39.4 31.5 %collective-permute-start.1 = (bf16[4,2,128,384]{3,2,1,0:T(8,128)(2,1)S(1)}, bf16[4,2,128,384]{3,2,1,0:T(8,128)(2,1)}, u32[]{:S(2)}, u32[]{:S(2)}) collective-permute-start(bf16[4,2,128,384]{3,2,1,0:T(8,128)(2,1)S(1)} %all-to-all-done.1.refs_1_), channel_id=1, source_target_pairs={{4,0},{5,1},{6,2},{7,3},{8,4},{9,5},{10,6},{11,7},{12,8},{13,9},{1... | collective-permute-start | bytes 2359304 | tf_op jit(solution)/shard_map/ppermute | solution.py:270
  54.0 16.4 %copy-start.2 = (s32[256,20]{0,1:T(8,128)S(1)}, s32[256,20]{0,1:T(8,128)}, u32[]{:S(2)}) copy-start(s32[256,20]{0,1:T(8,128)} %param.9) | copy-start | bytes 61444
  54.0 25.3 %all-to-all-start.2 = ((bf16[4,128,768]{2,1,0:T(8,128)(2,1)}), bf16[4,128,768]{2,1,0:T(8,128)(2,1)S(1)}, u32[]{:S(2)}, u32[]{:S(2)}) async-start(bf16[4,128,768]{2,1,0:T(8,128)(2,1)} %pack_q.1), calls=%async_computation.2 | async-start | bytes 1572864 | tf_op jit(solution)/shard_map/all_to_all | solution.py:277
  57.6 32.7 %collective-permute-start.4 = (bf16[4,2,128,384]{3,2,1,0:T(8,128)(2,1)}, bf16[4,2,128,384]{3,2,1,0:T(8,128)(2,1)}, u32[]{:S(2)}, u32[]{:S(2)}) collective-permute-start(bf16[4,2,128,384]{3,2,1,0:T(8,128)(2,1)} %collective-permute-done.2.refs_0_), channel_id=1, source_target_pairs={{0,4},{1,5},{2,6},{3,7},{4,8},{5,9},{6,10},{7,11},{8,12},{9,13},{1... | collective-permute-start | bytes 2359304 | tf_op jit(solution)/shard_map/ppermute | solution.py:270
  59.5 30.8 %collective-permute-start.5 = (bf16[4,2,128,384]{3,2,1,0:T(8,128)(2,1)}, bf16[4,2,128,384]{3,2,1,0:T(8,128)(2,1)}, u32[]{:S(2)}, u32[]{:S(2)}) collective-permute-start(bf16[4,2,128,384]{3,2,1,0:T(8,128)(2,1)} %collective-permute-done.3.refs_2_), channel_id=1, source_target_pairs={{4,0},{5,1},{6,2},{7,3},{8,4},{9,5},{10,6},{11,7},{12,8},{13,9},{1... | collective-permute-start | bytes 2359304 | tf_op jit(solution)/shard_map/ppermute | solution.py:270
  68.5 32.5 %collective-permute-start.6 = (bf16[4,2,128,384]{3,2,1,0:T(8,128)(2,1)}, bf16[4,2,128,384]{3,2,1,0:T(8,128)(2,1)S(1)}, u32[]{:S(2)}, u32[]{:S(2)}) collective-permute-start(bf16[4,2,128,384]{3,2,1,0:T(8,128)(2,1)} %collective-permute-done.refs_0_), channel_id=1, source_target_pairs={{0,4},{1,5},{2,6},{3,7},{4,8},{5,9},{6,10},{7,11},{8,12},{9,13},{1... | collective-permute-start | bytes 2359304 | tf_op jit(solution)/shard_map/ppermute | solution.py:270
  70.9 32.6 %collective-permute-start.7 = (bf16[4,2,128,384]{3,2,1,0:T(8,128)(2,1)}, bf16[4,2,128,384]{3,2,1,0:T(8,128)(2,1)}, u32[]{:S(2)}, u32[]{:S(2)}) collective-permute-start(bf16[4,2,128,384]{3,2,1,0:T(8,128)(2,1)} %collective-permute-done.1.refs_2_), channel_id=1, source_target_pairs={{4,0},{5,1},{6,2},{7,3},{8,4},{9,5},{10,6},{11,7},{12,8},{13,9},{1... | collective-permute-start | bytes 2359304 | tf_op jit(solution)/shard_map/ppermute | solution.py:270
  84.7 5.6 %copy-start = (f32[3,128,512]{2,1,0:T(8,128)}, f32[3,128,512]{2,1,0:T(8,128)S(1)}, u32[]{:S(2)}) copy-start(f32[3,128,512]{2,1,0:T(8,128)S(1)} %get-tuple-element.23.refs_1_) | copy-start | bytes 2359300
  95.3 5.7 %copy-start.1 = (f32[3,128,512]{2,1,0:T(8,128)S(1)}, f32[3,128,512]{2,1,0:T(8,128)}, u32[]{:S(2)}) copy-start(f32[3,128,512]{2,1,0:T(8,128)} %copy-done) | copy-start | bytes 2359300
  95.3 15.9 %all-to-all-start.3 = ((bf16[4,128,384]{2,1,0:T(8,128)(2,1)}), bf16[4,128,384]{2,1,0:T(8,128)(2,1)S(1)}, u32[]{:S(2)}, u32[]{:S(2)}) async-start(bf16[4,128,384]{2,1,0:T(8,128)(2,1)} %attend.7), calls=%async_computation.3 | async-start | bytes 786432 | tf_op jit(solution)/shard_map/all_to_all | solution.py:277
  106.5 4.7 %collective-permute-start.10 = (bf16[128,384]{1,0:T(8,128)(2,1)S(1)}, bf16[128,384]{1,0:T(8,128)(2,1)S(1)}, u32[]{:S(2)}, u32[]{:S(2)}) collective-permute-start(bf16[128,384]{1,0:T(8,128)(2,1)S(1)} %get-tuple-element.36), channel_id=1, source_target_pairs={{0,3},{1,2},{2,1},{3,0},{4,7},{5,6},{6,5},{7,4},{8,11},{9,10},{10,... | collective-permute-start | bytes 294920 | tf_op jit(solution)/shard_map/ppermute | solution.py:288
  107.9 6.3 %collective-permute-start.8 = (bf16[128,384]{1,0:T(8,128)(2,1)S(1)}, bf16[128,384]{1,0:T(8,128)(2,1)S(1)}, u32[]{:S(2)}, u32[]{:S(2)}) collective-permute-start(bf16[128,384]{1,0:T(8,128)(2,1)S(1)} %get-tuple-element.34), channel_id=1, source_target_pairs={{0,1},{1,0},{2,3},{3,2},{4,5},{5,4},{6,7},{7,6},{8,9},{9,8},{10,11... | collective-permute-start | bytes 294920 | tf_op jit(solution)/shard_map/ppermute | solution.py:288
  110.3 6.3 %collective-permute-start.9 = (bf16[128,384]{1,0:T(8,128)(2,1)S(1)}, bf16[128,384]{1,0:T(8,128)(2,1)S(1)}, u32[]{:S(2)}, u32[]{:S(2)}) collective-permute-start(bf16[128,384]{1,0:T(8,128)(2,1)S(1)} %get-tuple-element.35), channel_id=1, source_target_pairs={{0,2},{1,3},{2,0},{3,1},{4,6},{5,7},{6,4},{7,5},{8,10},{9,11},{10,... | collective-permute-start | bytes 294920 | tf_op jit(solution)/shard_map/ppermute | solution.py:288

commit v6 on v5

--- a/solution.py
+++ b/solution.py
@@ -92,31 +92,32 @@
     )(queries)
 
 
-def unpack_kernel(groups, place_ref, first_ref, *refs):
-    rest, out_ref, sems = refs[:groups], refs[groups], refs[groups + 1]
-    width, cols = out_ref.shape[1] // groups, first_ref.shape[-1]
-    place = place_ref[0]
-    pairs = []
-    for t in range(groups):
-        start = pl.multiple_of((place ^ t) * width + cols, HEAD)
-        pairs.append((rest[t], out_ref.at[:, pl.ds(start, width - cols)]))
-    for u in range(groups):
-        pairs.append((first_ref.at[u], out_ref.at[:, pl.ds(u * width, cols)]))
+def unpack_kernel(groups, place_ref, *refs):
+    pieces, out_ref, sems = refs[:-2], refs[-2], refs[-1]
+    width = out_ref.shape[1] // groups
+    pairs, first = [], 0
+    for c in range(len(pieces) // groups):
+        cols = pieces[c * groups].shape[-1]
+        for t in range(groups):
+            start = pl.multiple_of((place_ref[0] ^ t) * width + first, HEAD)
+            pairs.append((pieces[c * groups + t], out_ref.at[:, pl.ds(start, cols)]))
+        first += cols
     run_copies(pairs, sems)
 
 
-def unpack(place, first, rest):
-    groups, rows, cols = first.shape
-    width = groups * (cols + rest[0].shape[-1])
+def unpack(place, chunks):
+    groups, rows = len(chunks[0]), chunks[0][0].shape[0]
+    width = groups * sum(c[0].shape[-1] for c in chunks)
+    pieces = [p for c in chunks for p in c]
     return pl.pallas_call(
         functools.partial(unpack_kernel, groups),
         in_specs=[pl.BlockSpec(memory_space=pltpu.SMEM)]
-        + [pl.BlockSpec(memory_space=pl.ANY)] * (1 + groups),
+        + [pl.BlockSpec(memory_space=pl.ANY)] * len(pieces),
         out_shape=jax.ShapeDtypeStruct((rows, width), jnp.bfloat16),
-        scratch_shapes=[pltpu.SemaphoreType.DMA((2 * groups,))],
+        scratch_shapes=[pltpu.SemaphoreType.DMA((len(pieces),))],
         compiler_params=pltpu.CompilerParams(vmem_limit_bytes=SMALL),
         name="unpack",
-    )(place, first, *rest)
+    )(place, *pieces)
 
 
 def attend_kernel(scale, offsets, carried, final, spread, first, bias_ref, place_ref, q_ref, *refs):
@@ -297,6 +298,10 @@
     frames = lax.axis_size("blk")
     position = lax.axis_index("blk")
     move = functools.partial(shifted, frames=frames, groups=groups)
+    def spread_out(parts):
+        moved = {t: swapped(parts[t], t, frames, groups) for t in (2, 3, 1)}
+        return [parts[0]] + [moved[t] for t in (1, 2, 3)]
+
     swap = functools.partial(exchanged, frames=frames, groups=groups)
     u = lax.axis_index("uly")
     place = jnp.where((position >= frames // 2) & (u % 2 == 1), u ^ 2, u).astype(jnp.int32).reshape(1)
@@ -315,16 +320,13 @@
     part1 = attend(bias, place, own_q, {-1: up1, 0: own1, 1: down1}, CHUNKS[0], None, False)
     bias0 = after(bias, part1[0])
     part0 = attend(bias0, place, own_q, {-1: up0, 0: own0, 1: down0}, 0, None, False)
-    out0 = attend(after(bias0, part0[0]), place, own_q, {-2: up0b, 2: down0b}, 0, part0)
-    res0 = swap(out0)
-    bias1 = after(bias, out0)
+    out0 = attend(after(bias0, part0[0]), place, own_q, {-2: up0b, 2: down0b}, 0, part0, spread=True)
+    res0 = spread_out(out0)
+    bias1 = after(bias, out0[0])
     part1 = attend(bias1, place, own_q, {-2: up1b}, CHUNKS[0], part1, False)
     bias1 = after(bias1, part1[0])
     out1 = attend(bias1, place, own_q, {2: down1b}, CHUNKS[0], part1, spread=True)
-    res1 = [out1[0]] + [
-        swapped(out1[t], t, frames, groups) for t in (2, 3, 1)
-    ]
-    return unpack(place, res0, [res1[0], res1[3], res1[1], res1[2]])
+    return unpack(place, [res0, spread_out(out1)])
 
 
 def solution(mesh):

time: 119 us -> 119 us (level)
    ppermute x3 -> x6, starting transfers between devices: 4.73 us -> 10.1 us  [swapped(): return lax.ppermute(x, AXES, route)]
    all_to_all x4 -> x3, starting transfers between devices: 15.7 us -> 10.6 us  [exchanged(): lax.all_to_all(x, AXES, split_axis=0, concat_axis=0, axis_index_groups=pl...]
    ppermute x8, waiting for transfers between devices: 1.43 us -> 2.94 us  [shifted(): return lax.ppermute(block, AXES, route)]
    ppermute x3 -> x6, waiting for transfers between devices: 5.47 us -> 4.68 us  [swapped(): return lax.ppermute(x, AXES, route)]
    all_to_all x4 -> x3, waiting for transfers between devices: 11.1 us -> 11.1 us  [exchanged(): lax.all_to_all(x, AXES, split_axis=0, concat_axis=0, axis_index_groups=pl...]
  transfers between devices with their start and end apart: 15 -> 17, of which waited for: 5 -> 5; matrix products, arithmetic and copies ran while one was open for 4% -> 4% of each run, Pallas kernels for 21% -> 21%
where the time goes in v6:
time: 119 us; the launch traced here: 118 us
  starting transfers between devices  66.7 us (56%)
  Pallas kernels  27.3 us (23%)
  waiting for transfers between devices  18.8 us (16%)
  other arithmetic  3.13 us (3%)
  local copies, waits for them, and re-layouts  1.54 us (1%)
    ppermute x8, starting transfers between devices, shifted(): return lax.ppermute(block, AXES, route)  46 us
    pallas_call x5, Pallas kernels, attend(): pl.pallas_call(functools.partial(attend_kernel, math.log2(math.e) / math....  20.2 us
    all_to_all x3, waiting for transfers between devices, exchanged(): lax.all_to_all(x, AXES, split_axis=0, concat_axis=0, axis_index_groups=pl...  11.1 us
    all_to_all x3, starting transfers between devices, exchanged(): lax.all_to_all(x, AXES, split_axis=0, concat_axis=0, axis_index_groups=pl...  10.6 us
    ppermute x6, starting transfers between devices, swapped(): return lax.ppermute(x, AXES, route)  10.1 us
    ppermute x6, waiting for transfers between devices, swapped(): return lax.ppermute(x, AXES, route)  4.68 us
    pallas_call x2, Pallas kernels, pack_kv(): pl.pallas_call(functools.partial(pack_kv_kernel, groups, skip), in_specs=...  4 us
    ppermute x8, waiting for transfers between devices, shifted(): return lax.ppermute(block, AXES, route)  2.94 us
  transfers between devices with their start and end apart: 17, of which 5 were waited for; matrix products, arithmetic and copies ran while one was open for 4% of the time, Pallas kernels for 21%

profile of v6, /device:TPU:8, one launch (start us, length us, event | category | flops | bytes accessed | tf_op | source)
XLA Modules:
  0.0 117.8 jit_solution(3774670273788394231)
XLA Ops:
  0.0 2.0 %pack_kv.3 = bf16[4,2,128,384]{3,2,1,0:T(8,128)(2,1)} custom-call(bf16[128,3072]{1,0:T(8,128)(2,1)} %k_ref.3, bf16[128,3072]{1,0:T(8,128)(2,1)} %v_ref.3), custom_call_target="tpu_custom_call" | custom-call | tf_op jit(solution)/shard_map/pack_kv/pallas_call | solution.py:56
  2.0 3.6 %all-to-all-start = ((bf16[4,2,128,384]{3,2,1,0:T(8,128)(2,1)}), bf16[4,2,128,384]{3,2,1,0:T(8,128)(2,1)S(1)}, u32[]{:S(2)}, u32[]{:S(2)}) async-start(bf16[4,2,128,384]{3,2,1,0:T(8,128)(2,1)} %pack_kv.3), calls=%async_computation | async-start | bytes 1572864 | tf_op jit(solution)/shard_map/all_to_all | solution.py:278
  5.6 2.0 %pack_kv.2 = bf16[4,2,128,384]{3,2,1,0:T(8,128)(2,1)} custom-call(bf16[128,3072]{1,0:T(8,128)(2,1)} %k_ref.3, bf16[128,3072]{1,0:T(8,128)(2,1)} %v_ref.3), custom_call_target="tpu_custom_call" | custom-call | tf_op jit(solution)/shard_map/pack_kv/pallas_call | solution.py:56
  7.6 11.1 %all-to-all-done.refs_1_ = bf16[4,2,128,384]{3,2,1,0:T(8,128)(2,1)S(1)} async-done(((bf16[4,2,128,384]{3,2,1,0:T(8,128)(2,1)}), bf16[4,2,128,384]{3,2,1,0:T(8,128)(2,1)S(1)}, u32[]{:S(2)}, u32[]{:S(2)}) %all-to-all-start) | async-done | bytes 786464 | tf_op jit(solution)/shard_map/all_to_all | solution.py:278
  18.7 3.5 %all-to-all-start.1 = ((bf16[4,2,128,384]{3,2,1,0:T(8,128)(2,1)}), bf16[4,2,128,384]{3,2,1,0:T(8,128)(2,1)S(1)}, u32[]{:S(2)}, u32[]{:S(2)}) async-start(bf16[4,2,128,384]{3,2,1,0:T(8,128)(2,1)} %pack_kv.2), calls=%async_computation.1 | async-start | bytes 1572864 | tf_op jit(solution)/shard_map/all_to_all | solution.py:278
  22.5 3.8 %collective-permute-start.2 = (bf16[4,2,128,384]{3,2,1,0:T(8,128)(2,1)S(1)}, bf16[4,2,128,384]{3,2,1,0:T(8,128)(2,1)}, u32[]{:S(2)}, u32[]{:S(2)}) collective-permute-start(bf16[4,2,128,384]{3,2,1,0:T(8,128)(2,1)S(1)} %all-to-all-done.refs_1_), channel_id=1, source_target_pairs={{0,4},{1,5},{2,6},{3,7},{4,8},{5,9},{6,10},{7,11},{8,12},{9,13},{1... | collective-permute-start | bytes 2359304 | tf_op jit(solution)/shard_map/ppermute | solution.py:271
  26.4 8.9 %collective-permute-start.3 = (bf16[4,2,128,384]{3,2,1,0:T(8,128)(2,1)S(1)}, bf16[4,2,128,384]{3,2,1,0:T(8,128)(2,1)}, u32[]{:S(2)}, u32[]{:S(2)}) collective-permute-start(bf16[4,2,128,384]{3,2,1,0:T(8,128)(2,1)S(1)} %all-to-all-done.refs_1_), channel_id=1, source_target_pairs={{4,0},{5,1},{6,2},{7,3},{8,4},{9,5},{10,6},{11,7},{12,8},{13,9},{1... | collective-permute-start | bytes 2359304 | tf_op jit(solution)/shard_map/ppermute | solution.py:271
  35.3 3.8 %collective-permute-start = (bf16[4,2,128,384]{3,2,1,0:T(8,128)(2,1)S(1)}, bf16[4,2,128,384]{3,2,1,0:T(8,128)(2,1)}, u32[]{:S(2)}, u32[]{:S(2)}) collective-permute-start(bf16[4,2,128,384]{3,2,1,0:T(8,128)(2,1)S(1)} %all-to-all-done.1.refs_1_), channel_id=1, source_target_pairs={{0,4},{1,5},{2,6},{3,7},{4,8},{5,9},{6,10},{7,11},{8,12},{9,13},{1... | collective-permute-start | bytes 2359304 | tf_op jit(solution)/shard_map/ppermute | solution.py:271
  39.2 9.4 %collective-permute-start.1 = (bf16[4,2,128,384]{3,2,1,0:T(8,128)(2,1)S(1)}, bf16[4,2,128,384]{3,2,1,0:T(8,128)(2,1)}, u32[]{:S(2)}, u32[]{:S(2)}) collective-permute-start(bf16[4,2,128,384]{3,2,1,0:T(8,128)(2,1)S(1)} %all-to-all-done.1.refs_1_), channel_id=1, source_target_pairs={{4,0},{5,1},{6,2},{7,3},{8,4},{9,5},{10,6},{11,7},{12,8},{13,9},{1... | collective-permute-start | bytes 2359304 | tf_op jit(solution)/shard_map/ppermute | solution.py:271
  48.7 2.0 %pack_q.1 = bf16[4,128,768]{2,1,0:T(8,128)(2,1)} custom-call(bf16[128,3072]{1,0:T(8,128)(2,1)} %q_ref.1), custom_call_target="tpu_custom_call" | custom-call | tf_op jit(solution)/shard_map/pack_q/pallas_call | solution.py:81
  50.8 0.7 fusion.2
  51.4 2.6 %broadcast_select_fusion.1 = s32[4]{0:T(128)S(1)} fusion(pred[]{:T(512)S(6)} %ge.21, s32[1]{0:T(128)} %get-tuple-element.50, s32[1]{0:T(128)} %get-tuple-element.51, s32[1]{0:T(128)} %get-tuple-element.52, s32[1]{0:T(128)} %get-tuple-element.49, s32[]{:T(128)S(6)} %mul.14, s32[256]{0:T(256)S(1)} %copy-done.1, s32[]{:T(128)S(6)} %select_n.44), kind=kLoop, calls=%fused_computation.10 | loop fusion | flops 20 | bytes 57 | tf_op jit(solution)/shard_map/jit(_where)/select_n | solution.py:241
  54.0 3.5 %all-to-all-start.2 = ((bf16[4,128,768]{2,1,0:T(8,128)(2,1)}), bf16[4,128,768]{2,1,0:T(8,128)(2,1)S(1)}, u32[]{:S(2)}, u32[]{:S(2)}) async-start(bf16[4,128,768]{2,1,0:T(8,128)(2,1)} %pack_q.1), calls=%async_computation.2 | async-start | bytes 1572864 | tf_op jit(solution)/shard_map/all_to_all | solution.py:278
  57.6 1.9 %collective-permute-start.4 = (bf16[4,2,128,384]{3,2,1,0:T(8,128)(2,1)}, bf16[4,2,128,384]{3,2,1,0:T(8,128)(2,1)}, u32[]{:S(2)}, u32[]{:S(2)}) collective-permute-start(bf16[4,2,128,384]{3,2,1,0:T(8,128)(2,1)} %collective-permute-done.2.refs_0_), channel_id=1, source_target_pairs={{0,4},{1,5},{2,6},{3,7},{4,8},{5,9},{6,10},{7,11},{8,12},{9,13},{1... | collective-permute-start | bytes 2359304 | tf_op jit(solution)/shard_map/ppermute | solution.py:271
  59.5 8.1 %collective-permute-start.5 = (bf16[4,2,128,384]{3,2,1,0:T(8,128)(2,1)}, bf16[4,2,128,384]{3,2,1,0:T(8,128)(2,1)}, u32[]{:S(2)}, u32[]{:S(2)}) collective-permute-start(bf16[4,2,128,384]{3,2,1,0:T(8,128)(2,1)} %collective-permute-done.3.refs_2_), channel_id=1, source_target_pairs={{4,0},{5,1},{6,2},{7,3},{8,4},{9,5},{10,6},{11,7},{12,8},{13,9},{1... | collective-permute-start | bytes 2359304 | tf_op jit(solution)/shard_map/ppermute | solution.py:271
  67.7 0.9 collective-permute-done.refs_0_
  68.5 1.9 %collective-permute-start.9 = (bf16[4,2,128,384]{3,2,1,0:T(8,128)(2,1)}, bf16[4,2,128,384]{3,2,1,0:T(8,128)(2,1)S(1)}, u32[]{:S(2)}, u32[]{:S(2)}) collective-permute-start(bf16[4,2,128,384]{3,2,1,0:T(8,128)(2,1)} %collective-permute-done.refs_0_), channel_id=1, source_target_pairs={{0,4},{1,5},{2,6},{3,7},{4,8},{5,9},{6,10},{7,11},{8,12},{9,13},{1... | collective-permute-start | bytes 2359304 | tf_op jit(solution)/shard_map/ppermute | solution.py:271
  70.5 8.1 %collective-permute-start.10 = (bf16[4,2,128,384]{3,2,1,0:T(8,128)(2,1)}, bf16[4,2,128,384]{3,2,1,0:T(8,128)(2,1)}, u32[]{:S(2)}, u32[]{:S(2)}) collective-permute-start(bf16[4,2,128,384]{3,2,1,0:T(8,128)(2,1)} %collective-permute-done.1.refs_2_), channel_id=1, source_target_pairs={{4,0},{5,1},{6,2},{7,3},{8,4},{9,5},{10,6},{11,7},{12,8},{13,9},{1... | collective-permute-start | bytes 2359304 | tf_op jit(solution)/shard_map/ppermute | solution.py:271
  79.1 0.1 and_reduce_fusion
  79.5 5.3 %attend.5 = (f32[3,128,512]{2,1,0:T(8,128)S(1)}, f32[3,2,512]{2,1,0:T(2,128)S(1)}) custom-call(f32[80]{0:T(128)S(1)} %select_n.49.bias_ref, s32[1]{0:T(128)} %bitcast.place_ref, bf16[4,128,768]{2,1,0:T(8,128)(2,1)S(1)} %all-to-all-done.2.q_ref, bf16[4,2,128,384]{3,2,1,0:T(8,128)(2,1)} %collective-permute-done.refs_0_, ...), custom_call_target="tpu_custom_call" | custom-call | flops 1207959552 | bytes 3145728 | tf_op jit(solution)/shard_map/attend/pallas_call | solution.py:203
  84.8 5.3 %attend.6 = (f32[3,128,512]{2,1,0:T(8,128)S(1)}, f32[3,2,512]{2,1,0:T(2,128)S(1)}) custom-call(f32[80]{0:T(128)S(1)} %select_n.49.bias_ref, s32[1]{0:T(128)} %bitcast.place_ref, bf16[4,128,768]{2,1,0:T(8,128)(2,1)S(1)} %all-to-all-done.2.q_ref, bf16[4,2,128,384]{3,2,1,0:T(8,128)(2,1)} %collective-permute-done.2.refs_0_, ...), custom_call_target="tpu_custom_call" | custom-call | flops 1207959552 | bytes 3145728 | tf_op jit(solution)/shard_map/attend/pallas_call | solution.py:203
  90.1 4.3 %attend.7 = (bf16[128,384]{1,0:T(8,128)(2,1)S(1)}, bf16[128,384]{1,0:T(8,128)(2,1)S(1)}, bf16[128,384]{1,0:T(8,128)(2,1)S(1)}, bf16[128,384]{1,0:T(8,128)(2,1)S(1)}) custom-call(f32[80]{0:T(128)S(1)} %select_n.49.bias_ref, s32[1]{0:T(128)} %bitcast.place_ref, bf16[4,128,768]{2,1,0:T(8,128)(2,1)S(1)} %all-to-all-done.2.q_ref, ...), custom_call_target="tpu_custom_call" | custom-call | flops 805306368 | bytes 2359296 | tf_op jit(solution)/shard_map/attend/pallas_call | solution.py:203
  94.4 4.0 %collective-permute-start.6 = (bf16[128,384]{1,0:T(8,128)(2,1)S(1)}, bf16[128,384]{1,0:T(8,128)(2,1)S(1)}, u32[]{:S(2)}, u32[]{:S(2)}) collective-permute-start(bf16[128,384]{1,0:T(8,128)(2,1)S(1)} %get-tuple-element.33), channel_id=1, source_target_pairs={{0,1},{1,0},{2,3},{3,2},{4,5},{5,4},{6,7},{7,6},{8,9},{9,8},{10,11... | collective-permute-start | bytes 294920 | tf_op jit(solution)/shard_map/ppermute | solution.py:289
  98.4 0.5 collective-permute-start.7
  98.9 2.0 %collective-permute-done.9.refs_0_ = bf16[4,2,128,384]{3,2,1,0:T(8,128)(2,1)S(1)} collective-permute-done((bf16[4,2,128,384]{3,2,1,0:T(8,128)(2,1)}, bf16[4,2,128,384]{3,2,1,0:T(8,128)(2,1)S(1)}, u32[]{:S(2)}, u32[]{:S(2)}) %collective-permute-start.9) | collective-permute-done | bytes 786464 | tf_op jit(solution)/shard_map/ppermute | solution.py:271
  100.9 2.3 %attend.8 = (f32[3,128,512]{2,1,0:T(8,128)S(1)}, f32[3,2,512]{2,1,0:T(2,128)S(1)}) custom-call(f32[80]{0:T(128)S(1)} %select_n.49.bias_ref, s32[1]{0:T(128)} %bitcast.place_ref, bf16[4,128,768]{2,1,0:T(8,128)(2,1)S(1)} %all-to-all-done.2.q_ref, bf16[4,2,128,384]{3,2,1,0:T(8,128)(2,1)S(1)} %collective-permute-done.9.refs_0_, ...), custom_call_target="tpu_custom_call" | custom-call | flops 402653184 | bytes 1572864 | tf_op jit(solution)/shard_map/attend/pallas_call | solution.py:203
  103.3 3.0 %attend.9 = (bf16[128,384]{1,0:T(8,128)(2,1)S(1)}, bf16[128,384]{1,0:T(8,128)(2,1)S(1)}, bf16[128,384]{1,0:T(8,128)(2,1)S(1)}, bf16[128,384]{1,0:T(8,128)(2,1)S(1)}) custom-call(f32[80]{0:T(128)S(1)} %select_n.49.bias_ref, s32[1]{0:T(128)} %bitcast.place_ref, bf16[4,128,768]{2,1,0:T(8,128)(2,1)S(1)} %all-to-all-done.2.q_ref, ...), custom_call_target="tpu_custom_call" | custom-call | flops 402653184 | bytes 1572864 | tf_op jit(solution)/shard_map/attend/pallas_call | solution.py:203
  106.3 3.9 %collective-permute-start.11 = (bf16[128,384]{1,0:T(8,128)(2,1)S(1)}, bf16[128,384]{1,0:T(8,128)(2,1)S(1)}, u32[]{:S(2)}, u32[]{:S(2)}) collective-permute-start(bf16[128,384]{1,0:T(8,128)(2,1)S(1)} %get-tuple-element.42), channel_id=1, source_target_pairs={{0,1},{1,0},{2,3},{3,2},{4,5},{5,4},{6,7},{7,6},{8,9},{9,8},{10,11... | collective-permute-start | bytes 294920 | tf_op jit(solution)/shard_map/ppermute | solution.py:289
  110.2 1.7 %collective-permute-start.12 = (bf16[128,384]{1,0:T(8,128)(2,1)S(1)}, bf16[128,384]{1,0:T(8,128)(2,1)S(1)}, u32[]{:S(2)}, u32[]{:S(2)}) collective-permute-start(bf16[128,384]{1,0:T(8,128)(2,1)S(1)} %get-tuple-element.43), channel_id=1, source_target_pairs={{0,2},{1,3},{2,0},{3,1},{4,6},{5,7},{6,4},{7,5},{8,10},{9,11},{10,... | collective-permute-start | bytes 294920 | tf_op jit(solution)/shard_map/ppermute | solution.py:289
  111.9 1.5 %collective-permute-done.11.refs_5_ = bf16[128,384]{1,0:T(8,128)(2,1)S(1)} collective-permute-done((bf16[128,384]{1,0:T(8,128)(2,1)S(1)}, bf16[128,384]{1,0:T(8,128)(2,1)S(1)}, u32[]{:S(2)}, u32[]{:S(2)}) %collective-permute-start.11) | collective-permute-done | bytes 98336 | tf_op jit(solution)/shard_map/ppermute | solution.py:289
  113.4 3.2 %collective-permute-done.12.refs_6_ = bf16[128,384]{1,0:T(8,128)(2,1)S(1)} collective-permute-done((bf16[128,384]{1,0:T(8,128)(2,1)S(1)}, bf16[128,384]{1,0:T(8,128)(2,1)S(1)}, u32[]{:S(2)}, u32[]{:S(2)}) %collective-permute-start.12) | collective-permute-done | bytes 98336 | tf_op jit(solution)/shard_map/ppermute | solution.py:289
  116.6 1.1 unpack.1
  (36 shorter events, 1.4 us)
Async XLA Ops:
  2.0 16.7 %all-to-all-start = ((bf16[4,2,128,384]{3,2,1,0:T(8,128)(2,1)}), bf16[4,2,128,384]{3,2,1,0:T(8,128)(2,1)S(1)}, u32[]{:S(2)}, u32[]{:S(2)}) async-start(bf16[4,2,128,384]{3,2,1,0:T(8,128)(2,1)} %pack_kv.3), calls=%async_computation | async-start | bytes 1572864 | tf_op jit(solution)/shard_map/all_to_all | solution.py:278
  7.6 14.6 %copy-start.1 = (s32[256]{0:T(256)S(1)}, s32[256]{0:T(256)}, u32[]{:S(2)}) copy-start(s32[256]{0:T(256)} %param.8) | copy-start | bytes 3076
  18.7 16.6 %all-to-all-start.1 = ((bf16[4,2,128,384]{3,2,1,0:T(8,128)(2,1)}), bf16[4,2,128,384]{3,2,1,0:T(8,128)(2,1)S(1)}, u32[]{:S(2)}, u32[]{:S(2)}) async-start(bf16[4,2,128,384]{3,2,1,0:T(8,128)(2,1)} %pack_kv.2), calls=%async_computation.1 | async-start | bytes 1572864 | tf_op jit(solution)/shard_map/all_to_all | solution.py:278
  22.5 35.0 %collective-permute-start.2 = (bf16[4,2,128,384]{3,2,1,0:T(8,128)(2,1)S(1)}, bf16[4,2,128,384]{3,2,1,0:T(8,128)(2,1)}, u32[]{:S(2)}, u32[]{:S(2)}) collective-permute-start(bf16[4,2,128,384]{3,2,1,0:T(8,128)(2,1)S(1)} %all-to-all-done.refs_1_), channel_id=1, source_target_pairs={{0,4},{1,5},{2,6},{3,7},{4,8},{5,9},{6,10},{7,11},{8,12},{9,13},{1... | collective-permute-start | bytes 2359304 | tf_op jit(solution)/shard_map/ppermute | solution.py:271
  26.4 33.1 %collective-permute-start.3 = (bf16[4,2,128,384]{3,2,1,0:T(8,128)(2,1)S(1)}, bf16[4,2,128,384]{3,2,1,0:T(8,128)(2,1)}, u32[]{:S(2)}, u32[]{:S(2)}) collective-permute-start(bf16[4,2,128,384]{3,2,1,0:T(8,128)(2,1)S(1)} %all-to-all-done.refs_1_), channel_id=1, source_target_pairs={{4,0},{5,1},{6,2},{7,3},{8,4},{9,5},{10,6},{11,7},{12,8},{13,9},{1... | collective-permute-start | bytes 2359304 | tf_op jit(solution)/shard_map/ppermute | solution.py:271
  35.3 33.2 %collective-permute-start = (bf16[4,2,128,384]{3,2,1,0:T(8,128)(2,1)S(1)}, bf16[4,2,128,384]{3,2,1,0:T(8,128)(2,1)}, u32[]{:S(2)}, u32[]{:S(2)}) collective-permute-start(bf16[4,2,128,384]{3,2,1,0:T(8,128)(2,1)S(1)} %all-to-all-done.1.refs_1_), channel_id=1, source_target_pairs={{0,4},{1,5},{2,6},{3,7},{4,8},{5,9},{6,10},{7,11},{8,12},{9,13},{1... | collective-permute-start | bytes 2359304 | tf_op jit(solution)/shard_map/ppermute | solution.py:271
  39.2 31.3 %collective-permute-start.1 = (bf16[4,2,128,384]{3,2,1,0:T(8,128)(2,1)S(1)}, bf16[4,2,128,384]{3,2,1,0:T(8,128)(2,1)}, u32[]{:S(2)}, u32[]{:S(2)}) collective-permute-start(bf16[4,2,128,384]{3,2,1,0:T(8,128)(2,1)S(1)} %all-to-all-done.1.refs_1_), channel_id=1, source_target_pairs={{4,0},{5,1},{6,2},{7,3},{8,4},{9,5},{10,6},{11,7},{12,8},{13,9},{1... | collective-permute-start | bytes 2359304 | tf_op jit(solution)/shard_map/ppermute | solution.py:271
  54.0 25.4 %all-to-all-start.2 = ((bf16[4,128,768]{2,1,0:T(8,128)(2,1)}), bf16[4,128,768]{2,1,0:T(8,128)(2,1)S(1)}, u32[]{:S(2)}, u32[]{:S(2)}) async-start(bf16[4,128,768]{2,1,0:T(8,128)(2,1)} %pack_q.1), calls=%async_computation.2 | async-start | bytes 1572864 | tf_op jit(solution)/shard_map/all_to_all | solution.py:278
  57.5 21.1 %copy-start = (s32[256,20]{0,1:T(8,128)S(1)}, s32[256,20]{0,1:T(8,128)}, u32[]{:S(2)}) copy-start(s32[256,20]{0,1:T(8,128)} %param.9) | copy-start | bytes 61444
  57.6 32.5 %collective-permute-start.4 = (bf16[4,2,128,384]{3,2,1,0:T(8,128)(2,1)}, bf16[4,2,128,384]{3,2,1,0:T(8,128)(2,1)}, u32[]{:S(2)}, u32[]{:S(2)}) collective-permute-start(bf16[4,2,128,384]{3,2,1,0:T(8,128)(2,1)} %collective-permute-done.2.refs_0_), channel_id=1, source_target_pairs={{0,4},{1,5},{2,6},{3,7},{4,8},{5,9},{6,10},{7,11},{8,12},{9,13},{1... | collective-permute-start | bytes 2359304 | tf_op jit(solution)/shard_map/ppermute | solution.py:271
  59.5 30.6 %collective-permute-start.5 = (bf16[4,2,128,384]{3,2,1,0:T(8,128)(2,1)}, bf16[4,2,128,384]{3,2,1,0:T(8,128)(2,1)}, u32[]{:S(2)}, u32[]{:S(2)}) collective-permute-start(bf16[4,2,128,384]{3,2,1,0:T(8,128)(2,1)} %collective-permute-done.3.refs_2_), channel_id=1, source_target_pairs={{4,0},{5,1},{6,2},{7,3},{8,4},{9,5},{10,6},{11,7},{12,8},{13,9},{1... | collective-permute-start | bytes 2359304 | tf_op jit(solution)/shard_map/ppermute | solution.py:271
  68.5 32.4 %collective-permute-start.9 = (bf16[4,2,128,384]{3,2,1,0:T(8,128)(2,1)}, bf16[4,2,128,384]{3,2,1,0:T(8,128)(2,1)S(1)}, u32[]{:S(2)}, u32[]{:S(2)}) collective-permute-start(bf16[4,2,128,384]{3,2,1,0:T(8,128)(2,1)} %collective-permute-done.refs_0_), channel_id=1, source_target_pairs={{0,4},{1,5},{2,6},{3,7},{4,8},{5,9},{6,10},{7,11},{8,12},{9,13},{1... | collective-permute-start | bytes 2359304 | tf_op jit(solution)/shard_map/ppermute | solution.py:271
  70.5 32.8 %collective-permute-start.10 = (bf16[4,2,128,384]{3,2,1,0:T(8,128)(2,1)}, bf16[4,2,128,384]{3,2,1,0:T(8,128)(2,1)}, u32[]{:S(2)}, u32[]{:S(2)}) collective-permute-start(bf16[4,2,128,384]{3,2,1,0:T(8,128)(2,1)} %collective-permute-done.1.refs_2_), channel_id=1, source_target_pairs={{4,0},{5,1},{6,2},{7,3},{8,4},{9,5},{10,6},{11,7},{12,8},{13,9},{1... | collective-permute-start | bytes 2359304 | tf_op jit(solution)/shard_map/ppermute | solution.py:271
  94.4 17.5 %collective-permute-start.6 = (bf16[128,384]{1,0:T(8,128)(2,1)S(1)}, bf16[128,384]{1,0:T(8,128)(2,1)S(1)}, u32[]{:S(2)}, u32[]{:S(2)}) collective-permute-start(bf16[128,384]{1,0:T(8,128)(2,1)S(1)} %get-tuple-element.33), channel_id=1, source_target_pairs={{0,1},{1,0},{2,3},{3,2},{4,5},{5,4},{6,7},{7,6},{8,9},{9,8},{10,11... | collective-permute-start | bytes 294920 | tf_op jit(solution)/shard_map/ppermute | solution.py:289
  98.4 13.5 %collective-permute-start.7 = (bf16[128,384]{1,0:T(8,128)(2,1)S(1)}, bf16[128,384]{1,0:T(8,128)(2,1)S(1)}, u32[]{:S(2)}, u32[]{:S(2)}) collective-permute-start(bf16[128,384]{1,0:T(8,128)(2,1)S(1)} %get-tuple-element.34), channel_id=1, source_target_pairs={{0,2},{1,3},{2,0},{3,1},{4,6},{5,7},{6,4},{7,5},{8,10},{9,11},{10,... | collective-permute-start | bytes 294920 | tf_op jit(solution)/shard_map/ppermute | solution.py:289
  98.9 13.0 %collective-permute-start.8 = (bf16[128,384]{1,0:T(8,128)(2,1)S(1)}, bf16[128,384]{1,0:T(8,128)(2,1)S(1)}, u32[]{:S(2)}, u32[]{:S(2)}) collective-permute-start(bf16[128,384]{1,0:T(8,128)(2,1)S(1)} %get-tuple-element.35), channel_id=1, source_target_pairs={{0,3},{1,2},{2,1},{3,0},{4,7},{5,6},{6,5},{7,4},{8,11},{9,10},{10,... | collective-permute-start | bytes 294920 | tf_op jit(solution)/shard_map/ppermute | solution.py:289
  106.3 7.0 %collective-permute-start.11 = (bf16[128,384]{1,0:T(8,128)(2,1)S(1)}, bf16[128,384]{1,0:T(8,128)(2,1)S(1)}, u32[]{:S(2)}, u32[]{:S(2)}) collective-permute-start(bf16[128,384]{1,0:T(8,128)(2,1)S(1)} %get-tuple-element.42), channel_id=1, source_target_pairs={{0,1},{1,0},{2,3},{3,2},{4,5},{5,4},{6,7},{7,6},{8,9},{9,8},{10,11... | collective-permute-start | bytes 294920 | tf_op jit(solution)/shard_map/ppermute | solution.py:289
  110.2 6.4 %collective-permute-start.12 = (bf16[128,384]{1,0:T(8,128)(2,1)S(1)}, bf16[128,384]{1,0:T(8,128)(2,1)S(1)}, u32[]{:S(2)}, u32[]{:S(2)}) collective-permute-start(bf16[128,384]{1,0:T(8,128)(2,1)S(1)} %get-tuple-element.43), channel_id=1, source_target_pairs={{0,2},{1,3},{2,0},{3,1},{4,6},{5,7},{6,4},{7,5},{8,10},{9,11},{10,... | collective-permute-start | bytes 294920 | tf_op jit(solution)/shard_map/ppermute | solution.py:289
  111.9 4.7 %collective-permute-start.13 = (bf16[128,384]{1,0:T(8,128)(2,1)S(1)}, bf16[128,384]{1,0:T(8,128)(2,1)S(1)}, u32[]{:S(2)}, u32[]{:S(2)}) collective-permute-start(bf16[128,384]{1,0:T(8,128)(2,1)S(1)} %get-tuple-element.44), channel_id=1, source_target_pairs={{0,3},{1,2},{2,1},{3,0},{4,7},{5,6},{6,5},{7,4},{8,11},{9,10},{10,... | collective-permute-start | bytes 294920 | tf_op jit(solution)/shard_map/ppermute | solution.py:289

commit v7 on v6

--- a/solution.py
+++ b/solution.py
@@ -320,7 +320,8 @@
     part1 = attend(bias, place, own_q, {-1: up1, 0: own1, 1: down1}, CHUNKS[0], None, False)
     bias0 = after(bias, part1[0])
     part0 = attend(bias0, place, own_q, {-1: up0, 0: own0, 1: down0}, 0, None, False)
-    out0 = attend(after(bias0, part0[0]), place, own_q, {-2: up0b, 2: down0b}, 0, part0, spread=True)
+    part0 = attend(after(bias0, part0[0]), place, own_q, {-2: up0b}, 0, part0, False)
+    out0 = attend(after(bias0, part0[0]), place, own_q, {2: down0b}, 0, part0, spread=True)
     res0 = spread_out(out0)
     bias1 = after(bias, out0[0])
     part1 = attend(bias1, place, own_q, {-2: up1b}, CHUNKS[0], part1, False)

time: 119 us -> 119 us (level)
  Pallas kernels: 27.3 us -> 29 us
  waiting for transfers between devices: 18.8 us -> 17.3 us
    pallas_call x5 -> x6, Pallas kernels: 20.2 us -> 21.9 us  [attend(): pl.pallas_call(functools.partial(attend_kernel, math.log2(math.e) / math....]
    ppermute x8, waiting for transfers between devices: 2.94 us -> 1.52 us  [shifted(): return lax.ppermute(block, AXES, route)]
  transfers between devices with their start and end apart: 17 -> 17, of which waited for: 5 -> 5; matrix products, arithmetic and copies ran while one was open for 4% -> 4% of each run, Pallas kernels for 21% -> 22%
where the time goes in v7:
time: 119 us; the launch traced here: 118 us
  starting transfers between devices  66.2 us (56%)
  Pallas kernels  29 us (24%)
  waiting for transfers between devices  17.3 us (15%)
  other arithmetic  3.07 us (3%)
  local copies, waits for them, and re-layouts  1.55 us (1%)
    ppermute x8, starting transfers between devices, shifted(): return lax.ppermute(block, AXES, route)  46 us
    pallas_call x6, Pallas kernels, attend(): pl.pallas_call(functools.partial(attend_kernel, math.log2(math.e) / math....  21.9 us
    all_to_all x3, waiting for transfers between devices, exchanged(): lax.all_to_all(x, AXES, split_axis=0, concat_axis=0, axis_index_groups=pl...  11.1 us
    all_to_all x3, starting transfers between devices, exchanged(): lax.all_to_all(x, AXES, split_axis=0, concat_axis=0, axis_index_groups=pl...  10.6 us
    ppermute x6, starting transfers between devices, swapped(): return lax.ppermute(x, AXES, route)  9.66 us
    ppermute x6, waiting for transfers between devices, swapped(): return lax.ppermute(x, AXES, route)  4.68 us
    pallas_call x2, Pallas kernels, pack_kv(): pl.pallas_call(functools.partial(pack_kv_kernel, groups, skip), in_specs=...  4.01 us
    select_n x1, other arithmetic, tile_bias(): own = jnp.where(position >= frames // 2, traded(own), own)  2.51 us
  transfers between devices with their start and end apart: 17, of which 5 were waited for; matrix products, arithmetic and copies ran while one was open for 4% of the time, Pallas kernels for 22%

profile of v7, /device:TPU:8, one launch (start us, length us, event | category | flops | bytes accessed | tf_op | source)
XLA Modules:
  0.0 117.6 jit_solution(548800127631674457)
XLA Ops:
  0.0 2.0 %pack_kv.3 = bf16[4,2,128,384]{3,2,1,0:T(8,128)(2,1)} custom-call(bf16[128,3072]{1,0:T(8,128)(2,1)} %k_ref.3, bf16[128,3072]{1,0:T(8,128)(2,1)} %v_ref.3), custom_call_target="tpu_custom_call" | custom-call | tf_op jit(solution)/shard_map/pack_kv/pallas_call | solution.py:56
  2.0 3.6 %all-to-all-start = ((bf16[4,2,128,384]{3,2,1,0:T(8,128)(2,1)}), bf16[4,2,128,384]{3,2,1,0:T(8,128)(2,1)S(1)}, u32[]{:S(2)}, u32[]{:S(2)}) async-start(bf16[4,2,128,384]{3,2,1,0:T(8,128)(2,1)} %pack_kv.3), calls=%async_computation | async-start | bytes 1572864 | tf_op jit(solution)/shard_map/all_to_all | solution.py:278
  5.6 2.0 %pack_kv.2 = bf16[4,2,128,384]{3,2,1,0:T(8,128)(2,1)} custom-call(bf16[128,3072]{1,0:T(8,128)(2,1)} %k_ref.3, bf16[128,3072]{1,0:T(8,128)(2,1)} %v_ref.3), custom_call_target="tpu_custom_call" | custom-call | tf_op jit(solution)/shard_map/pack_kv/pallas_call | solution.py:56
  7.6 11.1 %all-to-all-done.refs_1_ = bf16[4,2,128,384]{3,2,1,0:T(8,128)(2,1)S(1)} async-done(((bf16[4,2,128,384]{3,2,1,0:T(8,128)(2,1)}), bf16[4,2,128,384]{3,2,1,0:T(8,128)(2,1)S(1)}, u32[]{:S(2)}, u32[]{:S(2)}) %all-to-all-start) | async-done | bytes 786464 | tf_op jit(solution)/shard_map/all_to_all | solution.py:278
  18.7 3.5 %all-to-all-start.1 = ((bf16[4,2,128,384]{3,2,1,0:T(8,128)(2,1)}), bf16[4,2,128,384]{3,2,1,0:T(8,128)(2,1)S(1)}, u32[]{:S(2)}, u32[]{:S(2)}) async-start(bf16[4,2,128,384]{3,2,1,0:T(8,128)(2,1)} %pack_kv.2), calls=%async_computation.1 | async-start | bytes 1572864 | tf_op jit(solution)/shard_map/all_to_all | solution.py:278
  22.5 3.8 %collective-permute-start.2 = (bf16[4,2,128,384]{3,2,1,0:T(8,128)(2,1)S(1)}, bf16[4,2,128,384]{3,2,1,0:T(8,128)(2,1)}, u32[]{:S(2)}, u32[]{:S(2)}) collective-permute-start(bf16[4,2,128,384]{3,2,1,0:T(8,128)(2,1)S(1)} %all-to-all-done.refs_1_), channel_id=1, source_target_pairs={{0,4},{1,5},{2,6},{3,7},{4,8},{5,9},{6,10},{7,11},{8,12},{9,13},{1... | collective-permute-start | bytes 2359304 | tf_op jit(solution)/shard_map/ppermute | solution.py:271
  26.4 8.9 %collective-permute-start.3 = (bf16[4,2,128,384]{3,2,1,0:T(8,128)(2,1)S(1)}, bf16[4,2,128,384]{3,2,1,0:T(8,128)(2,1)}, u32[]{:S(2)}, u32[]{:S(2)}) collective-permute-start(bf16[4,2,128,384]{3,2,1,0:T(8,128)(2,1)S(1)} %all-to-all-done.refs_1_), channel_id=1, source_target_pairs={{4,0},{5,1},{6,2},{7,3},{8,4},{9,5},{10,6},{11,7},{12,8},{13,9},{1... | collective-permute-start | bytes 2359304 | tf_op jit(solution)/shard_map/ppermute | solution.py:271
  35.3 3.8 %collective-permute-start = (bf16[4,2,128,384]{3,2,1,0:T(8,128)(2,1)S(1)}, bf16[4,2,128,384]{3,2,1,0:T(8,128)(2,1)}, u32[]{:S(2)}, u32[]{:S(2)}) collective-permute-start(bf16[4,2,128,384]{3,2,1,0:T(8,128)(2,1)S(1)} %all-to-all-done.1.refs_1_), channel_id=1, source_target_pairs={{0,4},{1,5},{2,6},{3,7},{4,8},{5,9},{6,10},{7,11},{8,12},{9,13},{1... | collective-permute-start | bytes 2359304 | tf_op jit(solution)/shard_map/ppermute | solution.py:271
  39.2 9.4 %collective-permute-start.1 = (bf16[4,2,128,384]{3,2,1,0:T(8,128)(2,1)S(1)}, bf16[4,2,128,384]{3,2,1,0:T(8,128)(2,1)}, u32[]{:S(2)}, u32[]{:S(2)}) collective-permute-start(bf16[4,2,128,384]{3,2,1,0:T(8,128)(2,1)S(1)} %all-to-all-done.1.refs_1_), channel_id=1, source_target_pairs={{4,0},{5,1},{6,2},{7,3},{8,4},{9,5},{10,6},{11,7},{12,8},{13,9},{1... | collective-permute-start | bytes 2359304 | tf_op jit(solution)/shard_map/ppermute | solution.py:271
  48.7 2.0 %pack_q.1 = bf16[4,128,768]{2,1,0:T(8,128)(2,1)} custom-call(bf16[128,3072]{1,0:T(8,128)(2,1)} %q_ref.1), custom_call_target="tpu_custom_call" | custom-call | tf_op jit(solution)/shard_map/pack_q/pallas_call | solution.py:81
  50.8 0.7 fusion.2
  51.4 2.5 %broadcast_select_fusion.1 = s32[4]{0:T(128)S(1)} fusion(pred[]{:T(512)S(6)} %ge.21, s32[1]{0:T(128)} %get-tuple-element.56, s32[1]{0:T(128)} %get-tuple-element.57, s32[1]{0:T(128)} %get-tuple-element.58, s32[1]{0:T(128)} %get-tuple-element.55, s32[]{:T(128)S(6)} %mul.14, s32[256]{0:T(256)S(1)} %copy-done.1, s32[]{:T(128)S(6)} %select_n.44), kind=kLoop, calls=%fused_computation.10 | loop fusion | flops 20 | bytes 57 | tf_op jit(solution)/shard_map/jit(_where)/select_n | solution.py:241
  54.0 3.5 %all-to-all-start.2 = ((bf16[4,128,768]{2,1,0:T(8,128)(2,1)}), bf16[4,128,768]{2,1,0:T(8,128)(2,1)S(1)}, u32[]{:S(2)}, u32[]{:S(2)}) async-start(bf16[4,128,768]{2,1,0:T(8,128)(2,1)} %pack_q.1), calls=%async_computation.2 | async-start | bytes 1572864 | tf_op jit(solution)/shard_map/all_to_all | solution.py:278
  57.5 1.9 %collective-permute-start.4 = (bf16[4,2,128,384]{3,2,1,0:T(8,128)(2,1)}, bf16[4,2,128,384]{3,2,1,0:T(8,128)(2,1)}, u32[]{:S(2)}, u32[]{:S(2)}) collective-permute-start(bf16[4,2,128,384]{3,2,1,0:T(8,128)(2,1)} %collective-permute-done.2.refs_0_), channel_id=1, source_target_pairs={{0,4},{1,5},{2,6},{3,7},{4,8},{5,9},{6,10},{7,11},{8,12},{9,13},{1... | collective-permute-start | bytes 2359304 | tf_op jit(solution)/shard_map/ppermute | solution.py:271
  59.4 8.1 %collective-permute-start.5 = (bf16[4,2,128,384]{3,2,1,0:T(8,128)(2,1)}, bf16[4,2,128,384]{3,2,1,0:T(8,128)(2,1)}, u32[]{:S(2)}, u32[]{:S(2)}) collective-permute-start(bf16[4,2,128,384]{3,2,1,0:T(8,128)(2,1)} %collective-permute-done.3.refs_2_), channel_id=1, source_target_pairs={{4,0},{5,1},{6,2},{7,3},{8,4},{9,5},{10,6},{11,7},{12,8},{13,9},{1... | collective-permute-start | bytes 2359304 | tf_op jit(solution)/shard_map/ppermute | solution.py:271
  67.6 0.9 collective-permute-done.refs_0_
  68.5 1.9 %collective-permute-start.9 = (bf16[4,2,128,384]{3,2,1,0:T(8,128)(2,1)}, bf16[4,2,128,384]{3,2,1,0:T(8,128)(2,1)S(1)}, u32[]{:S(2)}, u32[]{:S(2)}) collective-permute-start(bf16[4,2,128,384]{3,2,1,0:T(8,128)(2,1)} %collective-permute-done.refs_0_), channel_id=1, source_target_pairs={{0,4},{1,5},{2,6},{3,7},{4,8},{5,9},{6,10},{7,11},{8,12},{9,13},{1... | collective-permute-start | bytes 2359304 | tf_op jit(solution)/shard_map/ppermute | solution.py:271
  70.5 8.1 %collective-permute-start.10 = (bf16[4,2,128,384]{3,2,1,0:T(8,128)(2,1)}, bf16[4,2,128,384]{3,2,1,0:T(8,128)(2,1)}, u32[]{:S(2)}, u32[]{:S(2)}) collective-permute-start(bf16[4,2,128,384]{3,2,1,0:T(8,128)(2,1)} %collective-permute-done.1.refs_2_), channel_id=1, source_target_pairs={{4,0},{5,1},{6,2},{7,3},{8,4},{9,5},{10,6},{11,7},{12,8},{13,9},{1... | collective-permute-start | bytes 2359304 | tf_op jit(solution)/shard_map/ppermute | solution.py:271
  79.5 5.3 %attend.6 = (f32[3,128,512]{2,1,0:T(8,128)S(1)}, f32[3,2,512]{2,1,0:T(2,128)S(1)}) custom-call(f32[80]{0:T(128)S(1)} %select_n.49.bias_ref, s32[1]{0:T(128)} %bitcast.place_ref, bf16[4,128,768]{2,1,0:T(8,128)(2,1)S(1)} %all-to-all-done.2.q_ref, bf16[4,2,128,384]{3,2,1,0:T(8,128)(2,1)} %collective-permute-done.refs_0_, ...), custom_call_target="tpu_custom_call" | custom-call | flops 1207959552 | bytes 3145728 | tf_op jit(solution)/shard_map/attend/pallas_call | solution.py:203
  84.8 5.3 %attend.7 = (f32[3,128,512]{2,1,0:T(8,128)S(1)}, f32[3,2,512]{2,1,0:T(2,128)S(1)}) custom-call(f32[80]{0:T(128)S(1)} %select_n.49.bias_ref, s32[1]{0:T(128)} %bitcast.place_ref, bf16[4,128,768]{2,1,0:T(8,128)(2,1)S(1)} %all-to-all-done.2.q_ref, bf16[4,2,128,384]{3,2,1,0:T(8,128)(2,1)} %collective-permute-done.2.refs_0_, ...), custom_call_target="tpu_custom_call" | custom-call | flops 1207959552 | bytes 3145728 | tf_op jit(solution)/shard_map/attend/pallas_call | solution.py:203
  90.1 2.9 %attend.8 = (f32[3,128,512]{2,1,0:T(8,128)S(1)}, f32[3,2,512]{2,1,0:T(2,128)S(1)}) custom-call(f32[80]{0:T(128)S(1)} %select_n.49.bias_ref, s32[1]{0:T(128)} %bitcast.place_ref, bf16[4,128,768]{2,1,0:T(8,128)(2,1)S(1)} %all-to-all-done.2.q_ref, bf16[4,2,128,384]{3,2,1,0:T(8,128)(2,1)} %collective-permute-done.4.refs_0_, ...), custom_call_target="tpu_custom_call" | custom-call | flops 402653184 | bytes 1572864 | tf_op jit(solution)/shard_map/attend/pallas_call | solution.py:203
  93.0 3.0 %attend.9 = (bf16[128,384]{1,0:T(8,128)(2,1)S(1)}, bf16[128,384]{1,0:T(8,128)(2,1)S(1)}, bf16[128,384]{1,0:T(8,128)(2,1)S(1)}, bf16[128,384]{1,0:T(8,128)(2,1)S(1)}) custom-call(f32[80]{0:T(128)S(1)} %select_n.49.bias_ref, s32[1]{0:T(128)} %bitcast.place_ref, bf16[4,128,768]{2,1,0:T(8,128)(2,1)S(1)} %all-to-all-done.2.q_ref, ...), custom_call_target="tpu_custom_call" | custom-call | flops 402653184 | bytes 1572864 | tf_op jit(solution)/shard_map/attend/pallas_call | solution.py:203
  96.1 3.8 %collective-permute-start.6 = (bf16[128,384]{1,0:T(8,128)(2,1)S(1)}, bf16[128,384]{1,0:T(8,128)(2,1)S(1)}, u32[]{:S(2)}, u32[]{:S(2)}) collective-permute-start(bf16[128,384]{1,0:T(8,128)(2,1)S(1)} %get-tuple-element.39), channel_id=1, source_target_pairs={{0,1},{1,0},{2,3},{3,2},{4,5},{5,4},{6,7},{7,6},{8,9},{9,8},{10,11... | collective-permute-start | bytes 294920 | tf_op jit(solution)/shard_map/ppermute | solution.py:289
  99.9 0.6 collective-permute-start.7
  100.4 0.6 collective-permute-done.9.refs_0_
  101.0 2.3 %attend.10 = (f32[3,128,512]{2,1,0:T(8,128)S(1)}, f32[3,2,512]{2,1,0:T(2,128)S(1)}) custom-call(f32[80]{0:T(128)S(1)} %select_n.49.bias_ref, s32[1]{0:T(128)} %bitcast.place_ref, bf16[4,128,768]{2,1,0:T(8,128)(2,1)S(1)} %all-to-all-done.2.q_ref, bf16[4,2,128,384]{3,2,1,0:T(8,128)(2,1)S(1)} %collective-permute-done.9.refs_0_, ...), custom_call_target="tpu_custom_call" | custom-call | flops 402653184 | bytes 1572864 | tf_op jit(solution)/shard_map/attend/pallas_call | solution.py:203
  103.4 3.0 %attend.11 = (bf16[128,384]{1,0:T(8,128)(2,1)S(1)}, bf16[128,384]{1,0:T(8,128)(2,1)S(1)}, bf16[128,384]{1,0:T(8,128)(2,1)S(1)}, bf16[128,384]{1,0:T(8,128)(2,1)S(1)}) custom-call(f32[80]{0:T(128)S(1)} %select_n.49.bias_ref, s32[1]{0:T(128)} %bitcast.place_ref, bf16[4,128,768]{2,1,0:T(8,128)(2,1)S(1)} %all-to-all-done.2.q_ref, ...), custom_call_target="tpu_custom_call" | custom-call | flops 402653184 | bytes 1572864 | tf_op jit(solution)/shard_map/attend/pallas_call | solution.py:203
  106.4 3.1 %collective-permute-start.11 = (bf16[128,384]{1,0:T(8,128)(2,1)S(1)}, bf16[128,384]{1,0:T(8,128)(2,1)S(1)}, u32[]{:S(2)}, u32[]{:S(2)}) collective-permute-start(bf16[128,384]{1,0:T(8,128)(2,1)S(1)} %get-tuple-element.48), channel_id=1, source_target_pairs={{0,1},{1,0},{2,3},{3,2},{4,5},{5,4},{6,7},{7,6},{8,9},{9,8},{10,11... | collective-permute-start | bytes 294920 | tf_op jit(solution)/shard_map/ppermute | solution.py:289
  109.5 2.2 %collective-permute-start.12 = (bf16[128,384]{1,0:T(8,128)(2,1)S(1)}, bf16[128,384]{1,0:T(8,128)(2,1)S(1)}, u32[]{:S(2)}, u32[]{:S(2)}) collective-permute-start(bf16[128,384]{1,0:T(8,128)(2,1)S(1)} %get-tuple-element.49), channel_id=1, source_target_pairs={{0,2},{1,3},{2,0},{3,1},{4,6},{5,7},{6,4},{7,5},{8,10},{9,11},{10,... | collective-permute-start | bytes 294920 | tf_op jit(solution)/shard_map/ppermute | solution.py:289
  111.7 0.9 collective-permute-done.11.refs_5_
  112.6 3.8 %collective-permute-done.12.refs_6_ = bf16[128,384]{1,0:T(8,128)(2,1)S(1)} collective-permute-done((bf16[128,384]{1,0:T(8,128)(2,1)S(1)}, bf16[128,384]{1,0:T(8,128)(2,1)S(1)}, u32[]{:S(2)}, u32[]{:S(2)}) %collective-permute-start.12) | collective-permute-done | bytes 98336 | tf_op jit(solution)/shard_map/ppermute | solution.py:289
  116.4 1.1 unpack.1
  (37 shorter events, 1.5 us)
Async XLA Ops:
  2.0 16.7 %all-to-all-start = ((bf16[4,2,128,384]{3,2,1,0:T(8,128)(2,1)}), bf16[4,2,128,384]{3,2,1,0:T(8,128)(2,1)S(1)}, u32[]{:S(2)}, u32[]{:S(2)}) async-start(bf16[4,2,128,384]{3,2,1,0:T(8,128)(2,1)} %pack_kv.3), calls=%async_computation | async-start | bytes 1572864 | tf_op jit(solution)/shard_map/all_to_all | solution.py:278
  7.6 14.6 %copy-start.1 = (s32[256]{0:T(256)S(1)}, s32[256]{0:T(256)}, u32[]{:S(2)}) copy-start(s32[256]{0:T(256)} %param.8) | copy-start | bytes 3076
  18.7 16.6 %all-to-all-start.1 = ((bf16[4,2,128,384]{3,2,1,0:T(8,128)(2,1)}), bf16[4,2,128,384]{3,2,1,0:T(8,128)(2,1)S(1)}, u32[]{:S(2)}, u32[]{:S(2)}) async-start(bf16[4,2,128,384]{3,2,1,0:T(8,128)(2,1)} %pack_kv.2), calls=%async_computation.1 | async-start | bytes 1572864 | tf_op jit(solution)/shard_map/all_to_all | solution.py:278
  22.5 35.0 %collective-permute-start.2 = (bf16[4,2,128,384]{3,2,1,0:T(8,128)(2,1)S(1)}, bf16[4,2,128,384]{3,2,1,0:T(8,128)(2,1)}, u32[]{:S(2)}, u32[]{:S(2)}) collective-permute-start(bf16[4,2,128,384]{3,2,1,0:T(8,128)(2,1)S(1)} %all-to-all-done.refs_1_), channel_id=1, source_target_pairs={{0,4},{1,5},{2,6},{3,7},{4,8},{5,9},{6,10},{7,11},{8,12},{9,13},{1... | collective-permute-start | bytes 2359304 | tf_op jit(solution)/shard_map/ppermute | solution.py:271
  26.4 33.1 %collective-permute-start.3 = (bf16[4,2,128,384]{3,2,1,0:T(8,128)(2,1)S(1)}, bf16[4,2,128,384]{3,2,1,0:T(8,128)(2,1)}, u32[]{:S(2)}, u32[]{:S(2)}) collective-permute-start(bf16[4,2,128,384]{3,2,1,0:T(8,128)(2,1)S(1)} %all-to-all-done.refs_1_), channel_id=1, source_target_pairs={{4,0},{5,1},{6,2},{7,3},{8,4},{9,5},{10,6},{11,7},{12,8},{13,9},{1... | collective-permute-start | bytes 2359304 | tf_op jit(solution)/shard_map/ppermute | solution.py:271
  35.3 33.2 %collective-permute-start = (bf16[4,2,128,384]{3,2,1,0:T(8,128)(2,1)S(1)}, bf16[4,2,128,384]{3,2,1,0:T(8,128)(2,1)}, u32[]{:S(2)}, u32[]{:S(2)}) collective-permute-start(bf16[4,2,128,384]{3,2,1,0:T(8,128)(2,1)S(1)} %all-to-all-done.1.refs_1_), channel_id=1, source_target_pairs={{0,4},{1,5},{2,6},{3,7},{4,8},{5,9},{6,10},{7,11},{8,12},{9,13},{1... | collective-permute-start | bytes 2359304 | tf_op jit(solution)/shard_map/ppermute | solution.py:271
  39.2 31.3 %collective-permute-start.1 = (bf16[4,2,128,384]{3,2,1,0:T(8,128)(2,1)S(1)}, bf16[4,2,128,384]{3,2,1,0:T(8,128)(2,1)}, u32[]{:S(2)}, u32[]{:S(2)}) collective-permute-start(bf16[4,2,128,384]{3,2,1,0:T(8,128)(2,1)S(1)} %all-to-all-done.1.refs_1_), channel_id=1, source_target_pairs={{4,0},{5,1},{6,2},{7,3},{8,4},{9,5},{10,6},{11,7},{12,8},{13,9},{1... | collective-permute-start | bytes 2359304 | tf_op jit(solution)/shard_map/ppermute | solution.py:271
  54.0 25.5 %all-to-all-start.2 = ((bf16[4,128,768]{2,1,0:T(8,128)(2,1)}), bf16[4,128,768]{2,1,0:T(8,128)(2,1)S(1)}, u32[]{:S(2)}, u32[]{:S(2)}) async-start(bf16[4,128,768]{2,1,0:T(8,128)(2,1)} %pack_q.1), calls=%async_computation.2 | async-start | bytes 1572864 | tf_op jit(solution)/shard_map/all_to_all | solution.py:278
  57.5 21.2 %copy-start = (s32[256,20]{0,1:T(8,128)S(1)}, s32[256,20]{0,1:T(8,128)}, u32[]{:S(2)}) copy-start(s32[256,20]{0,1:T(8,128)} %param.9) | copy-start | bytes 61444
  57.5 32.6 %collective-permute-start.4 = (bf16[4,2,128,384]{3,2,1,0:T(8,128)(2,1)}, bf16[4,2,128,384]{3,2,1,0:T(8,128)(2,1)}, u32[]{:S(2)}, u32[]{:S(2)}) collective-permute-start(bf16[4,2,128,384]{3,2,1,0:T(8,128)(2,1)} %collective-permute-done.2.refs_0_), channel_id=1, source_target_pairs={{0,4},{1,5},{2,6},{3,7},{4,8},{5,9},{6,10},{7,11},{8,12},{9,13},{1... | collective-permute-start | bytes 2359304 | tf_op jit(solution)/shard_map/ppermute | solution.py:271
  59.4 33.6 %collective-permute-start.5 = (bf16[4,2,128,384]{3,2,1,0:T(8,128)(2,1)}, bf16[4,2,128,384]{3,2,1,0:T(8,128)(2,1)}, u32[]{:S(2)}, u32[]{:S(2)}) collective-permute-start(bf16[4,2,128,384]{3,2,1,0:T(8,128)(2,1)} %collective-permute-done.3.refs_2_), channel_id=1, source_target_pairs={{4,0},{5,1},{6,2},{7,3},{8,4},{9,5},{10,6},{11,7},{12,8},{13,9},{1... | collective-permute-start | bytes 2359304 | tf_op jit(solution)/shard_map/ppermute | solution.py:271
  68.5 32.5 %collective-permute-start.9 = (bf16[4,2,128,384]{3,2,1,0:T(8,128)(2,1)}, bf16[4,2,128,384]{3,2,1,0:T(8,128)(2,1)S(1)}, u32[]{:S(2)}, u32[]{:S(2)}) collective-permute-start(bf16[4,2,128,384]{3,2,1,0:T(8,128)(2,1)} %collective-permute-done.refs_0_), channel_id=1, source_target_pairs={{0,4},{1,5},{2,6},{3,7},{4,8},{5,9},{6,10},{7,11},{8,12},{9,13},{1... | collective-permute-start | bytes 2359304 | tf_op jit(solution)/shard_map/ppermute | solution.py:271
  70.5 32.8 %collective-permute-start.10 = (bf16[4,2,128,384]{3,2,1,0:T(8,128)(2,1)}, bf16[4,2,128,384]{3,2,1,0:T(8,128)(2,1)}, u32[]{:S(2)}, u32[]{:S(2)}) collective-permute-start(bf16[4,2,128,384]{3,2,1,0:T(8,128)(2,1)} %collective-permute-done.1.refs_2_), channel_id=1, source_target_pairs={{4,0},{5,1},{6,2},{7,3},{8,4},{9,5},{10,6},{11,7},{12,8},{13,9},{1... | collective-permute-start | bytes 2359304 | tf_op jit(solution)/shard_map/ppermute | solution.py:271
  96.1 15.6 %collective-permute-start.6 = (bf16[128,384]{1,0:T(8,128)(2,1)S(1)}, bf16[128,384]{1,0:T(8,128)(2,1)S(1)}, u32[]{:S(2)}, u32[]{:S(2)}) collective-permute-start(bf16[128,384]{1,0:T(8,128)(2,1)S(1)} %get-tuple-element.39), channel_id=1, source_target_pairs={{0,1},{1,0},{2,3},{3,2},{4,5},{5,4},{6,7},{7,6},{8,9},{9,8},{10,11... | collective-permute-start | bytes 294920 | tf_op jit(solution)/shard_map/ppermute | solution.py:289
  99.9 11.9 %collective-permute-start.7 = (bf16[128,384]{1,0:T(8,128)(2,1)S(1)}, bf16[128,384]{1,0:T(8,128)(2,1)S(1)}, u32[]{:S(2)}, u32[]{:S(2)}) collective-permute-start(bf16[128,384]{1,0:T(8,128)(2,1)S(1)} %get-tuple-element.40), channel_id=1, source_target_pairs={{0,2},{1,3},{2,0},{3,1},{4,6},{5,7},{6,4},{7,5},{8,10},{9,11},{10,... | collective-permute-start | bytes 294920 | tf_op jit(solution)/shard_map/ppermute | solution.py:289
  100.4 11.3 %collective-permute-start.8 = (bf16[128,384]{1,0:T(8,128)(2,1)S(1)}, bf16[128,384]{1,0:T(8,128)(2,1)S(1)}, u32[]{:S(2)}, u32[]{:S(2)}) collective-permute-start(bf16[128,384]{1,0:T(8,128)(2,1)S(1)} %get-tuple-element.41), channel_id=1, source_target_pairs={{0,3},{1,2},{2,1},{3,0},{4,7},{5,6},{6,5},{7,4},{8,11},{9,10},{10,... | collective-permute-start | bytes 294920 | tf_op jit(solution)/shard_map/ppermute | solution.py:289
  106.4 6.2 %collective-permute-start.11 = (bf16[128,384]{1,0:T(8,128)(2,1)S(1)}, bf16[128,384]{1,0:T(8,128)(2,1)S(1)}, u32[]{:S(2)}, u32[]{:S(2)}) collective-permute-start(bf16[128,384]{1,0:T(8,128)(2,1)S(1)} %get-tuple-element.48), channel_id=1, source_target_pairs={{0,1},{1,0},{2,3},{3,2},{4,5},{5,4},{6,7},{7,6},{8,9},{9,8},{10,11... | collective-permute-start | bytes 294920 | tf_op jit(solution)/shard_map/ppermute | solution.py:289
  109.5 6.9 %collective-permute-start.12 = (bf16[128,384]{1,0:T(8,128)(2,1)S(1)}, bf16[128,384]{1,0:T(8,128)(2,1)S(1)}, u32[]{:S(2)}, u32[]{:S(2)}) collective-permute-start(bf16[128,384]{1,0:T(8,128)(2,1)S(1)} %get-tuple-element.49), channel_id=1, source_target_pairs={{0,2},{1,3},{2,0},{3,1},{4,6},{5,7},{6,4},{7,5},{8,10},{9,11},{10,... | collective-permute-start | bytes 294920 | tf_op jit(solution)/shard_map/ppermute | solution.py:289
  111.7 4.7 %collective-permute-start.13 = (bf16[128,384]{1,0:T(8,128)(2,1)S(1)}, bf16[128,384]{1,0:T(8,128)(2,1)S(1)}, u32[]{:S(2)}, u32[]{:S(2)}) collective-permute-start(bf16[128,384]{1,0:T(8,128)(2,1)S(1)} %get-tuple-element.50), channel_id=1, source_target_pairs={{0,3},{1,2},{2,1},{3,0},{4,7},{5,6},{6,5},{7,4},{8,11},{9,10},{10,... | collective-permute-start | bytes 294920 | tf_op jit(solution)/shard_map/ppermute | solution.py:289
